TPU v7x, 32 devices: a whole 2x2x4 slice. The times are simulated.
32 devices in a mesh: seq: 4 (over x, core), blk: 8 (over z, y).
Axes of the slice: x: 2, y: 2, z: 4, core: 2. Of those that a mesh axis runs over, the one named last changes fastest.
Arguments:
- tokens: bfloat16 [8192, 2048], P(('seq', 'blk')), may hold values from -6 to 6
- cotangent: bfloat16 [8192, 2048], P(('seq', 'blk')), may hold values from -6 to 6
- grouping: int32 [4, 1], P('seq'), may hold values from 0 to 1
- memory_start: float32 [4, 16, 128, 128], P('seq', 'blk'), may hold values from -128 to 128
- normalizer_start: float32 [4, 16, 128], P('seq', 'blk'), may hold values from 64 to 1024
- gain_attention: float32 [2048], replicated, may hold values from 0.1 to 1.9
- attention_in: bfloat16 [2048, 3, 2048], P('seq', None, 'blk'), may hold values from -0.125 to 0.125
- gate_logit: float32 [16], replicated, may hold values from -2.5 to 2.5
- attention_out: bfloat16 [2048, 2048], P('blk', 'seq'), may hold values from -0.5 to 0.5
- gain_feed: float32 [2048], replicated, may hold values from 0.1 to 1.9
- feed_in: bfloat16 [2048, 2, 8192], P('seq', None, 'blk'), may hold values from -0.125 to 0.125
- feed_out: bfloat16 [8192, 2048], P('blk', 'seq'), may hold values from -0.0625 to 0.0625
Outputs:
- mixed: bfloat16 [8192, 2048], P(('seq', 'blk'))
- token_grad: float32 [8192, 2048], P(('seq', 'blk'))
- gain_attention_grad: float32 [2048], replicated
- attention_in_grad: float32 [2048, 3, 2048], P('seq', None, 'blk')
- gate_logit_grad: float32 [16], replicated
- attention_out_grad: float32 [2048, 2048], P('blk', 'seq')
- gain_feed_grad: float32 [2048], replicated
- feed_in_grad: float32 [2048, 2, 8192], P('seq', None, 'blk')
- feed_out_grad: float32 [8192, 2048], P('blk', 'seq')
- memory_final: float32 [4, 16, 128, 128], P('seq', 'blk')
- normalizer_final: float32 [4, 16, 128], P('seq', 'blk')
All inputs are finite; a program needn't handle non-finite values.
Results may differ from a plain program's by a relative error of at most 0.02.
Values may be sent and summed in bfloat16 or wider, within the bound.
No kernel may reach another device: no remote copies, remote signals or barrier semaphores. Data moves between devices by JAX's collectives and lax.ppermute only.
A program may use at most 320 MiB of HBM per device.

v0:
```python
import jax
import jax.numpy as jnp
from jax import lax
from jax.sharding import PartitionSpec as P

SHORT = 1024


EPSILON = 1e-06
MASKED = -1e30
PRECISE = lax.Precision.HIGHEST


def gather_rows(values):
    return lax.all_gather(values, "blk", axis=0, tiled=True)


def sum_rows(left, right, form):
    return lax.psum_scatter(
        jnp.einsum(form, left, right, preferred_element_type=jnp.float32).astype(jnp.bfloat16),
        "blk",
        scatter_dimension=0,
        tiled=True,
    ).astype(jnp.float32)


def column_grads(left, gradient):
    return lax.psum_scatter(
        jnp.einsum("td,tpc->dpc", left, gradient, preferred_element_type=jnp.float32).astype(
            jnp.bfloat16
        ),
        "seq",
        scatter_dimension=0,
        tiled=True,
    ).astype(jnp.float32)


def rms_parts(values):
    scale_rows = lax.rsqrt(jnp.mean(values * values, axis=-1, keepdims=True) + EPSILON)
    return (scale_rows, values * scale_rows)


def rms_back(unit_grad, unit, scale_rows):
    return scale_rows * (unit_grad - unit * jnp.mean(unit_grad * unit, axis=-1, keepdims=True))


def feature(values):
    return jax.nn.elu(values) + 1.0


def feature_slope(values):
    return jnp.where(values > 0, 1.0, jnp.exp(jnp.minimum(values, 0.0)))


def segment_table(splits, length):
    positions = jnp.arange(length, dtype=jnp.int32)
    slot = positions // (2 * SHORT)
    within = positions % (2 * SHORT)
    widths = 1 + splits
    before = jnp.cumsum(widths) - widths
    half = within // SHORT * splits[slot]
    segment = before[slot] + half
    begin = slot * (2 * SHORT) + half * SHORT
    return (segment, begin)


def memory_delta(key_feat, value_heads, member, memory, normalizer):
    numerator = jnp.einsum("tha,hab->thb", key_feat, memory, precision=PRECISE)
    denominator = jnp.einsum("tha,ha->th", key_feat, normalizer, precision=PRECISE)
    mismatch = value_heads - numerator / denominator[:, :, None]
    chosen = key_feat * member[:, None, None]
    return (
        jnp.einsum("tha,thb->hab", chosen, mismatch, precision=PRECISE),
        jnp.sum(chosen, axis=0),
    )


def per_device(
    tokens,
    cotangent,
    grouping,
    memory_start,
    normalizer_start,
    gain_attention,
    attention_in,
    gate_logit,
    attention_out,
    gain_feed,
    feed_in,
    feed_out,
):
    rows, width = tokens.shape
    heads_all = gate_logit.shape[0]
    heads_here = memory_start.shape[1]
    head_size = memory_start.shape[2]
    length = rows * lax.axis_size("blk")
    scale = head_size ** (-0.5)
    head_first = lax.axis_index("blk") * heads_here
    splits = grouping[0]
    segments = 2 * splits.shape[0]
    segment, begin = segment_table(splits, length)
    w_in, w_out, f_in, f_out = (
        lax.all_gather(attention_in, "seq", axis=0, tiled=True),
        lax.all_gather(attention_out, "seq", axis=1, tiled=True),
        lax.all_gather(feed_in, "seq", axis=0, tiled=True),
        lax.all_gather(feed_out, "seq", axis=1, tiled=True),
    )
    cols_here = w_in.shape[2]
    tokens_full = tokens.astype(jnp.float32)
    scale_first, unit_first = rms_parts(tokens_full)
    normed_whole_a = gather_rows((unit_first * gain_attention).astype(jnp.bfloat16))
    projected = jnp.einsum(
        "td,dpc->tpc", normed_whole_a, w_in, preferred_element_type=jnp.float32
    ).astype(jnp.bfloat16)
    queries = projected[:, 0].reshape(length, heads_here, head_size)
    keys = projected[:, 1].reshape(length, heads_here, head_size)
    values = projected[:, 2].reshape(length, heads_here, head_size)
    block = min(512, SHORT, length)
    span = min(length, 2 * SHORT)
    count = length // block

    def window(index):
        start_q = index * block
        start_k = jnp.clip(start_q + block - span, 0, length - span)
        return (start_q, start_k)

    def scores_of(start_q, start_k):
        query_block = lax.dynamic_slice_in_dim(queries, start_q, block, 0)
        key_block = lax.dynamic_slice_in_dim(keys, start_k, span, 0)
        value_block = lax.dynamic_slice_in_dim(values, start_k, span, 0)
        raw = (
            jnp.einsum("qhe,khe->hqk", query_block, key_block, preferred_element_type=jnp.float32)
            * scale
        )
        query_pos = start_q + jnp.arange(block, dtype=jnp.int32)
        key_pos = start_k + jnp.arange(span, dtype=jnp.int32)
        query_begin = lax.dynamic_slice_in_dim(begin, start_q, block, 0)
        allowed = (key_pos[None, :] <= query_pos[:, None]) & (
            key_pos[None, :] >= query_begin[:, None]
        )
        return (query_block, key_block, value_block, raw, allowed[None])

    def forward_block(index):
        start_q, start_k = window(index)
        query_block, key_block, value_block, raw, allowed = scores_of(start_q, start_k)
        masked = jnp.where(allowed, raw, MASKED)
        highest = jnp.max(masked, axis=-1)
        total = jnp.sum(jnp.exp(masked - highest[:, :, None]), axis=-1)
        log_total = highest + jnp.log(total)
        weights = jnp.exp(masked - log_total[:, :, None]).astype(jnp.bfloat16)
        return (
            jnp.einsum("hqk,khe->qhe", weights, value_block, preferred_element_type=jnp.float32),
            log_total,
        )

    block_ids = jnp.arange(count, dtype=jnp.int32)
    attended_blocks, log_blocks = lax.map(forward_block, block_ids)
    attended = attended_blocks.reshape(length, heads_here, head_size)
    query_heads = queries.astype(jnp.float32)
    key_heads = keys.astype(jnp.float32)
    value_heads = values.astype(jnp.float32)
    query_feat = feature(query_heads)
    key_feat = feature(key_heads)
    states_memory = [memory_start[0]]
    states_norm = [normalizer_start[0]]
    for part in range(segments):
        member = (segment == part).astype(jnp.float32)
        added, grown = memory_delta(
            key_feat, value_heads, member, states_memory[-1], states_norm[-1]
        )
        states_memory.append(states_memory[-1] + added)
        states_norm.append(states_norm[-1] + grown)
    recalled = jnp.zeros_like(attended)
    denominator = jnp.ones((length, heads_here), jnp.float32)
    for part in range(segments):
        numerator = jnp.einsum("tha,hab->thb", query_feat, states_memory[part], precision=PRECISE)
        part_den = jnp.einsum("tha,ha->th", query_feat, states_norm[part], precision=PRECISE)
        inside = segment == part
        recalled = jnp.where(inside[:, None, None], numerator / part_den[:, :, None], recalled)
        denominator = jnp.where(inside[:, None], part_den, denominator)
    mix_flat = jax.nn.sigmoid(lax.dynamic_slice_in_dim(gate_logit, head_first, heads_here, 0))
    mix = mix_flat[None, :, None]
    merged = (
        (mix * recalled + (1.0 - mix) * attended).reshape(length, cols_here).astype(jnp.bfloat16)
    )
    middle = tokens_full + sum_rows(merged, w_out, "tc,cd->td")
    scale_second, unit_second = rms_parts(middle)
    normed_whole_f = gather_rows((unit_second * gain_feed).astype(jnp.bfloat16))
    gate_up = jnp.einsum("td,dpf->tpf", normed_whole_f, f_in, preferred_element_type=jnp.float32)
    gate_part = gate_up[:, 0]
    up_part = gate_up[:, 1]
    activated = jax.nn.silu(gate_part)
    hidden = (activated * up_part).astype(jnp.bfloat16)
    result = middle + sum_rows(hidden, f_out, "tf,fd->td")
    upstream = cotangent.astype(jnp.float32)
    cot_whole = gather_rows(cotangent)
    hidden_grad = jnp.einsum("td,fd->tf", cot_whole, f_out, preferred_element_type=jnp.float32)
    feed_out_local = jnp.einsum("tf,td->fd", hidden, cot_whole, preferred_element_type=jnp.float32)
    sigmoid_gate = jax.nn.sigmoid(gate_part)
    gate_grad = hidden_grad * up_part * sigmoid_gate * (1.0 + gate_part * (1.0 - sigmoid_gate))
    up_grad = hidden_grad * activated
    gate_up_grad = jnp.stack([gate_grad, up_grad], axis=1).astype(jnp.bfloat16)
    normed_second_grad = sum_rows(gate_up_grad, f_in, "tpf,dpf->td")
    gain_feed_part = jnp.sum(normed_second_grad * unit_second, axis=0)
    middle_grad = upstream + rms_back(normed_second_grad * gain_feed, unit_second, scale_second)
    out_grad = middle_grad.astype(jnp.bfloat16)
    out_whole = gather_rows(out_grad)
    attention_out_local = jnp.einsum(
        "tc,td->cd", merged, out_whole, preferred_element_type=jnp.float32
    )
    combined_grad = jnp.einsum(
        "td,cd->tc", out_whole, w_out, preferred_element_type=jnp.float32
    ).reshape(length, heads_here, head_size)
    gate_part_grad = (
        jnp.sum(combined_grad * (recalled - attended), axis=(0, 2)) * mix_flat * (1.0 - mix_flat)
    )
    gate_full = lax.dynamic_update_slice_in_dim(
        jnp.zeros((heads_all,), jnp.float32), gate_part_grad, head_first, 0
    )
    recalled_grad = mix * combined_grad
    attended_grad = ((1.0 - mix) * combined_grad).astype(jnp.bfloat16)
    delta = jnp.einsum("the,the->ht", attended_grad.astype(jnp.float32), attended)

    def back_block(carry, inputs):
        index, log_total = inputs
        start_q, start_k = window(index)
        query_block, key_block, value_block, raw, allowed = scores_of(start_q, start_k)
        grad_block = lax.dynamic_slice_in_dim(attended_grad, start_q, block, 0)
        delta_block = lax.dynamic_slice_in_dim(delta, start_q, block, 1)
        probs = jnp.where(allowed, jnp.exp(raw - log_total[:, :, None]), 0.0)
        prob_grad = jnp.einsum(
            "qhe,khe->hqk", grad_block, value_block, preferred_element_type=jnp.float32
        )
        score_grad = (probs * (prob_grad - delta_block[:, :, None])).astype(jnp.bfloat16)
        query_part = scale * jnp.einsum(
            "hqk,khe->qhe", score_grad, key_block, preferred_element_type=jnp.float32
        )
        key_add = scale * jnp.einsum(
            "hqk,qhe->khe", score_grad, query_block, preferred_element_type=jnp.float32
        )
        value_add = jnp.einsum(
            "hqk,qhe->khe",
            probs.astype(jnp.bfloat16),
            grad_block,
            preferred_element_type=jnp.float32,
        )
        key_acc, value_acc = carry
        key_acc = lax.dynamic_update_slice_in_dim(
            key_acc, lax.dynamic_slice_in_dim(key_acc, start_k, span, 0) + key_add, start_k, 0
        )
        value_acc = lax.dynamic_update_slice_in_dim(
            value_acc, lax.dynamic_slice_in_dim(value_acc, start_k, span, 0) + value_add, start_k, 0
        )
        return ((key_acc, value_acc), query_part)

    empty_heads = jnp.zeros((length, heads_here, head_size), jnp.float32)
    (key_grad, value_grad), query_blocks = lax.scan(
        back_block, (empty_heads, empty_heads), (block_ids, log_blocks)
    )
    query_grad = query_blocks.reshape(length, heads_here, head_size)
    scaled = recalled_grad / denominator[:, :, None]
    denom_grad = -jnp.sum(recalled_grad * recalled, axis=-1) / denominator
    query_feat_grad = jnp.zeros_like(query_feat)
    memory_grads = [None]
    norm_grads = [None]
    for part in range(segments):
        inside = segment == part
        reading = (
            jnp.einsum("thb,hab->tha", scaled, states_memory[part], precision=PRECISE)
            + denom_grad[:, :, None] * states_norm[part][None]
        )
        query_feat_grad = jnp.where(inside[:, None, None], reading, query_feat_grad)
        if part >= 1:
            picked = query_feat * inside.astype(jnp.float32)[:, None, None]
            memory_grads.append(jnp.einsum("tha,thb->hab", picked, scaled, precision=PRECISE))
            norm_grads.append(jnp.sum(denom_grad[:, :, None] * picked, axis=0))
    key_feat_grad = jnp.zeros_like(key_feat)
    value_memory = jnp.zeros_like(value_heads)
    for part in range(segments - 1):
        inside = segment == part
        memory = states_memory[part]
        normalizer = states_norm[part]
        carried_memory = memory_grads[part + 1]
        carried_norm = norm_grads[part + 1]
        key_numerator = jnp.einsum("tha,hab->thb", key_feat, memory, precision=PRECISE)
        key_denominator = jnp.einsum("tha,ha->th", key_feat, normalizer, precision=PRECISE)
        retrieved = key_numerator / key_denominator[:, :, None]
        mismatch = value_heads - retrieved
        mismatch_grad = jnp.einsum("tha,hab->thb", key_feat, carried_memory, precision=PRECISE)
        writing = (
            jnp.einsum("thb,hab->tha", mismatch, carried_memory, precision=PRECISE)
            - jnp.einsum(
                "thb,hab->tha",
                mismatch_grad / key_denominator[:, :, None],
                memory,
                precision=PRECISE,
            )
            + (jnp.sum(mismatch_grad * retrieved, axis=-1) / key_denominator)[:, :, None]
            * normalizer[None]
            + carried_norm[None]
        )
        key_feat_grad = jnp.where(inside[:, None, None], writing, key_feat_grad)
        value_memory = jnp.where(inside[:, None, None], mismatch_grad, value_memory)
    query_total = query_grad + query_feat_grad * feature_slope(query_heads)
    key_total = key_grad + key_feat_grad * feature_slope(key_heads)
    value_total = value_grad + value_memory
    projected_grad = jnp.stack(
        [
            query_total.reshape(length, cols_here),
            key_total.reshape(length, cols_here),
            value_total.reshape(length, cols_here),
        ],
        axis=1,
    ).astype(jnp.bfloat16)
    normed_first_grad = sum_rows(projected_grad, w_in, "tpc,dpc->td")
    gain_attention_part = jnp.sum(normed_first_grad * unit_first, axis=0)
    token_grad = middle_grad + rms_back(normed_first_grad * gain_attention, unit_first, scale_first)
    attention_in_grad = column_grads(normed_whole_a, projected_grad)
    feed_in_grad = column_grads(normed_whole_f, gate_up_grad)
    attention_out_grad, feed_out_grad = (
        lax.psum_scatter(
            attention_out_local.astype(jnp.bfloat16), "seq", scatter_dimension=1, tiled=True
        ).astype(jnp.float32),
        lax.psum_scatter(
            feed_out_local.astype(jnp.bfloat16), "seq", scatter_dimension=1, tiled=True
        ).astype(jnp.float32),
    )
    gain_attention_grad, gain_feed_grad, gate_logit_grad = lax.psum(
        (gain_attention_part, gain_feed_part, gate_full), ("seq", "blk")
    )
    return (
        result.astype(jnp.bfloat16),
        token_grad,
        gain_attention_grad,
        attention_in_grad,
        gate_logit_grad,
        attention_out_grad,
        gain_feed_grad,
        feed_in_grad,
        feed_out_grad,
        states_memory[-1][None],
        states_norm[-1][None],
    )


def solution(mesh):
    in_specs = (
        P(("seq", "blk"), None),
        P(("seq", "blk"), None),
        P("seq", None),
        P("seq", "blk", None, None),
        P("seq", "blk", None),
        P(),
        P("seq", None, "blk"),
        P(),
        P("blk", "seq"),
        P(),
        P("seq", None, "blk"),
        P("blk", "seq"),
    )
    out_specs = (
        P(("seq", "blk"), None),
        P(("seq", "blk"), None),
        P(),
        P("seq", None, "blk"),
        P(),
        P("blk", "seq"),
        P(),
        P("seq", None, "blk"),
        P("blk", "seq"),
        P("seq", "blk", None, None),
        P("seq", "blk", None),
    )
    return jax.shard_map(
        per_device, mesh=mesh, in_specs=in_specs, out_specs=out_specs, check_vma=False
    )
```

profile of v0, /device:TPU:0, one launch (start us, length us, event | category | flops | bytes accessed | tf_op | source)
XLA Modules:
  0.0 1719.8 jit_solution(18118836627334874925)
XLA Ops:
  13.5 27.9 %all-gather.11.cloned.1.call-done = bf16[2048,3,256]{0,2,1:T(8,128)(2,1)} async-done(((bf16[512,3,256]{0,2,1:T(8,128)(2,1)}), bf16[2048,3,256]{0,2,1:T(8,128)(2,1)}) %all-gather.11.cloned.1.call-update) | async-done | bytes 3145744 | tf_op jit(solution)/shard_map/all_gather | solution.py:103
  41.4 127.7 %all-gather.9.cloned.1.call-done = bf16[2048,2048]{1,0:T(8,128)(2,1)} async-done(((bf16[256,2048]{1,0:T(8,128)(2,1)}), bf16[2048,2048]{1,0:T(8,128)(2,1)}) %all-gather.9.cloned.1.call-update) | async-done | bytes 8388624 | tf_op jit(solution)/shard_map/all_gather | solution.py:15
  169.1 10.1 fusion.47
  192.9 89.6 %while.35 = (s32[]{:T(128)}, f32[4,512,2,128]{1,0,3,2:T(4,128)}, f32[4,2,512]{2,1,0:T(2,128)}, s32[4]{0:T(128)S(1)}, s32[2048]{0:T(1024)S(1)}, /*index=5*/bf16[2...) while((s32[]{:T(128)}, f32[4,512,2,128]{1,0,3,2:T(4,128)}, ...), condition=%wide.region_5.6_spmd, body=%wide.region_2.5_spmd.sunk | while | flops 1099957760 | bytes 38595340 | solution.py:157
  204.4 11.1 dynamic_update_slice.42
  226.7 11.1 dynamic_update_slice.42
  249.1 11.1 dynamic_update_slice.42
  271.4 11.1 dynamic_update_slice.42
  282.5 4.2 reshape.330
  300.8 4.5 add_convert_fusion.2
  305.3 7.3 convolution_convert_fusion.1
  316.2 143.8 %reduce-scatter.9.cloned.1.call-done = bf16[256,2048]{1,0:T(8,128)(2,1)} async-done(((bf16[2048,2048]{1,0:T(8,128)(2,1)}), bf16[256,2048]{1,0:T(8,128)(2,1)}) %reduce-scatter.9.cloned.1.call-update) | async-done | bytes 1048592 | tf_op jit(solution)/shard_map/reduce_scatter | solution.py:19
  464.8 54.6 %all-gather.17.cloned.1.call-done = bf16[2048,2,1024]{2,0,1:T(8,128)(2,1)} async-done(((bf16[512,2,1024]{2,0,1:T(8,128)(2,1)}), bf16[2048,2,1024]{2,0,1:T(8,128)(2,1)}) %all-gather.17.cloned.1.call-update) | async-done | bytes 8388624 | tf_op jit(solution)/shard_map/all_gather | solution.py:105
  519.4 127.7 %all-gather.15.cloned.1.call-done = bf16[2048,2048]{1,0:T(8,128)(2,1)} async-done(((bf16[256,2048]{1,0:T(8,128)(2,1)}), bf16[2048,2048]{1,0:T(8,128)(2,1)}) %all-gather.15.cloned.1.call-update) | async-done | bytes 8388624 | tf_op jit(solution)/shard_map/all_gather | solution.py:15
  647.1 24.4 %fusion.35 = f32[2048,2,1024]{2,0,1:T(8,128)} fusion(bf16[2048,2,1024]{2,0,1:T(8,128)(2,1)} %all-gather.17.cloned.1.call-done, bf16[2048,2048]{1,0:T(8,128)(2,1)} %all-gather.15.cloned.1.call-done), kind=kOutput, calls=%fused_computation.52 | convolution fusion | flops 17179869184 | bytes 33554432 | tf_op jit(solution)/shard_map/td,dpf->tpf/dot_general | solution.py:189
  671.5 9.9 all-gather.19.cloned.1.call-done
  681.4 127.3 %all-gather.21.cloned.1.call-done = bf16[2048,2048]{1,0:T(8,128)(2,1)} async-done(((bf16[256,2048]{1,0:T(8,128)(2,1)}), bf16[2048,2048]{1,0:T(8,128)(2,1)}) %all-gather.21.cloned.1.call-update) | async-done | bytes 8388624 | tf_op jit(solution)/shard_map/all_gather | solution.py:15
  808.8 23.6 %fusion.46 = (bf16[2048,1,1024]{2,0,1:T(8,128)(2,1)}, bf16[2048,1,1024]{2,0,1:T(8,128)(2,1)}, bf16[2048,1024]{1,0:T(8,128)(2,1)}) fusion(f32[2048,2,1024]{2,0,1:T(8,128)} %fusion.35, bf16[2048,2048]{1,0:T(8,128)(2,1)} %all-gather.21.cloned.1.call-done, bf16[1024,2048]{1,0:T(8,128)(2,1)} %all-gather.19.cloned.1.call-done), kind=kOutput, calls=%fused_computation.71 | convolution fusion | flops 8621391872 | bytes 41943040 | tf_op jit(solution)/shard_map/td,fd->tf/dot_general | solution.py:197
  832.3 24.0 %bitcast_convert_fusion.1 = bf16[2048,2048]{1,0:T(8,128)(2,1)} fusion(bf16[2048,2,1024]{2,0,1:T(8,128)(2,1)} %all-gather.17.cloned.1.call-done, bf16[2048,1,1024]{2,0,1:T(8,128)(2,1)} %get-tuple-element.545, bf16[2048,1,1024]{2,0,1:T(8,128)(2,1)} %get-tuple-element.544), kind=kOutput, calls=%fused_computation.46 | convolution fusion | flops 17188257792 | bytes 25165824 | tf_op jit(solution)/shard_map/tpf,dpf->td/dot_general | solution.py:20
  856.5 147.3 %reduce-scatter.13.cloned.1.call-done = bf16[256,2048]{1,0:T(8,128)(2,1)} async-done(((bf16[2048,2048]{1,0:T(8,128)(2,1)}), bf16[256,2048]{1,0:T(8,128)(2,1)}) %reduce-scatter.13.cloned.1.call-update) | async-done | bytes 1048592 | tf_op jit(solution)/shard_map/reduce_scatter | solution.py:19
  1009.3 14.1 convolution_convert_fusion.2
  1023.5 24.3 %fusion.42 = bf16[2048,2,1024]{2,0,1:T(8,128)(2,1)} fusion(bf16[2048,1,1024]{2,0,1:T(8,128)(2,1)} %get-tuple-element.545, bf16[2048,1,1024]{2,0,1:T(8,128)(2,1)} %get-tuple-element.544, bf16[2048,2048]{1,0:T(8,128)(2,1)} %all-gather.15.cloned.1.call-done), kind=kOutput, calls=%fused_computation.69 | convolution fusion | flops 17200840704 | bytes 25165824 | tf_op jit(solution)/shard_map/td,tpc->dpc/dot_general | solution.py:29
  1048.0 85.4 %all-gather.23.cloned.1.call-done = bf16[2048,2048]{1,0:T(8,128)(2,1)} async-done(((bf16[256,2048]{1,0:T(8,128)(2,1)}), bf16[2048,2048]{1,0:T(8,128)(2,1)}) %all-gather.23.cloned.1.call-update) | async-done | bytes 8388624 | tf_op jit(solution)/shard_map/all_gather | solution.py:15
  1133.4 5.9 fusion.203
  1143.3 151.9 %while.36 = (s32[]{:T(128)}, f32[2048,2,128]{0,2,1:T(8,128)S(1)}, f32[2048,2,128]{0,2,1:T(8,128)}, f32[4,512,2,128]{1,0,3,2:T(4,128)}, s32[4]{0:T(128)S(1)}, /*i...) while((s32[]{:T(128)}, f32[2048,2,128]{0,2,1:T(8,128)S(1)}, ...), condition=%wide.region_12.13_spmd.clone, body=%wide.region_11.12_spmd.clone.sunk | while | flops 2711226880 | bytes 148429264 | solution.py:257
  1149.6 4.5 multiply_convert_fusion.7
  1160.1 11.1 dynamic_update_slice.43
  1176.1 5.0 fusion.271
  1187.2 4.5 multiply_convert_fusion.7
  1198.2 11.2 dynamic_update_slice.43
  1214.1 5.3 fusion.271
  1225.6 4.5 multiply_convert_fusion.7
  1236.1 11.1 dynamic_update_slice.43
  1252.0 5.4 fusion.271
  1263.6 4.5 multiply_convert_fusion.7
  1274.1 11.1 dynamic_update_slice.43
  1289.9 5.3 fusion.271
  1312.9 4.9 fusion.110
  1331.8 6.8 convolution_convert_fusion.3
  1338.7 11.0 fusion.50
  1350.9 10.9 bitcast_convert_fusion
  1361.8 14.2 convolution_convert_fusion
  1388.0 5.8 copy.57
  1395.8 6.5 reduce-scatter.17.cloned.1.call-done
  1404.7 150.1 %reduce-scatter.15.cloned.1.call-done = bf16[256,2048]{1,0:T(8,128)(2,1)} async-done(((bf16[2048,2048]{1,0:T(8,128)(2,1)}), bf16[256,2048]{1,0:T(8,128)(2,1)}) %reduce-scatter.15.cloned.1.call-update) | async-done | bytes 1048592 | tf_op jit(solution)/shard_map/reduce_scatter | solution.py:19
  1557.0 43.1 %all-reduce = (f32[2048]{0:T(1024)}, f32[16]{0:T(128)}, f32[2048]{0:T(1024)}) all-reduce(f32[2048]{0:T(1024)S(1)} %get-tuple-element.489, f32[16]{0:T(128)S(1)} %multiply_dynamic-update-slice_fusion, f32[2048]{0:T(1024)S(1)} %copy-done.53), channel_id=1, replica_groups=mesh['seq'=4,'blk'=8] {'seq','blk'}, use_global_device_ids=true, to_apply=%region_19.20 | all-reduce | flops 4112 | bytes 32896 | tf_op jit(solution)/shard_map/psum | solution.py:328
  1600.1 107.7 %reduce-scatter.11.cloned.1.call-done = bf16[256,2048]{1,0:T(8,128)(2,1)} async-done(((bf16[2048,2048]{1,0:T(8,128)(2,1)}), bf16[256,2048]{1,0:T(8,128)(2,1)}) %reduce-scatter.11.cloned.1.call-update) | async-done | bytes 1048592 | tf_op jit(solution)/shard_map/reduce_scatter | solution.py:19
  1707.8 5.2 fusion.84
  (385 shorter events, 209.9 us)
Async XLA Ops:
  7.2 34.2 %all-gather.11.cloned.1.call-start = ((), (), s32[]{:S(2)}) async-start(), calls=%async_computation.9 | async-start | bytes 3932160 | tf_op jit(solution)/shard_map/all_gather | solution.py:103
  9.7 159.5 %all-gather.9.cloned.1.call-start = ((), (), s32[]{:S(2)}) async-start(), calls=%async_computation.8 | async-start | bytes 9437184 | tf_op jit(solution)/shard_map/all_gather | solution.py:15
  11.9 293.4 %all-gather.13.cloned.1.call-start = ((), (), s32[]{:S(2)}) async-start(), calls=%async_computation.10 | async-start | bytes 1310720 | tf_op jit(solution)/shard_map/all_gather | solution.py:104
  12.6 447.3 %reduce-scatter.9.cloned.1.call-start = ((), (), s32[]{:S(2)}) async-start(), calls=%async_computation.11 | async-start | bytes 9437184 | tf_op jit(solution)/shard_map/reduce_scatter | solution.py:19
  13.4 284.0 %copy-start.56 = (pred[2048]{0:T(1024)(128)(4,1)}, pred[2048]{0:T(1024)(128)(4,1)S(1)}, u32[]{:S(2)}) copy-start(pred[2048]{0:T(1024)(128)(4,1)S(1)} %get-tuple-element.560) | copy-start | bytes 6148
  13.4 287.3 %copy-start.66 = (pred[2048]{0:T(1024)(128)(4,1)}, pred[2048]{0:T(1024)(128)(4,1)S(1)}, u32[]{:S(2)}) copy-start(pred[2048]{0:T(1024)(128)(4,1)S(1)} %broadcast_compare_fusion) | copy-start | bytes 6148
  13.5 287.2 %copy-start.68 = (f32[2]{0:T(128)}, f32[2]{0:T(128)S(1)}, u32[]{:S(2)}) copy-start(f32[2]{0:T(128)S(1)} %get-tuple-element.541) | copy-start | bytes 28
  13.5 287.2 %copy-start.72 = (f32[2]{0:T(128)}, f32[2]{0:T(128)S(1)}, u32[]{:S(2)}) copy-start(f32[2]{0:T(128)S(1)} %get-tuple-element.540) | copy-start | bytes 28
  184.3 5.6 copy-start.47
  190.0 96.8 %copy-start.49 = (f32[2,1,2048]{2,1,0:T(1,128)}, f32[2,1,2048]{2,1,0:T(1,128)S(1)}, u32[]{:S(2)}) copy-start(f32[2,1,2048]{2,1,0:T(1,128)S(1)} %fusion.116) | copy-start | bytes 49156
  190.0 99.2 %copy-start.60 = (f32[2,1,2048]{2,0,1:T(2,128)}, f32[2,1,2048]{2,0,1:T(2,128)S(1)}, u32[]{:S(2)}) copy-start(f32[2,1,2048]{2,0,1:T(2,128)S(1)} %copy.125) | copy-start | bytes 49156
  282.5 6.7 copy-start.17
  282.5 6.7 copy-start.78
  305.3 7.3 copy-start.35
  312.6 206.7 %all-gather.17.cloned.1.call-start = ((), (), s32[]{:S(2)}) async-start(), calls=%async_computation.13 | async-start | bytes 10485760 | tf_op jit(solution)/shard_map/all_gather | solution.py:105
  316.1 145.6 %copy-start.42 = (f32[2048]{0:T(1024)S(1)}, f32[2048]{0:T(1024)}, u32[]{:S(2)}) copy-start(f32[2048]{0:T(1024)} %param.25) | copy-start | bytes 24580
  316.2 330.9 %all-gather.15.cloned.1.call-start = ((), (), s32[]{:S(2)}) async-start(), calls=%async_computation.12 | async-start | bytes 9437184 | tf_op jit(solution)/shard_map/all_gather | solution.py:15
  461.7 544.9 %copy-start.54 = (f32[256]{0:T(256)}, f32[256]{0:T(256)S(1)}, u32[]{:S(2)}) copy-start(f32[256]{0:T(256)S(1)} %add_rsqrt_fusion) | copy-start | bytes 3076
  463.3 218.2 %all-gather.19.cloned.1.call-start = ((), (), s32[]{:S(2)}) async-start(), calls=%async_computation.14 | async-start | bytes 5242880 | tf_op jit(solution)/shard_map/all_gather | solution.py:106
  464.0 344.7 %all-gather.21.cloned.1.call-start = ((), (), s32[]{:S(2)}) async-start(), calls=%async_computation.16 | async-start | bytes 9437184 | tf_op jit(solution)/shard_map/all_gather | solution.py:15
  464.8 539.0 %reduce-scatter.13.cloned.1.call-start = ((), (), s32[]{:S(2)}) async-start(), calls=%async_computation.17 | async-start | bytes 9437184 | tf_op jit(solution)/shard_map/reduce_scatter | solution.py:19
  856.4 150.8 %copy-start.13 = (bf16[256,2048]{1,0:T(8,128)(2,1)S(1)}, bf16[256,2048]{1,0:T(8,128)(2,1)}, u32[]{:S(2)}) copy-start(bf16[256,2048]{1,0:T(8,128)(2,1)} %param.17) | copy-start | bytes 3145732
  856.4 276.9 %all-gather.23.cloned.1.call-start = ((), (), s32[]{:S(2)}) async-start(), calls=%async_computation.18 | async-start | bytes 9437184 | tf_op jit(solution)/shard_map/all_gather | solution.py:15
  1009.3 375.9 %reduce-scatter.23.cloned.1.call-start = ((), (), s32[]{:S(2)}) async-start(), calls=%async_computation.23 | async-start | bytes 5242880 | tf_op jit(solution)/shard_map/reduce_scatter | solution.py:324
  1023.5 364.5 %reduce-scatter.21.cloned.1.call-start = ((), (), s32[]{:S(2)}) async-start(), calls=%async_computation.22 | async-start | bytes 10485760 | tf_op jit(solution)/shard_map/reduce_scatter | solution.py:28
  1047.9 85.5 %copy-start.37 = (bf16[256,2048]{1,0:T(8,128)(2,1)S(1)}, bf16[256,2048]{1,0:T(8,128)(2,1)}, u32[]{:S(2)}) copy-start(bf16[256,2048]{1,0:T(8,128)(2,1)} %all-gather.13.cloned.1.call-done) | copy-start | bytes 3145732
  1047.9 91.4 %copy-start.69 = (f32[2]{0:T(128)S(1)}, f32[2]{0:T(128)}, u32[]{:S(2)}) copy-start(f32[2]{0:T(128)} %copy-done.68) | copy-start | bytes 28
  1047.9 91.4 %copy-start.73 = (f32[2]{0:T(128)S(1)}, f32[2]{0:T(128)}, u32[]{:S(2)}) copy-start(f32[2]{0:T(128)} %copy-done.72) | copy-start | bytes 28
  1047.9 346.0 %reduce-scatter.19.cloned.1.call-start = ((), (), s32[]{:S(2)}) async-start(), calls=%async_computation.21 | async-start | bytes 1310720 | tf_op jit(solution)/shard_map/reduce_scatter | solution.py:321
  1133.4 5.9 copy-start.11
  1133.4 5.9 copy-start.31
  1148.9 5.2 copy-start.1
  1186.5 5.2 copy-start.1
  1262.8 5.2 copy-start.1
  1331.8 6.8 copy-start.40
  1338.6 63.7 %reduce-scatter.17.cloned.1.call-start = ((), (), s32[]{:S(2)}) async-start(), calls=%async_computation.20 | async-start | bytes 3932160 | tf_op jit(solution)/shard_map/reduce_scatter | solution.py:28
  1349.7 205.2 %reduce-scatter.15.cloned.1.call-start = ((), (), s32[]{:S(2)}) async-start(), calls=%async_computation.19 | async-start | bytes 9437184 | tf_op jit(solution)/shard_map/reduce_scatter | solution.py:19
  1361.8 346.0 %reduce-scatter.11.cloned.1.call-start = ((), (), s32[]{:S(2)}) async-start(), calls=%async_computation.15 | async-start | bytes 9437184 | tf_op jit(solution)/shard_map/reduce_scatter | solution.py:19
  1388.0 5.8 copy-start.74
  1393.8 161.1 %copy-start.6 = (bf16[256,2048]{1,0:T(8,128)(2,1)S(1)}, bf16[256,2048]{1,0:T(8,128)(2,1)}, u32[]{:S(2)}) copy-start(bf16[256,2048]{1,0:T(8,128)(2,1)} %param.16) | copy-start | bytes 3145732
  1393.8 161.1 %copy-start.46 = (f32[2048]{0:T(1024)S(1)}, f32[2048]{0:T(1024)}, u32[]{:S(2)}) copy-start(f32[2048]{0:T(1024)} %param.21) | copy-start | bytes 24580
  1393.8 161.1 %copy-start.59 = (f32[256]{0:T(256)S(1)}, f32[256]{0:T(256)}, u32[]{:S(2)}) copy-start(f32[256]{0:T(256)} %copy-done.58) | copy-start | bytes 3076
  1395.8 161.2 %copy-start.53 = (f32[2048]{0:T(1024)S(1)}, f32[2048]{0:T(1024)}, u32[]{:S(2)}) copy-start(f32[2048]{0:T(1024)} %get-tuple-element.487) | copy-start | bytes 24580
  1395.8 312.0 %copy-start.8 = (bf16[256,2048]{1,0:T(8,128)(2,1)S(1)}, bf16[256,2048]{1,0:T(8,128)(2,1)}, u32[]{:S(2)}) copy-start(bf16[256,2048]{1,0:T(8,128)(2,1)} %reduce-scatter.9.cloned.1.call-done) | copy-start | bytes 3145732
  1395.8 312.0 %copy-start.14 = (bf16[256,2048]{1,0:T(8,128)(2,1)S(1)}, bf16[256,2048]{1,0:T(8,128)(2,1)}, u32[]{:S(2)}) copy-start(bf16[256,2048]{1,0:T(8,128)(2,1)} %param.17) | copy-start | bytes 3145732
  1395.8 312.0 %copy-start.43 = (f32[2048]{0:T(1024)S(1)}, f32[2048]{0:T(1024)}, u32[]{:S(2)}) copy-start(f32[2048]{0:T(1024)} %param.25) | copy-start | bytes 24580
  1395.8 312.0 %copy-start.55 = (f32[256]{0:T(256)S(1)}, f32[256]{0:T(256)}, u32[]{:S(2)}) copy-start(f32[256]{0:T(256)} %copy-done.54) | copy-start | bytes 3076
  1395.8 312.0 %copy-start.63 = (f32[256]{0:T(256)S(1)}, f32[256]{0:T(256)}, u32[]{:S(2)}) copy-start(f32[256]{0:T(256)} %copy-done.62) | copy-start | bytes 3076
  (68 other events, 209.6 us)
Sparse Core Ops, SparseCore 0:
  10.2 31.2 all-gather.10
  44.1 124.9 all-gather.8
  170.7 14.8 all-gather.12
  312.8 147.1 reduce-scatter.8
  462.0 57.2 all-gather.16
  522.1 124.9 all-gather.14
  648.7 32.6 all-gather.18
  683.8 124.9 all-gather.20
  856.5 147.1 reduce-scatter.12
  1009.4 123.9 all-gather.22
  1135.9 42.6 reduce-scatter.22
  1181.2 71.7 reduce-scatter.20
  1338.7 23.0 reduce-scatter.18
  1364.3 37.9 reduce-scatter.16
  1405.8 149.0 reduce-scatter.14
  1558.8 148.9 reduce-scatter.10
where the time goes:
time: 1730 us; the launch traced here: 1720 us
  waiting for transfers between devices  1120 us (65%)
  matrix products  321 us (19%)
  local copies, waits for them, and re-layouts  162 us (9%)
  other arithmetic  53 us (3%)
  blocking collectives  43.1 us (2%)
    reduce_scatter x4, waiting for transfers between devices, sum_rows(): lax.psum_scatter(jnp.einsum(form, left, right, preferred_element_type=jnp...  549 us
    all_gather x4, waiting for transfers between devices, gather_rows(): return lax.all_gather(values, 'blk', axis=0, tiled=True)  468 us
    dynamic_update_slice x16, local copies, waits for them, and re-layouts, per_device(): attended_blocks, log_blocks = lax.map(forward_block, block_ids)  98.2 us
    dot_general x4, matrix products, sum_rows(): jnp.einsum(form, left, right, preferred_element_type=jnp.float32)  56.4 us
    all_gather x1, waiting for transfers between devices, per_device(): lax.all_gather(feed_in, 'seq', axis=0, tiled=True)  54.6 us
    psum x1, blocking collectives, per_device(): lax.psum((gain_attention_part, gain_feed_part, gate_full), ('seq', 'blk'))  43.1 us
    dot_general x2, matrix products, column_grads(): jnp.einsum('td,tpc->dpc', left, gradient, preferred_element_type=jnp.floa...  35.3 us
  transfers between devices with their start and end apart: 16, of which 12 were waited for; matrix products, arithmetic and copies ran while one was open for 26% of the time, Pallas kernels for 0%

commit v1 on v0

v1 whole, which is shorter than its diff:
```python
import functools
import math

import jax
import jax.numpy as jnp
from jax import lax
from jax.experimental import pallas as pl
from jax.experimental.pallas import tpu as pltpu
from jax.sharding import PartitionSpec as P

SHORT = 1024
TILE = 512
EPSILON = 1e-06
MASKED = -1e30
LOG2E = math.log2(math.e)
VMEM_LIMIT = 48 * 1024 * 1024


def dot_nn(left, right):
    return lax.dot_general(left, right, (((1,), (0,)), ((), ())), preferred_element_type=jnp.float32)


def dot_nt(left, right):
    return lax.dot_general(left, right, (((1,), (1,)), ((), ())), preferred_element_type=jnp.float32)


def dot_tn(left, right):
    return lax.dot_general(left, right, (((0,), (0,)), ((), ())), preferred_element_type=jnp.float32)


def low(values):
    return values.astype(jnp.bfloat16)


def feature(values):
    return jnp.where(values > 0, values + 1.0, jnp.exp(jnp.minimum(values, 0.0)))


def first_key_tile(index, splits):
    per = 2 * SHORT // TILE
    slot = lax.div(index, per)
    second = (lax.rem(index, per) >= per // 2) & (splits[slot] == 1)
    return slot * per + jnp.where(second, per // 2, 0)


def tile_rows(index):
    return pl.ds(pl.multiple_of(index * TILE, TILE), TILE)


def causal(scores):
    key_pos = lax.broadcasted_iota(jnp.int32, scores.shape, 0)
    query_pos = lax.broadcasted_iota(jnp.int32, scores.shape, 1)
    return jnp.where(key_pos <= query_pos, scores, MASKED)


def state_matrix(memory, norm_row):
    spread = jnp.transpose(jnp.broadcast_to(norm_row, memory.shape))
    return low(jnp.concatenate([memory, spread], axis=1))


def forward_kernel(
    order, splits, mix, proj, memory, norm,
    merged, attended, lse, states, norms, memory_out, norm_out,
    q_s, k_s, v_s, vt_s, *, rows, heads, size,
):
    length = proj.shape[0]
    width = heads * size
    factor = size ** (-0.5) * LOG2E
    for b in range(length // rows):
        src = pl.ds(pl.multiple_of(order[b] * rows, rows), rows)
        dst = slice(b * rows, (b + 1) * rows)
        q_s[dst, :] = proj[src, 0:width]
        k_s[dst, :] = proj[src, width : 2 * width]
        value = proj[src, 2 * width : 3 * width]
        v_s[dst, :] = value
        vt_s[:, dst] = jnp.transpose(value)
    cols = [slice(h * size, (h + 1) * size) for h in range(heads)]

    def query_block(index, _):
        here = tile_rows(index)
        queries = [q_s[here, c] for c in cols]

        def scores_of(tile, h):
            return dot_nt(k_s[tile_rows(tile), cols[h]], queries[h]) * factor

        def weigh(tile, h, scores, highest):
            weights = jnp.exp2(scores - highest)
            total = jnp.sum(weights, axis=0, keepdims=True)
            return total, dot_nn(vt_s[cols[h], tile_rows(tile)], low(weights))

        start = []
        for h in range(heads):
            scores = causal(scores_of(index, h))
            highest = jnp.max(scores, axis=0, keepdims=True)
            start.append((highest, *weigh(index, h, scores, highest)))

        def step(tile, carry):
            out = []
            for h in range(heads):
                highest, total, acc = carry[h]
                scores = scores_of(tile, h)
                higher = jnp.maximum(highest, jnp.max(scores, axis=0, keepdims=True))
                keep = jnp.exp2(highest - higher)
                more, add = weigh(tile, h, scores, higher)
                out.append((higher, total * keep + more, acc * keep + add))
            return tuple(out)

        done = lax.fori_loop(first_key_tile(index, splits), index, step, tuple(start))
        for h in range(heads):
            highest, total, acc = done[h]
            attended[here, cols[h]] = jnp.transpose(acc / total)
            lse[index, h : h + 1, :] = highest + jnp.log2(total)
        return 0

    lax.fori_loop(0, length // TILE, query_block, 0)

    for h in range(heads):
        total_m, total_n = memory[h], norm[h : h + 1, :]
        now_m, now_n = total_m, total_n
        share = mix[h]
        for half in range(length // SHORT):
            fresh = True if half % 2 == 0 else splits[half // 2] == 1
            now_m = jnp.where(fresh, total_m, now_m)
            now_n = jnp.where(fresh, total_n, now_n)
            states[half, h] = now_m
            norms[half, h : h + 1, :] = now_n
            both = state_matrix(now_m, now_n)

            def chunk(index, carry):
                here = tile_rows(index)
                grown_m, grown_n = carry
                query_feat = feature(q_s[here, cols[h]].astype(jnp.float32))
                key_feat = feature(k_s[here, cols[h]].astype(jnp.float32))
                read = dot_nn(low(query_feat), both)
                recalled = read[:, :size] / read[:, size:]
                merged[here, cols[h]] = low(share * recalled + (1.0 - share) * attended[here, cols[h]])
                back = dot_nn(low(key_feat), both)
                miss = v_s[here, cols[h]].astype(jnp.float32) - back[:, :size] / back[:, size:]
                return (
                    grown_m + dot_tn(low(key_feat), low(miss)),
                    grown_n + jnp.sum(key_feat, axis=0, keepdims=True),
                )

            per = SHORT // TILE
            total_m, total_n = lax.fori_loop(half * per, (half + 1) * per, chunk, (total_m, total_n))
        memory_out[h] = total_m
        norm_out[h : h + 1, :] = total_n


def backward_kernel(
    order, splits, mix, proj, combined_grad, attended, lse, states, norms,
    proj_grad, gate,
    q_s, k_s, v_s, kt_s, g_s, delta_s, dq_s, dk_s, dv_s, *, rows, heads, size,
):
    length = proj.shape[0]
    width = heads * size
    scale = size ** (-0.5)
    factor = scale * LOG2E
    for b in range(length // rows):
        src = pl.ds(pl.multiple_of(order[b] * rows, rows), rows)
        dst = slice(b * rows, (b + 1) * rows)
        q_s[dst, :] = proj[src, 0:width]
        key = proj[src, width : 2 * width]
        k_s[dst, :] = key
        v_s[dst, :] = proj[src, 2 * width : 3 * width]
        kt_s[:, dst] = jnp.transpose(key)
    cols = [slice(h * size, (h + 1) * size) for h in range(heads)]
    ones = jnp.ones((8, size), jnp.float32)
    slots = length // (2 * SHORT)
    per = SHORT // TILE

    for h in range(heads):
        share = mix[h]
        col = cols[h]
        gate_sum = jnp.zeros((1, size), jnp.float32)
        next_m, next_n = jnp.zeros((size, size), jnp.float32), jnp.zeros((1, size), jnp.float32)
        for slot in reversed(range(slots)):
            split = splits[slot] == 1
            later_m, later_n = None, None
            for half in (2 * slot + 1, 2 * slot):
                last = half == 2 * slots - 1
                if half % 2 == 1:
                    up_m, up_n = next_m, next_n
                else:
                    up_m = jnp.where(split, later_m, next_m)
                    up_n = jnp.where(split, later_n, next_n)
                memory = states[half, h]
                norm_row = norms[half, h : h + 1, :]
                both = state_matrix(memory, norm_row)
                low_memory = low(memory)
                low_up = low(up_m)
                up_both = jnp.concatenate([low_up, low_memory], axis=1)

                def chunk(index, carry, both=both, low_memory=low_memory, low_up=low_up, up_both=up_both, norm_row=norm_row, up_n=up_n, last=last):
                    here = tile_rows(index)
                    sum_m, sum_n, sum_gate = carry
                    att = attended[here, col]
                    grad = combined_grad[here, col].astype(jnp.float32)
                    query_feat = feature(q_s[here, col].astype(jnp.float32))
                    read = dot_nn(low(query_feat), both)
                    inverse = 1.0 / read[:, size:]
                    recalled = read[:, :size] * inverse
                    recalled_grad = share * grad
                    attended_grad = low((1.0 - share) * grad)
                    g_s[here, col] = attended_grad
                    sums = lax.dot_general(
                        ones, attended_grad.astype(jnp.float32) * att, (((1,), (1,)), ((), ())),
                        precision=lax.Precision.HIGHEST, preferred_element_type=jnp.float32,
                    )
                    delta_s[index, h : h + 1, :] = sums[0:1, :]
                    sum_gate = sum_gate + jnp.sum(grad * (recalled - att), axis=0, keepdims=True)
                    scaled = recalled_grad * inverse
                    den_grad = -jnp.sum(recalled_grad * recalled, axis=1, keepdims=True) * inverse
                    query_feat_grad = dot_nt(low(scaled), low_memory) + den_grad * norm_row
                    dq_s[here, col] = query_feat_grad * jnp.minimum(query_feat, 1.0)
                    sum_m = sum_m + dot_tn(low(query_feat), low(scaled))
                    sum_n = sum_n + jnp.sum(den_grad * query_feat, axis=0, keepdims=True)
                    if last:
                        dk_s[here, col] = jnp.zeros((TILE, size), jnp.float32)
                        dv_s[here, col] = jnp.zeros((TILE, size), jnp.float32)
                    else:
                        key_feat = feature(k_s[here, col].astype(jnp.float32))
                        back = dot_nn(low(key_feat), both)
                        key_inverse = 1.0 / back[:, size:]
                        retrieved = back[:, :size] * key_inverse
                        miss = v_s[here, col].astype(jnp.float32) - retrieved
                        miss_grad = dot_nn(low(key_feat), low_up)
                        dv_s[here, col] = miss_grad
                        pair = jnp.concatenate([low(miss), low(-miss_grad * key_inverse)], axis=1)
                        along = jnp.sum(miss_grad * retrieved, axis=1, keepdims=True) * key_inverse
                        key_feat_grad = dot_nt(pair, up_both) + along * norm_row + up_n
                        dk_s[here, col] = key_feat_grad * jnp.minimum(key_feat, 1.0)
                    return sum_m, sum_n, sum_gate

                sum_m, sum_n, gate_sum = lax.fori_loop(
                    half * per, (half + 1) * per, chunk,
                    (jnp.zeros((size, size), jnp.float32), jnp.zeros((1, size), jnp.float32), gate_sum),
                )
                if half % 2 == 1:
                    later_m, later_n = sum_m, sum_n
                else:
                    next_m = jnp.where(split, sum_m, sum_m + later_m)
                    next_n = jnp.where(split, sum_n, sum_n + later_n)
        gate[h : h + 1, :] = gate_sum

    def query_block(index, _):
        here = tile_rows(index)

        def part(tile, h, mask):
            there = tile_rows(tile)
            col = cols[h]
            queries, grads, keys = q_s[here, col], g_s[here, col], k_s[there, col]
            scores = dot_nt(keys, queries) * factor
            if mask:
                scores = causal(scores)
            probs = jnp.exp2(scores - lse[index, h : h + 1, :])
            prob_grad = dot_nt(v_s[there, col], grads)
            score_grad = low(probs * (prob_grad - delta_s[index, h : h + 1, :]))
            dv_s[there, col] += dot_nn(low(probs), grads)
            dk_s[there, col] += dot_nn(score_grad, queries) * scale
            return dot_nn(kt_s[col, there], score_grad)

        start = tuple(part(index, h, True) for h in range(heads))

        def step(tile, carry):
            return tuple(carry[h] + part(tile, h, False) for h in range(heads))

        done = lax.fori_loop(first_key_tile(index, splits), index, step, start)
        for h in range(heads):
            dq_s[here, cols[h]] += jnp.transpose(done[h]) * scale
        return 0

    lax.fori_loop(0, length // TILE, query_block, 0)
    for b in range(length // rows):
        dst = pl.ds(pl.multiple_of(order[b] * rows, rows), rows)
        src = slice(b * rows, (b + 1) * rows)
        proj_grad[dst, 0:width] = low(dq_s[src, :])
        proj_grad[dst, width : 2 * width] = low(dk_s[src, :])
        proj_grad[dst, 2 * width : 3 * width] = low(dv_s[src, :])


SMEM = pl.BlockSpec(memory_space=pltpu.SMEM)
VMEM = pl.BlockSpec(memory_space=pltpu.VMEM)


def attend_forward(order, splits, mix, proj, memory, norm, rows):
    heads, size, _ = memory.shape
    length, width = proj.shape[0], heads * size
    halves, tiles = length // SHORT, length // TILE
    shapes = [
        jax.ShapeDtypeStruct((length, width), jnp.bfloat16),
        jax.ShapeDtypeStruct((length, width), jnp.float32),
        jax.ShapeDtypeStruct((tiles, heads, TILE), jnp.float32),
        jax.ShapeDtypeStruct((halves, heads, size, size), jnp.float32),
        jax.ShapeDtypeStruct((halves, heads, size), jnp.float32),
        jax.ShapeDtypeStruct((heads, size, size), jnp.float32),
        jax.ShapeDtypeStruct((heads, size), jnp.float32),
    ]
    whole = pltpu.VMEM((length, width), jnp.bfloat16)
    return pl.pallas_call(
        functools.partial(forward_kernel, rows=rows, heads=heads, size=size),
        out_shape=shapes,
        in_specs=[SMEM] * 3 + [VMEM] * 3,
        out_specs=[VMEM] * len(shapes),
        scratch_shapes=[whole, whole, whole, pltpu.VMEM((width, length), jnp.bfloat16)],
        compiler_params=pltpu.CompilerParams(vmem_limit_bytes=VMEM_LIMIT),
        cost_estimate=pl.CostEstimate(
            flops=4 * length * length * width, bytes_accessed=12 * length * width, transcendentals=0
        ),
    )(order, splits, mix, proj, memory, norm)


def attend_backward(order, splits, mix, proj, combined_grad, attended, lse, states, norms, rows):
    _, heads, size, _ = states.shape
    length, width = proj.shape[0], heads * size
    tiles = length // TILE
    shapes = [
        jax.ShapeDtypeStruct((length, 3 * width), jnp.bfloat16),
        jax.ShapeDtypeStruct((heads, size), jnp.float32),
    ]
    whole = pltpu.VMEM((length, width), jnp.bfloat16)
    wide = pltpu.VMEM((length, width), jnp.float32)
    return pl.pallas_call(
        functools.partial(backward_kernel, rows=rows, heads=heads, size=size),
        out_shape=shapes,
        in_specs=[SMEM] * 3 + [VMEM] * 6,
        out_specs=[VMEM] * len(shapes),
        scratch_shapes=[
            whole, whole, whole, pltpu.VMEM((width, length), jnp.bfloat16), whole,
            pltpu.VMEM((tiles, heads, TILE), jnp.float32), wide, wide, wide,
        ],
        compiler_params=pltpu.CompilerParams(vmem_limit_bytes=VMEM_LIMIT),
        cost_estimate=pl.CostEstimate(
            flops=10 * length * length * width, bytes_accessed=20 * length * width, transcendentals=0
        ),
    )(order, splits, mix, proj, combined_grad, attended, lse, states, norms)


def ring_of(count):
    deep = 4 if count % 4 == 0 else count
    across = count // deep
    ring = [z * across for z in range(deep)]
    for z in reversed(range(deep)):
        turn = range(1, across)
        ring += [z * across + y for y in (turn if (deep - 1 - z) % 2 == 0 else reversed(turn))]
    return ring


class Ring:
    def __init__(self, count):
        self.count = count
        ring = ring_of(count)
        self.ahead = [(ring[p], ring[(p + 1) % count]) for p in range(count)]
        self.behind = [(b, a) for a, b in self.ahead]
        places = [0] * count
        for place, index in enumerate(ring):
            places[index] = place
        places = jnp.array(places, jnp.int32)
        self.order = lax.rem(places - places[lax.axis_index("blk")] + count, count)

    def forth(self, values):
        return lax.ppermute(values, "blk", self.ahead)

    def back(self, values):
        return lax.ppermute(values, "blk", self.behind)

    def gather(self, block):
        half = self.count // 2
        middle = block.shape[0] // 2
        blocks = {0: block}
        arrival = [0]
        from_behind = from_ahead = block
        for step in range(1, half):
            from_behind = self.forth(from_behind)
            from_ahead = self.back(from_ahead)
            blocks[self.count - step] = from_behind
            blocks[step] = from_ahead
            arrival += [self.count - step, step]
        blocks[half] = jnp.concatenate([self.forth(from_behind[:middle]), self.back(from_ahead[middle:])])
        arrival.append(half)
        return blocks, arrival

    def scatter(self, partial):
        half = self.count // 2
        far = low(partial(half))
        middle = far.shape[0] // 2
        forward = self.forth(far[:middle])
        backward = self.back(far[middle:])
        for step in range(half - 1, 0, -1):
            forward, backward = forward.astype(jnp.float32), backward.astype(jnp.float32)
            if step == half - 1:
                forward = jnp.pad(forward, ((0, middle), (0, 0)))
                backward = jnp.pad(backward, ((middle, 0), (0, 0)))
            forward = self.forth(low(partial(step) + forward))
            backward = self.back(low(partial(self.count - step) + backward))
        return partial(0) + forward.astype(jnp.float32) + backward.astype(jnp.float32)


def sum_everywhere(values):
    for axis in ("seq", "blk"):
        size = lax.axis_size(axis)
        step = 1
        while step < size:
            values = values + lax.ppermute(values, axis, [(i, i ^ step) for i in range(size)])
            step *= 2
    return values


def rms_parts(values):
    scale_rows = lax.rsqrt(jnp.mean(values * values, axis=-1, keepdims=True) + EPSILON)
    return (scale_rows, values * scale_rows)


def rms_back(unit_grad, unit, scale_rows):
    return scale_rows * (unit_grad - unit * jnp.mean(unit_grad * unit, axis=-1, keepdims=True))


def joined(blocks):
    return jnp.concatenate([blocks[d] for d in range(len(blocks))])


def sum_over_seq(values, dimension):
    return lax.psum_scatter(low(values), "seq", scatter_dimension=dimension, tiled=True)


def per_device(
    tokens,
    cotangent,
    grouping,
    memory_start,
    normalizer_start,
    gain_attention,
    attention_in,
    gate_logit,
    attention_out,
    gain_feed,
    feed_in,
    feed_out,
):
    rows, width = tokens.shape
    heads_here = memory_start.shape[1]
    count = lax.axis_size("blk")
    ring = Ring(count)
    splits = grouping[0]
    head_first = lax.axis_index("blk") * heads_here
    mix = jax.nn.sigmoid(lax.dynamic_slice_in_dim(gate_logit, head_first, heads_here, 0))

    def whole(weight, axis):
        return lax.all_gather(weight, "seq", axis=axis, tiled=True)

    w_in = whole(attention_in.reshape(attention_in.shape[0], -1), 0)
    w_out = whole(lax.all_gather(attention_out, "blk", axis=0, tiled=True), 1)
    f_in = whole(feed_in.reshape(feed_in.shape[0], -1), 0)
    f_out = whole(feed_out, 1)
    hidden_here = f_out.shape[0]

    tokens_full = tokens.astype(jnp.float32)
    scale_first, unit_first = rms_parts(tokens_full)
    normed_a, arrival = ring.gather(low(unit_first * gain_attention))
    proj = joined({d: low(dot_nn(normed_a[d], w_in)) for d in arrival})
    merged, attended, lse, states, norms, memory_final, norm_final = attend_forward(
        ring.order, splits, mix, proj, memory_start[0], normalizer_start[0], rows
    )
    merged_mine = lax.all_to_all(merged, "blk", 0, 1, tiled=True)
    middle = tokens_full + dot_nn(merged_mine, w_out)
    scale_second, unit_second = rms_parts(middle)

    cot, _ = ring.gather(cotangent)
    normed_f, arrival = ring.gather(low(unit_second * gain_feed))
    hidden, gate_up_grad = {}, {}
    for d in arrival:
        gate_up = dot_nn(normed_f[d], f_in)
        gate, up = gate_up[:, :hidden_here], gate_up[:, hidden_here:]
        sigmoid_gate = jax.nn.sigmoid(gate)
        activated = gate * sigmoid_gate
        hidden[d] = low(activated * up)
        hidden_grad = dot_nt(cot[d], f_out)
        gate_grad = hidden_grad * up * sigmoid_gate * (1.0 + gate * (1.0 - sigmoid_gate))
        gate_up_grad[d] = low(jnp.concatenate([gate_grad, hidden_grad * activated], axis=1))
    normed_f_grad = ring.scatter(lambda d: dot_nt(gate_up_grad[d], f_in))
    gain_feed_part = jnp.sum(normed_f_grad * unit_second, axis=0)
    middle_grad = cotangent.astype(jnp.float32) + rms_back(
        normed_f_grad * gain_feed, unit_second, scale_second
    )
    out_grad = low(middle_grad)
    combined_grad = lax.all_to_all(low(dot_nt(out_grad, w_out)), "blk", 1, 0, tiled=True)
    proj_grad, gate_rows = attend_backward(
        ring.order, splits, mix, proj, combined_grad, attended, lse, states, norms, rows
    )
    result = middle + ring.scatter(lambda d: dot_nn(hidden[d], f_out))

    normed_a_grad = ring.scatter(lambda d: dot_nt(proj_grad[d * rows : (d + 1) * rows], w_in))
    token_grad = middle_grad + rms_back(normed_a_grad * gain_attention, unit_first, scale_first)

    feed_out_grad = sum_over_seq(dot_tn(joined(hidden), joined(cot)), 1)
    feed_in_grad = sum_over_seq(dot_tn(joined(normed_f), joined(gate_up_grad)), 0)
    attention_out_grad = lax.psum_scatter(
        sum_over_seq(dot_tn(merged_mine, out_grad), 1), "blk", scatter_dimension=0, tiled=True
    )
    attention_in_local = dot_tn(joined(normed_a), proj_grad)
    attention_in_grad = sum_over_seq(attention_in_local, 0)
    gain_attention_part = jnp.sum(attention_in_local * w_in.astype(jnp.float32), axis=1) / gain_attention
    gate_part = jnp.sum(gate_rows, axis=1) * mix * (1.0 - mix)
    gate_full = lax.dynamic_update_slice_in_dim(
        jnp.zeros(gate_logit.shape, jnp.float32), gate_part, head_first, 0
    )
    sums = sum_everywhere(jnp.concatenate([gain_attention_part, gain_feed_part, gate_full]))
    return (
        low(result),
        token_grad,
        sums[:width],
        attention_in_grad.astype(jnp.float32).reshape(attention_in.shape),
        sums[2 * width :],
        attention_out_grad.astype(jnp.float32),
        sums[width : 2 * width],
        feed_in_grad.astype(jnp.float32).reshape(feed_in.shape),
        feed_out_grad.astype(jnp.float32),
        memory_final[None],
        norm_final[None],
    )


def solution(mesh):
    in_specs = (
        P(("seq", "blk"), None),
        P(("seq", "blk"), None),
        P("seq", None),
        P("seq", "blk", None, None),
        P("seq", "blk", None),
        P(),
        P("seq", None, "blk"),
        P(),
        P("blk", "seq"),
        P(),
        P("seq", None, "blk"),
        P("blk", "seq"),
    )
    out_specs = (
        P(("seq", "blk"), None),
        P(("seq", "blk"), None),
        P(),
        P("seq", None, "blk"),
        P(),
        P("blk", "seq"),
        P(),
        P("seq", None, "blk"),
        P("blk", "seq"),
        P("seq", "blk", None, None),
        P("seq", "blk", None),
    )
    return jax.shard_map(
        per_device, mesh=mesh, in_specs=in_specs, out_specs=out_specs, check_vma=False
    )
```

time: 1730 us -> 910 us (0.53)
  waiting for transfers between devices: 1120 us -> 443 us
  local copies, waits for them, and re-layouts: 162 us -> 73.1 us
  matrix products: 321 us -> 235 us
  starting transfers between devices: 0.65 us -> 66.7 us
  blocking collectives: 43.1 us -> 0 us
  Pallas kernels: 0 us -> 34 us
    reduce_scatter x8 -> x5, waiting for transfers between devices: 555 us -> 46.3 us  [the longest x1 46.2 us: per_device(): lax.psum_scatter(sum_over_seq(dot_tn(merged_mine, out_grad), 1), 'blk', s...]
    all_gather x8 -> x5, waiting for transfers between devices: 561 us -> 51.8 us  [the longest x1 51.8 us: per_device(): w_out = whole(lax.all_gather(attention_out, 'blk', axis=0, tiled=True), 1)]
    ppermute x0 -> x53, waiting for transfers between devices: none -> 339 us  [the longest x24 192 us: back(): return lax.ppermute(values, 'blk', self.behind)]
    dynamic_update_slice x16 -> x0, local copies, waits for them, and re-layouts: 98.2 us -> none  [per_device(): attended_blocks, log_blocks = lax.map(forward_block, block_ids)]
    dot_general x56 -> x54, matrix products: 321 us -> 235 us  [the longest x25 107 us: dot_nt(): lax.dot_general(left, right, (((1,), (1,)), ((), ())), preferred_element_...]
    ppermute x0 -> x53, starting transfers between devices: none -> 57.7 us  [the longest x24 31.4 us: forth(): return lax.ppermute(values, 'blk', self.ahead)]
    psum x1 -> x0, blocking collectives: 43.1 us -> none  [per_device(): lax.psum((gain_attention_part, gain_feed_part, gate_full), ('seq', 'blk'))]
    unnamed x155 -> x235, local copies, waits for them, and re-layouts: 15.6 us -> 50.8 us
  transfers between devices with their start and end apart: 16 -> 65, of which waited for: 12 -> 30; matrix products, arithmetic and copies ran while one was open for 26% -> 34% of each run, Pallas kernels for 0% -> 4%
where the time goes in v1:
time: 910 us; the launch traced here: 905 us
  waiting for transfers between devices  443 us (49%)
  matrix products  235 us (26%)
  local copies, waits for them, and re-layouts  73.1 us (8%)
  starting transfers between devices  66.7 us (7%)
  other arithmetic  36.2 us (4%)
  Pallas kernels  34 us (4%)
  between operations  16.8 us (2%)
    ppermute x24, waiting for transfers between devices, back(): return lax.ppermute(values, 'blk', self.behind)  192 us
    ppermute x24, waiting for transfers between devices, forth(): return lax.ppermute(values, 'blk', self.ahead)  117 us
    dot_general x25, matrix products, dot_nt(): lax.dot_general(left, right, (((1,), (1,)), ((), ())), preferred_element_...  107 us
    dot_general x25, matrix products, dot_nn(): lax.dot_general(left, right, (((1,), (0,)), ((), ())), preferred_element_...  72.4 us
    dot_general x4, matrix products, dot_tn(): lax.dot_general(left, right, (((0,), (0,)), ((), ())), preferred_element_...  55.3 us
    all_gather x1, waiting for transfers between devices, per_device(): w_out = whole(lax.all_gather(attention_out, 'blk', axis=0, tiled=True), 1)  51.8 us
    unnamed x235, local copies, waits for them, and re-layouts  50.8 us
    reduce_scatter x1, waiting for transfers between devices, per_device(): lax.psum_scatter(sum_over_seq(dot_tn(merged_mine, out_grad), 1), 'blk', s...  46.2 us
  transfers between devices with their start and end apart: 65, of which 30 were waited for; matrix products, arithmetic and copies ran while one was open for 34% of the time, Pallas kernels for 4%

profile of v1, /device:TPU:0, one launch (start us, length us, event | category | flops | bytes accessed | tf_op | source)
XLA Modules:
  0.0 905.2 jit_solution(13410698900972176371)
XLA Ops:
  10.3 51.8 %all-gather.8.cloned.1.call-done = bf16[2048,512]{1,0:T(8,128)(2,1)} async-done(((bf16[256,512]{1,0:T(8,128)(2,1)}), bf16[2048,512]{1,0:T(8,128)(2,1)}) %all-gather.8.cloned.1.call-update) | async-done | bytes 2097168 | tf_op jit(solution)/shard_map/all_gather | solution.py:452
  69.6 21.8 %collective-permute-done.3 = bf16[256,2048]{1,0:T(8,128)(2,1)S(1)} collective-permute-done((bf16[256,2048]{1,0:T(8,128)(2,1)S(1)}, bf16[256,2048]{1,0:T(8,128)(2,1)S(1)}, u32[]{:S(2)}, u32[]{:S(2)}) %collective-permute-start.3) | collective-permute-done | bytes 1048608 | tf_op jit(solution)/shard_map/ppermute | solution.py:362
  95.4 22.1 %collective-permute-done.4 = bf16[256,2048]{1,0:T(8,128)(2,1)} collective-permute-done((bf16[256,2048]{1,0:T(8,128)(2,1)S(1)}, bf16[256,2048]{1,0:T(8,128)(2,1)}, u32[]{:S(2)}, u32[]{:S(2)}) %collective-permute-start.4) | collective-permute-done | bytes 1048608 | tf_op jit(solution)/shard_map/ppermute | solution.py:362
  121.7 20.1 %collective-permute-done.24 = bf16[256,2048]{1,0:T(8,128)(2,1)} collective-permute-done((bf16[256,2048]{1,0:T(8,128)(2,1)S(1)}, bf16[256,2048]{1,0:T(8,128)(2,1)}, u32[]{:S(2)}, u32[]{:S(2)}) %collective-permute-start.24) | collective-permute-done | bytes 1048608 | tf_op jit(solution)/shard_map/ppermute | solution.py:365
  143.8 18.6 %collective-permute-done.5 = bf16[256,2048]{1,0:T(8,128)(2,1)S(1)} collective-permute-done((bf16[256,2048]{1,0:T(8,128)(2,1)}, bf16[256,2048]{1,0:T(8,128)(2,1)S(1)}, u32[]{:S(2)}, u32[]{:S(2)}) %collective-permute-start.5) | collective-permute-done | bytes 1048608 | tf_op jit(solution)/shard_map/ppermute | solution.py:362
  174.5 18.6 %collective-permute-done.6 = bf16[128,2048]{1,0:T(8,128)(2,1)} collective-permute-done((bf16[128,2048]{1,0:T(8,128)(2,1)}, bf16[128,2048]{1,0:T(8,128)(2,1)}, u32[]{:S(2)}, u32[]{:S(2)}) %collective-permute-start.6) | collective-permute-done | bytes 524320 | tf_op jit(solution)/shard_map/ppermute | solution.py:362
  203.2 14.2 %shard_map.212 = (bf16[2048,256]{1,0:T(8,128)(2,1)S(1)}, f32[2048,256]{1,0:T(8,128)S(1)}, f32[4,2,512]{2,1,0:T(2,128)S(1)}, f32[2,2,128,128]{3,2,1,0:T(8,128)S(1...) custom-call(s32[8]{0:T(128)S(1)} %compare_select_fusion.order, s32[1]{0:T(128)} %bitcast.109.splits, ...), custom_call_target="tpu_custom_call" | custom-call | flops 4294967296 | bytes 6291456 | tf_op jit(solution)/shard_map/pallas_call | solution.py:300
  225.5 39.7 %collective-permute-done.26 = bf16[256,2048]{1,0:T(8,128)(2,1)S(1)} collective-permute-done((bf16[256,2048]{1,0:T(8,128)(2,1)}, bf16[256,2048]{1,0:T(8,128)(2,1)S(1)}, u32[]{:S(2)}, u32[]{:S(2)}) %collective-permute-start.26) | collective-permute-done | bytes 1048608 | tf_op jit(solution)/shard_map/ppermute | solution.py:365
  267.8 6.9 collective-permute-start.30
  274.8 6.2 multiply_reduce_fusion.3
  285.9 6.1 fusion.91
  294.7 5.7 multiply_convert_fusion.16
  301.6 10.0 %collective-permute-done.8 = bf16[256,2048]{1,0:T(8,128)(2,1)} collective-permute-done((bf16[256,2048]{1,0:T(8,128)(2,1)}, bf16[256,2048]{1,0:T(8,128)(2,1)}, u32[]{:S(2)}, u32[]{:S(2)}) %collective-permute-start.8) | collective-permute-done | bytes 1048608 | tf_op jit(solution)/shard_map/ppermute | solution.py:365
  328.5 6.1 fusion.48
  334.6 5.8 fusion.41
  342.1 6.3 fusion.95
  359.8 7.4 fusion.46
  370.7 5.8 fusion.39
  379.0 5.8 fusion.97
  386.1 5.8 fusion.102
  396.8 4.9 multiply_convert_fusion.2
  404.2 4.9 multiply_convert_fusion.8
  409.1 7.3 convolution_convert_fusion.6
  434.2 6.9 add_convert_fusion.11
  441.5 7.0 add_convert_fusion.8
  458.5 8.9 collective-permute-done.33
  468.5 6.2 collective-permute-done.37
  476.8 20.4 %collective-permute-done.21 = bf16[256,2048]{1,0:T(8,128)(2,1)S(1)} collective-permute-done((bf16[256,2048]{1,0:T(8,128)(2,1)S(1)}, bf16[256,2048]{1,0:T(8,128)(2,1)S(1)}, u32[]{:S(2)}, u32[]{:S(2)}) %collective-permute-start.21) | collective-permute-done | bytes 1048608 | tf_op jit(solution)/shard_map/ppermute | solution.py:365
  500.0 12.3 %collective-permute-done.34 = bf16[256,2048]{1,0:T(8,128)(2,1)S(1)} collective-permute-done((bf16[256,2048]{1,0:T(8,128)(2,1)S(1)}, bf16[256,2048]{1,0:T(8,128)(2,1)S(1)}, u32[]{:S(2)}, u32[]{:S(2)}) %collective-permute-start.34) | collective-permute-done | bytes 1048608 | tf_op jit(solution)/shard_map/ppermute | solution.py:362
  513.1 6.6 collective-permute-done.38
  521.8 20.4 %collective-permute-done.22 = bf16[256,2048]{1,0:T(8,128)(2,1)S(1)} collective-permute-done((bf16[256,2048]{1,0:T(8,128)(2,1)S(1)}, bf16[256,2048]{1,0:T(8,128)(2,1)S(1)}, u32[]{:S(2)}, u32[]{:S(2)}) %collective-permute-start.22) | collective-permute-done | bytes 1048608 | tf_op jit(solution)/shard_map/ppermute | solution.py:365
  545.0 12.3 %collective-permute-done.35 = bf16[256,2048]{1,0:T(8,128)(2,1)S(1)} collective-permute-done((bf16[256,2048]{1,0:T(8,128)(2,1)S(1)}, bf16[256,2048]{1,0:T(8,128)(2,1)S(1)}, u32[]{:S(2)}, u32[]{:S(2)}) %collective-permute-start.35) | collective-permute-done | bytes 1048608 | tf_op jit(solution)/shard_map/ppermute | solution.py:362
  557.3 7.4 collective-permute-done.39
  564.7 6.5 multiply_reduce_fusion.1
  571.2 9.6 %collective-permute-done.23 = bf16[256,2048]{1,0:T(8,128)(2,1)S(1)} collective-permute-done((bf16[256,2048]{1,0:T(8,128)(2,1)S(1)}, bf16[256,2048]{1,0:T(8,128)(2,1)S(1)}, u32[]{:S(2)}, u32[]{:S(2)}) %collective-permute-start.23) | collective-permute-done | bytes 1048608 | tf_op jit(solution)/shard_map/ppermute | solution.py:365
  584.9 7.0 convolution_convert_fusion.1
  601.8 11.0 %convolution_convert_fusion.2 = bf16[1024,2048]{1,0:T(8,128)(2,1)} fusion(bf16[2048,1024]{1,0:T(8,128)(2,1)S(1)} %copy-done.88, bf16[2048,2048]{1,0:T(8,128)(2,1)S(1)} %constant_dynamic-update-slice_fusion.26), kind=kOutput, calls=%fused_computation.3 | convolution fusion | flops 8592031744 | bytes 16777216 | tf_op jit(solution)/shard_map/dot_general | solution.py:28
  622.7 5.8 convolution_convert_fusion.5
  646.5 5.0 all-to-all-done.1
  651.5 19.9 %shard_map.213 = (bf16[2048,768]{1,0:T(8,128)(2,1)}, f32[2,128]{1,0:T(2,128)S(1)}) custom-call(s32[8]{0:T(128)S(1)} %copy-done.5, s32[1]{0:T(128)} %bitcast.110.splits, f32[2]{0:T(128)S(1)} %copy-done.3, bf16[2048,768]{1,0:T(8,128)(2,1)} %copy-done.100, bf16[2048,256]{1,0:T(8,128)(2,1)S(1)} %bitcast.111, f32[2048,256]{1,0:T(8,128)S(1)} %get-tuple-element.21.attended, ...), custom_call_target="tpu_custom_call" | custom-call | flops 10737418240 | bytes 10485760 | tf_op jit(solution)/shard_map/pallas_call | solution.py:323
  671.4 13.7 %fusion.86 = (bf16[2048,768]{0,1:T(8,128)(2,1)}, f32[2048]{0:T(1024)S(1)}) fusion(bf16[2048,768]{0,1:T(8,128)(2,1)S(1)} %copy-done.7, bf16[2048,2048]{1,0:T(8,128)(2,1)} %constant_dynamic-update-slice_fusion, bf16[2048,768]{1,0:T(8,128)(2,1)} %get-tuple-element.25), kind=kOutput, calls=%fused_computation.211 | convolution fusion | flops 6448740352 | bytes 17833984 | tf_op jit(solution)/shard_map/dot_general | solution.py:28
  699.0 23.8 %convolution_convert_fusion = bf16[2048,2048]{1,0:T(8,128)(2,1)} fusion(bf16[2048,2048]{1,0:T(8,128)(2,1)} %constant_dynamic-update-slice_fusion.9, bf16[2048,2048]{1,0:T(8,128)(2,1)} %fusion.40), kind=kOutput, calls=%fused_computation | convolution fusion | flops 17184063488 | bytes 25165824 | tf_op jit(solution)/shard_map/dot_general | solution.py:28
  728.1 12.5 %collective-permute-done.44 = bf16[128,2048]{1,0:T(8,128)(2,1)S(1)} collective-permute-done((bf16[128,2048]{1,0:T(8,128)(2,1)S(1)}, bf16[128,2048]{1,0:T(8,128)(2,1)S(1)}, u32[]{:S(2)}, u32[]{:S(2)}) %collective-permute-start.44) | collective-permute-done | bytes 524320 | tf_op jit(solution)/shard_map/ppermute | solution.py:365
  746.8 20.5 %collective-permute-done.45 = bf16[256,2048]{1,0:T(8,128)(2,1)S(1)} collective-permute-done((bf16[256,2048]{1,0:T(8,128)(2,1)S(1)}, bf16[256,2048]{1,0:T(8,128)(2,1)S(1)}, u32[]{:S(2)}, u32[]{:S(2)}) %collective-permute-start.45) | collective-permute-done | bytes 1048608 | tf_op jit(solution)/shard_map/ppermute | solution.py:365
  775.9 16.5 %collective-permute-done.46 = bf16[256,2048]{1,0:T(8,128)(2,1)S(1)} collective-permute-done((bf16[256,2048]{1,0:T(8,128)(2,1)S(1)}, bf16[256,2048]{1,0:T(8,128)(2,1)S(1)}, u32[]{:S(2)}, u32[]{:S(2)}) %collective-permute-start.46) | collective-permute-done | bytes 1048608 | tf_op jit(solution)/shard_map/ppermute | solution.py:365
  805.4 16.7 %collective-permute-done.50 = f32[4112]{0:T(1024)S(1)} collective-permute-done((f32[4112]{0:T(1024)S(1)}, f32[4112]{0:T(1024)S(1)}, u32[]{:S(2)}, u32[]{:S(2)}) %collective-permute-start.50) | collective-permute-done | bytes 16480 | tf_op jit(solution)/shard_map/ppermute | solution.py:404
  843.2 6.6 reshape.81
  849.8 46.2 %reduce-scatter.10.cloned.1.call-done = bf16[256,512]{1,0:T(8,128)(2,1)} async-done(((bf16[2048,512]{1,0:T(8,128)(2,1)}), bf16[256,512]{1,0:T(8,128)(2,1)}) %reduce-scatter.10.cloned.1.call-update) | async-done | bytes 262160 | tf_op jit(solution)/shard_map/reduce_scatter | solution.py:497
  (454 shorter events, 256.8 us)
Async XLA Ops:
  7.2 55.0 %all-gather.8.cloned.1.call-start = ((), (), s32[]{:S(2)}) async-start(), calls=%async_computation.8 | async-start | bytes 2359296 | tf_op jit(solution)/shard_map/all_gather | solution.py:452
  7.9 158.8 %all-gather.6.cloned.1.call-start = ((), (), s32[]{:S(2)}) async-start(), calls=%async_computation.7 | async-start | bytes 3932160 | tf_op jit(solution)/shard_map/all_gather | solution.py:449
  10.3 264.5 %all-gather.10.cloned.1.call-start = ((), (), s32[]{:S(2)}) async-start(), calls=%async_computation.9 | async-start | bytes 10485760 | tf_op jit(solution)/shard_map/all_gather | solution.py:449
  62.2 223.8 %all-gather.12.cloned.1.call-start = ((), (), s32[]{:S(2)}) async-start(), calls=%async_computation.10 | async-start | bytes 10485760 | tf_op jit(solution)/shard_map/all_gather | solution.py:449
  65.9 228.8 %all-gather.14.cloned.1.call-start = ((), (), s32[]{:S(2)}) async-start(), calls=%async_computation.11 | async-start | bytes 5242880 | tf_op jit(solution)/shard_map/all_gather | solution.py:449
  91.4 26.2 %collective-permute-start.4 = (bf16[256,2048]{1,0:T(8,128)(2,1)S(1)}, bf16[256,2048]{1,0:T(8,128)(2,1)}, u32[]{:S(2)}, u32[]{:S(2)}) collective-permute-start(bf16[256,2048]{1,0:T(8,128)(2,1)S(1)} %collective-permute-done.3), channel_id=1, source_target_pairs={{0,2},{2,4},{4,6},{6,7},{7,5},{5,3},{3,1},{1,0},{8,10},{10,12},{12... | collective-permute-start | bytes 3145736 | tf_op jit(solution)/shard_map/ppermute | solution.py:362
  93.1 26.2 %collective-permute-start.1 = (bf16[256,2048]{1,0:T(8,128)(2,1)S(1)}, bf16[256,2048]{1,0:T(8,128)(2,1)}, u32[]{:S(2)}, u32[]{:S(2)}) collective-permute-start(bf16[256,2048]{1,0:T(8,128)(2,1)S(1)} %collective-permute-done), channel_id=1, source_target_pairs={{2,0},{4,2},{6,4},{7,6},{5,7},{3,5},{1,3},{0,1},{10,8},{12,10},{14... | collective-permute-start | bytes 3145736 | tf_op jit(solution)/shard_map/ppermute | solution.py:365
  93.4 48.4 %collective-permute-start.24 = (bf16[256,2048]{1,0:T(8,128)(2,1)S(1)}, bf16[256,2048]{1,0:T(8,128)(2,1)}, u32[]{:S(2)}, u32[]{:S(2)}) collective-permute-start(bf16[256,2048]{1,0:T(8,128)(2,1)S(1)} %copy-done.18), channel_id=1, source_target_pairs={{2,0},{4,2},{6,4},{7,6},{5,7},{3,5},{1,3},{0,1},{10,8},{12,10},{14... | collective-permute-start | bytes 3145736 | tf_op jit(solution)/shard_map/ppermute | solution.py:365
  93.9 48.1 %collective-permute-start.27 = (bf16[256,2048]{1,0:T(8,128)(2,1)S(1)}, bf16[256,2048]{1,0:T(8,128)(2,1)}, u32[]{:S(2)}, u32[]{:S(2)}) collective-permute-start(bf16[256,2048]{1,0:T(8,128)(2,1)S(1)} %copy-done.18), channel_id=1, source_target_pairs={{0,2},{2,4},{4,6},{6,7},{7,5},{5,3},{3,1},{1,0},{8,10},{10,12},{12... | collective-permute-start | bytes 3145736 | tf_op jit(solution)/shard_map/ppermute | solution.py:362
  117.6 44.8 %collective-permute-start.5 = (bf16[256,2048]{1,0:T(8,128)(2,1)}, bf16[256,2048]{1,0:T(8,128)(2,1)S(1)}, u32[]{:S(2)}, u32[]{:S(2)}) collective-permute-start(bf16[256,2048]{1,0:T(8,128)(2,1)} %collective-permute-done.4), channel_id=1, source_target_pairs={{0,2},{2,4},{4,6},{6,7},{7,5},{5,3},{3,1},{1,0},{8,10},{10,12},{12... | collective-permute-start | bytes 3145736 | tf_op jit(solution)/shard_map/ppermute | solution.py:362
  119.3 45.7 %collective-permute-start.2 = (bf16[256,2048]{1,0:T(8,128)(2,1)}, bf16[256,2048]{1,0:T(8,128)(2,1)S(1)}, u32[]{:S(2)}, u32[]{:S(2)}) collective-permute-start(bf16[256,2048]{1,0:T(8,128)(2,1)} %collective-permute-done.1), channel_id=1, source_target_pairs={{2,0},{4,2},{6,4},{7,6},{5,7},{3,5},{1,3},{0,1},{10,8},{12,10},{14... | collective-permute-start | bytes 3145736 | tf_op jit(solution)/shard_map/ppermute | solution.py:365
  141.8 81.4 %collective-permute-start.25 = (bf16[256,2048]{1,0:T(8,128)(2,1)}, bf16[256,2048]{1,0:T(8,128)(2,1)}, u32[]{:S(2)}, u32[]{:S(2)}) collective-permute-start(bf16[256,2048]{1,0:T(8,128)(2,1)} %collective-permute-done.24), channel_id=1, source_target_pairs={{2,0},{4,2},{6,4},{7,6},{5,7},{3,5},{1,3},{0,1},{10,8},{12,10},{14... | collective-permute-start | bytes 3145736 | tf_op jit(solution)/shard_map/ppermute | solution.py:365
  142.1 83.2 %collective-permute-start.28 = (bf16[256,2048]{1,0:T(8,128)(2,1)}, bf16[256,2048]{1,0:T(8,128)(2,1)}, u32[]{:S(2)}, u32[]{:S(2)}) collective-permute-start(bf16[256,2048]{1,0:T(8,128)(2,1)} %collective-permute-done.27), channel_id=1, source_target_pairs={{0,2},{2,4},{4,6},{6,7},{7,5},{5,3},{3,1},{1,0},{8,10},{10,12},{12... | collective-permute-start | bytes 3145736 | tf_op jit(solution)/shard_map/ppermute | solution.py:362
  163.3 29.8 %collective-permute-start.6 = (bf16[128,2048]{1,0:T(8,128)(2,1)}, bf16[128,2048]{1,0:T(8,128)(2,1)}, u32[]{:S(2)}, u32[]{:S(2)}) collective-permute-start(bf16[128,2048]{1,0:T(8,128)(2,1)} %slice.156), channel_id=1, source_target_pairs={{0,2},{2,4},{4,6},{6,7},{7,5},{5,3},{3,1},{1,0},{8,10},{10,12},{12... | collective-permute-start | bytes 1572872 | tf_op jit(solution)/shard_map/ppermute | solution.py:362
  165.9 28.9 %collective-permute-start.7 = (bf16[128,2048]{1,0:T(8,128)(2,1)}, bf16[128,2048]{1,0:T(8,128)(2,1)}, u32[]{:S(2)}, u32[]{:S(2)}) collective-permute-start(bf16[128,2048]{1,0:T(8,128)(2,1)} %slice.157), channel_id=1, source_target_pairs={{2,0},{4,2},{6,4},{7,6},{5,7},{3,5},{1,3},{0,1},{10,8},{12,10},{14... | collective-permute-start | bytes 1572872 | tf_op jit(solution)/shard_map/ppermute | solution.py:365
  218.7 56.1 %all-to-all-start = ((bf16[8,256,256]{1,2,0:T(8,128)(2,1)}), bf16[8,256,256]{1,2,0:T(8,128)(2,1)}, u32[]{:S(2)}, u32[]{:S(2)}) async-start(bf16[8,256,256]{1,2,0:T(8,128)(2,1)} %copy.28), calls=%async_computation | async-start | bytes 2097152 | tf_op jit(solution)/shard_map/all_to_all | solution.py:464
  223.1 547.6 %reduce-scatter.8.cloned.1.call-start = ((), (), s32[]{:S(2)}) async-start(), calls=%async_computation.13 | async-start | bytes 10485760 | tf_op jit(solution)/shard_map/reduce_scatter | solution.py:423
  223.2 41.9 %collective-permute-start.26 = (bf16[256,2048]{1,0:T(8,128)(2,1)}, bf16[256,2048]{1,0:T(8,128)(2,1)S(1)}, u32[]{:S(2)}, u32[]{:S(2)}) collective-permute-start(bf16[256,2048]{1,0:T(8,128)(2,1)} %collective-permute-done.25), channel_id=1, source_target_pairs={{2,0},{4,2},{6,4},{7,6},{5,7},{3,5},{1,3},{0,1},{10,8},{12,10},{14... | collective-permute-start | bytes 3145736 | tf_op jit(solution)/shard_map/ppermute | solution.py:365
  225.3 40.8 %collective-permute-start.29 = (bf16[256,2048]{1,0:T(8,128)(2,1)}, bf16[256,2048]{1,0:T(8,128)(2,1)S(1)}, u32[]{:S(2)}, u32[]{:S(2)}) collective-permute-start(bf16[256,2048]{1,0:T(8,128)(2,1)} %collective-permute-done.28), channel_id=1, source_target_pairs={{0,2},{2,4},{4,6},{6,7},{7,5},{5,3},{3,1},{1,0},{8,10},{10,12},{12... | collective-permute-start | bytes 3145736 | tf_op jit(solution)/shard_map/ppermute | solution.py:362
  266.0 138.2 %collective-permute-start.31 = (bf16[128,2048]{1,0:T(8,128)(2,1)}, bf16[128,2048]{1,0:T(8,128)(2,1)}, u32[]{:S(2)}, u32[]{:S(2)}) collective-permute-start(bf16[128,2048]{1,0:T(8,128)(2,1)} %slice.179), channel_id=1, source_target_pairs={{2,0},{4,2},{6,4},{7,6},{5,7},{3,5},{1,3},{0,1},{10,8},{12,10},{14... | collective-permute-start | bytes 1572872 | tf_op jit(solution)/shard_map/ppermute | solution.py:365
  267.8 136.3 %collective-permute-start.30 = (bf16[128,2048]{1,0:T(8,128)(2,1)}, bf16[128,2048]{1,0:T(8,128)(2,1)}, u32[]{:S(2)}, u32[]{:S(2)}) collective-permute-start(bf16[128,2048]{1,0:T(8,128)(2,1)} %slice.178), channel_id=1, source_target_pairs={{0,2},{2,4},{4,6},{6,7},{7,5},{5,3},{3,1},{1,0},{8,10},{10,12},{12... | collective-permute-start | bytes 1572872 | tf_op jit(solution)/shard_map/ppermute | solution.py:362
  283.9 32.8 %collective-permute-start.11 = (bf16[256,2048]{1,0:T(8,128)(2,1)}, bf16[256,2048]{1,0:T(8,128)(2,1)}, u32[]{:S(2)}, u32[]{:S(2)}) collective-permute-start(bf16[256,2048]{1,0:T(8,128)(2,1)} %get-tuple-element.70), channel_id=1, source_target_pairs={{0,2},{2,4},{4,6},{6,7},{7,5},{5,3},{3,1},{1,0},{8,10},{10,12},{12... | collective-permute-start | bytes 3145736 | tf_op jit(solution)/shard_map/ppermute | solution.py:362
  285.9 25.7 %collective-permute-start.8 = (bf16[256,2048]{1,0:T(8,128)(2,1)}, bf16[256,2048]{1,0:T(8,128)(2,1)}, u32[]{:S(2)}, u32[]{:S(2)}) collective-permute-start(bf16[256,2048]{1,0:T(8,128)(2,1)} %get-tuple-element.70), channel_id=1, source_target_pairs={{2,0},{4,2},{6,4},{7,6},{5,7},{3,5},{1,3},{0,1},{10,8},{12,10},{14... | collective-permute-start | bytes 3145736 | tf_op jit(solution)/shard_map/ppermute | solution.py:365
  311.7 30.1 %collective-permute-start.9 = (bf16[256,2048]{1,0:T(8,128)(2,1)}, bf16[256,2048]{1,0:T(8,128)(2,1)S(1)}, u32[]{:S(2)}, u32[]{:S(2)}) collective-permute-start(bf16[256,2048]{1,0:T(8,128)(2,1)} %collective-permute-done.8), channel_id=1, source_target_pairs={{2,0},{4,2},{6,4},{7,6},{5,7},{3,5},{1,3},{0,1},{10,8},{12,10},{14... | collective-permute-start | bytes 3145736 | tf_op jit(solution)/shard_map/ppermute | solution.py:365
  316.7 32.8 %collective-permute-start.12 = (bf16[256,2048]{1,0:T(8,128)(2,1)}, bf16[256,2048]{1,0:T(8,128)(2,1)S(1)}, u32[]{:S(2)}, u32[]{:S(2)}) collective-permute-start(bf16[256,2048]{1,0:T(8,128)(2,1)} %collective-permute-done.11), channel_id=1, source_target_pairs={{0,2},{2,4},{4,6},{6,7},{7,5},{5,3},{3,1},{1,0},{8,10},{10,12},{12... | collective-permute-start | bytes 3145736 | tf_op jit(solution)/shard_map/ppermute | solution.py:362
  341.8 35.3 %collective-permute-start.10 = (bf16[256,2048]{1,0:T(8,128)(2,1)S(1)}, bf16[256,2048]{1,0:T(8,128)(2,1)S(1)}, u32[]{:S(2)}, u32[]{:S(2)}) collective-permute-start(bf16[256,2048]{1,0:T(8,128)(2,1)S(1)} %collective-permute-done.9), channel_id=1, source_target_pairs={{2,0},{4,2},{6,4},{7,6},{5,7},{3,5},{1,3},{0,1},{10,8},{12,10},{14... | collective-permute-start | bytes 3145736 | tf_op jit(solution)/shard_map/ppermute | solution.py:365
  349.6 27.0 %collective-permute-start.13 = (bf16[256,2048]{1,0:T(8,128)(2,1)S(1)}, bf16[256,2048]{1,0:T(8,128)(2,1)S(1)}, u32[]{:S(2)}, u32[]{:S(2)}) collective-permute-start(bf16[256,2048]{1,0:T(8,128)(2,1)S(1)} %collective-permute-done.12), channel_id=1, source_target_pairs={{0,2},{2,4},{4,6},{6,7},{7,5},{5,3},{3,1},{1,0},{8,10},{10,12},{12... | collective-permute-start | bytes 3145736 | tf_op jit(solution)/shard_map/ppermute | solution.py:362
  426.7 28.0 %collective-permute-start.16 = (bf16[128,2048]{1,0:T(8,128)(2,1)S(1)}, bf16[128,2048]{1,0:T(8,128)(2,1)}, u32[]{:S(2)}, u32[]{:S(2)}) collective-permute-start(bf16[128,2048]{1,0:T(8,128)(2,1)S(1)} %get-tuple-element.97), channel_id=1, source_target_pairs={{0,2},{2,4},{4,6},{6,7},{7,5},{5,3},{3,1},{1,0},{8,10},{10,12},{12... | collective-permute-start | bytes 1572872 | tf_op jit(solution)/shard_map/ppermute | solution.py:362
  441.1 26.3 %collective-permute-start.33 = (bf16[256,2048]{1,0:T(8,128)(2,1)}, bf16[256,2048]{1,0:T(8,128)(2,1)S(1)}, u32[]{:S(2)}, u32[]{:S(2)}) collective-permute-start(bf16[256,2048]{1,0:T(8,128)(2,1)} %add_convert_fusion.11), channel_id=1, source_target_pairs={{0,2},{2,4},{4,6},{6,7},{7,5},{5,3},{3,1},{1,0},{8,10},{10,12},{12... | collective-permute-start | bytes 3145736 | tf_op jit(solution)/shard_map/ppermute | solution.py:362
  448.5 26.3 %collective-permute-start.37 = (bf16[256,2048]{1,0:T(8,128)(2,1)}, bf16[256,2048]{1,0:T(8,128)(2,1)S(1)}, u32[]{:S(2)}, u32[]{:S(2)}) collective-permute-start(bf16[256,2048]{1,0:T(8,128)(2,1)} %add_convert_fusion.8), channel_id=1, source_target_pairs={{2,0},{4,2},{6,4},{7,6},{5,7},{3,5},{1,3},{0,1},{10,8},{12,10},{14... | collective-permute-start | bytes 3145736 | tf_op jit(solution)/shard_map/ppermute | solution.py:365
  453.9 43.4 %collective-permute-start.21 = (bf16[256,2048]{1,0:T(8,128)(2,1)S(1)}, bf16[256,2048]{1,0:T(8,128)(2,1)S(1)}, u32[]{:S(2)}, u32[]{:S(2)}) collective-permute-start(bf16[256,2048]{1,0:T(8,128)(2,1)S(1)} %add_convert_fusion.15), channel_id=1, source_target_pairs={{2,0},{4,2},{6,4},{7,6},{5,7},{3,5},{1,3},{0,1},{10,8},{12,10},{14... | collective-permute-start | bytes 3145736 | tf_op jit(solution)/shard_map/ppermute | solution.py:365
  457.2 42.1 %collective-permute-start.17 = (bf16[256,2048]{1,0:T(8,128)(2,1)S(1)}, bf16[256,2048]{1,0:T(8,128)(2,1)S(1)}, u32[]{:S(2)}, u32[]{:S(2)}) collective-permute-start(bf16[256,2048]{1,0:T(8,128)(2,1)S(1)} %add_convert_fusion.18), channel_id=1, source_target_pairs={{0,2},{2,4},{4,6},{6,7},{7,5},{5,3},{3,1},{1,0},{8,10},{10,12},{12... | collective-permute-start | bytes 3145736 | tf_op jit(solution)/shard_map/ppermute | solution.py:362
  467.7 44.6 %collective-permute-start.34 = (bf16[256,2048]{1,0:T(8,128)(2,1)S(1)}, bf16[256,2048]{1,0:T(8,128)(2,1)S(1)}, u32[]{:S(2)}, u32[]{:S(2)}) collective-permute-start(bf16[256,2048]{1,0:T(8,128)(2,1)S(1)} %add_convert_fusion.10), channel_id=1, source_target_pairs={{0,2},{2,4},{4,6},{6,7},{7,5},{5,3},{3,1},{1,0},{8,10},{10,12},{12... | collective-permute-start | bytes 3145736 | tf_op jit(solution)/shard_map/ppermute | solution.py:362
  475.1 44.6 %collective-permute-start.38 = (bf16[256,2048]{1,0:T(8,128)(2,1)S(1)}, bf16[256,2048]{1,0:T(8,128)(2,1)S(1)}, u32[]{:S(2)}, u32[]{:S(2)}) collective-permute-start(bf16[256,2048]{1,0:T(8,128)(2,1)S(1)} %add_convert_fusion.7), channel_id=1, source_target_pairs={{2,0},{4,2},{6,4},{7,6},{5,7},{3,5},{1,3},{0,1},{10,8},{12,10},{14... | collective-permute-start | bytes 3145736 | tf_op jit(solution)/shard_map/ppermute | solution.py:365
  497.6 44.6 %collective-permute-start.22 = (bf16[256,2048]{1,0:T(8,128)(2,1)S(1)}, bf16[256,2048]{1,0:T(8,128)(2,1)S(1)}, u32[]{:S(2)}, u32[]{:S(2)}) collective-permute-start(bf16[256,2048]{1,0:T(8,128)(2,1)S(1)} %add_convert_fusion.14), channel_id=1, source_target_pairs={{2,0},{4,2},{6,4},{7,6},{5,7},{3,5},{1,3},{0,1},{10,8},{12,10},{14... | collective-permute-start | bytes 3145736 | tf_op jit(solution)/shard_map/ppermute | solution.py:365
  499.6 44.6 %collective-permute-start.18 = (bf16[256,2048]{1,0:T(8,128)(2,1)S(1)}, bf16[256,2048]{1,0:T(8,128)(2,1)S(1)}, u32[]{:S(2)}, u32[]{:S(2)}) collective-permute-start(bf16[256,2048]{1,0:T(8,128)(2,1)S(1)} %add_convert_fusion.17), channel_id=1, source_target_pairs={{0,2},{2,4},{4,6},{6,7},{7,5},{5,3},{3,1},{1,0},{8,10},{10,12},{12... | collective-permute-start | bytes 3145736 | tf_op jit(solution)/shard_map/ppermute | solution.py:362
  512.7 44.6 %collective-permute-start.35 = (bf16[256,2048]{1,0:T(8,128)(2,1)S(1)}, bf16[256,2048]{1,0:T(8,128)(2,1)S(1)}, u32[]{:S(2)}, u32[]{:S(2)}) collective-permute-start(bf16[256,2048]{1,0:T(8,128)(2,1)S(1)} %add_convert_fusion.9), channel_id=1, source_target_pairs={{0,2},{2,4},{4,6},{6,7},{7,5},{5,3},{3,1},{1,0},{8,10},{10,12},{12... | collective-permute-start | bytes 3145736 | tf_op jit(solution)/shard_map/ppermute | solution.py:362
  520.0 44.6 %collective-permute-start.39 = (bf16[256,2048]{1,0:T(8,128)(2,1)S(1)}, bf16[256,2048]{1,0:T(8,128)(2,1)S(1)}, u32[]{:S(2)}, u32[]{:S(2)}) collective-permute-start(bf16[256,2048]{1,0:T(8,128)(2,1)S(1)} %add_convert_fusion.6), channel_id=1, source_target_pairs={{2,0},{4,2},{6,4},{7,6},{5,7},{3,5},{1,3},{0,1},{10,8},{12,10},{14... | collective-permute-start | bytes 3145736 | tf_op jit(solution)/shard_map/ppermute | solution.py:365
  542.5 38.3 %collective-permute-start.23 = (bf16[256,2048]{1,0:T(8,128)(2,1)S(1)}, bf16[256,2048]{1,0:T(8,128)(2,1)S(1)}, u32[]{:S(2)}, u32[]{:S(2)}) collective-permute-start(bf16[256,2048]{1,0:T(8,128)(2,1)S(1)} %add_convert_fusion.13), channel_id=1, source_target_pairs={{2,0},{4,2},{6,4},{7,6},{5,7},{3,5},{1,3},{0,1},{10,8},{12,10},{14... | collective-permute-start | bytes 3145736 | tf_op jit(solution)/shard_map/ppermute | solution.py:365
  544.6 36.3 %collective-permute-start.19 = (bf16[256,2048]{1,0:T(8,128)(2,1)S(1)}, bf16[256,2048]{1,0:T(8,128)(2,1)S(1)}, u32[]{:S(2)}, u32[]{:S(2)}) collective-permute-start(bf16[256,2048]{1,0:T(8,128)(2,1)S(1)} %add_convert_fusion.16), channel_id=1, source_target_pairs={{0,2},{2,4},{4,6},{6,7},{7,5},{5,3},{3,1},{1,0},{8,10},{10,12},{12... | collective-permute-start | bytes 3145736 | tf_op jit(solution)/shard_map/ppermute | solution.py:362
  591.9 239.8 %reduce-scatter.14.cloned.1.call-start = ((), (), s32[]{:S(2)}) async-start(), calls=%async_computation.16 | async-start | bytes 5242880 | tf_op jit(solution)/shard_map/reduce_scatter | solution.py:423
  633.0 207.6 %reduce-scatter.6.cloned.1.call-start = ((), (), s32[]{:S(2)}) async-start(), calls=%async_computation.12 | async-start | bytes 3932160 | tf_op jit(solution)/shard_map/reduce_scatter | solution.py:423
  685.1 158.2 %reduce-scatter.12.cloned.1.call-start = ((), (), s32[]{:S(2)}) async-start(), calls=%async_computation.15 | async-start | bytes 10485760 | tf_op jit(solution)/shard_map/reduce_scatter | solution.py:423
  722.7 173.3 %reduce-scatter.10.cloned.1.call-start = ((), (), s32[]{:S(2)}) async-start(), calls=%async_computation.14 | async-start | bytes 2359296 | tf_op jit(solution)/shard_map/reduce_scatter | solution.py:497
  741.7 25.6 %collective-permute-start.45 = (bf16[256,2048]{1,0:T(8,128)(2,1)S(1)}, bf16[256,2048]{1,0:T(8,128)(2,1)S(1)}, u32[]{:S(2)}, u32[]{:S(2)}) collective-permute-start(bf16[256,2048]{1,0:T(8,128)(2,1)S(1)} %add_convert_fusion.2), channel_id=1, source_target_pairs={{2,0},{4,2},{6,4},{7,6},{5,7},{3,5},{1,3},{0,1},{10,8},{12,10},{14... | collective-permute-start | bytes 3145736 | tf_op jit(solution)/shard_map/ppermute | solution.py:365
  769.5 25.6 %collective-permute-start.42 = (bf16[256,2048]{1,0:T(8,128)(2,1)S(1)}, bf16[256,2048]{1,0:T(8,128)(2,1)}, u32[]{:S(2)}, u32[]{:S(2)}) collective-permute-start(bf16[256,2048]{1,0:T(8,128)(2,1)S(1)} %add_convert_fusion.4), channel_id=1, source_target_pairs={{0,2},{2,4},{4,6},{6,7},{7,5},{5,3},{3,1},{1,0},{8,10},{10,12},{12... | collective-permute-start | bytes 3145736 | tf_op jit(solution)/shard_map/ppermute | solution.py:362
  793.7 40.8 %collective-permute-start.47 = (bf16[256,2048]{1,0:T(8,128)(2,1)}, bf16[256,2048]{1,0:T(8,128)(2,1)S(1)}, u32[]{:S(2)}, u32[]{:S(2)}) collective-permute-start(bf16[256,2048]{1,0:T(8,128)(2,1)} %add_convert_fusion), channel_id=1, source_target_pairs={{2,0},{4,2},{6,4},{7,6},{5,7},{3,5},{1,3},{0,1},{10,8},{12,10},{14... | collective-permute-start | bytes 3145736 | tf_op jit(solution)/shard_map/ppermute | solution.py:365
  797.6 36.9 %collective-permute-start.43 = (bf16[256,2048]{1,0:T(8,128)(2,1)}, bf16[256,2048]{1,0:T(8,128)(2,1)S(1)}, u32[]{:S(2)}, u32[]{:S(2)}) collective-permute-start(bf16[256,2048]{1,0:T(8,128)(2,1)} %add_convert_fusion.3), channel_id=1, source_target_pairs={{0,2},{2,4},{4,6},{6,7},{7,5},{5,3},{3,1},{1,0},{8,10},{10,12},{12... | collective-permute-start | bytes 3145736 | tf_op jit(solution)/shard_map/ppermute | solution.py:362
  (122 other events, 1466.1 us)
Sparse Core Ops, SparseCore 0:
  10.1 51.9 all-gather.7
  64.3 27.0 all-gather.5
  92.9 58.2 all-gather.9
  153.2 58.2 all-gather.11
  213.0 34.4 all-gather.13
  592.0 69.3 reduce-scatter.7
  664.6 44.5 reduce-scatter.13
  711.7 37.9 reduce-scatter.5
  752.5 72.1 reduce-scatter.11
  828.1 67.9 reduce-scatter.9

commit v2 on v1

--- a/solution.py
+++ b/solution.py
@@ -10,10 +10,11 @@
 
 SHORT = 1024
 TILE = 512
+FEED_TILE = 256
 EPSILON = 1e-06
 MASKED = -1e30
 LOG2E = math.log2(math.e)
-VMEM_LIMIT = 48 * 1024 * 1024
+VMEM_LIMIT = 60 * 1024 * 1024
 
 
 def dot_nn(left, right):
@@ -304,9 +305,7 @@
         out_specs=[VMEM] * len(shapes),
         scratch_shapes=[whole, whole, whole, pltpu.VMEM((width, length), jnp.bfloat16)],
         compiler_params=pltpu.CompilerParams(vmem_limit_bytes=VMEM_LIMIT),
-        cost_estimate=pl.CostEstimate(
-            flops=4 * length * length * width, bytes_accessed=12 * length * width, transcendentals=0
-        ),
+        cost_estimate=NO_COST,
     )(order, splits, mix, proj, memory, norm)
 
 
@@ -330,10 +329,134 @@
             pltpu.VMEM((tiles, heads, TILE), jnp.float32), wide, wide, wide,
         ],
         compiler_params=pltpu.CompilerParams(vmem_limit_bytes=VMEM_LIMIT),
-        cost_estimate=pl.CostEstimate(
-            flops=10 * length * length * width, bytes_accessed=20 * length * width, transcendentals=0
-        ),
+        cost_estimate=NO_COST,
     )(order, splits, mix, proj, combined_grad, attended, lse, states, norms)
+
+
+def fill(whole, pieces):
+    rows = pieces[0].shape[0]
+    for place, piece in enumerate(pieces):
+        whole[place * rows : (place + 1) * rows, :] = piece[...]
+
+
+def project_kernel(*refs, count):
+    pieces, weight = refs[:count], refs[count]
+    normed_all, proj_all = refs[-2:]
+    rows, width = pieces[0].shape[0], normed_all.shape[1]
+
+    @pl.when(pl.program_id(0) == 0)
+    def _():
+        for place, piece in enumerate(pieces):
+            normed_all[place * rows : (place + 1) * rows, :] = piece[:, :width]
+
+    proj_all[...] = low(dot_nn(normed_all[...], weight[...]))
+
+
+def feed_kernel(*refs, count):
+    normed, cots = refs[:count], refs[count : 2 * count]
+    w_gate, w_up, w_down = refs[2 * count : 2 * count + 3]
+    result_s, grad_s = refs[-2:]
+    results, grads = refs[-2 - 2 * count : -2 - count], refs[-2 - count : -2]
+    normed_all, cot_all, hidden, gate_grad, up_grad = refs[-7 - 2 * count : -2 - 2 * count]
+    step = pl.program_id(0)
+
+    @pl.when(step == 0)
+    def _():
+        fill(normed_all, normed)
+        fill(cot_all, cots)
+
+    gate = dot_nn(normed_all[...], w_gate[...])
+    up = dot_nn(normed_all[...], w_up[...])
+    hidden_grad = dot_nt(cot_all[...], w_down[...])
+    sigmoid_gate = 1.0 / (1.0 + jnp.exp(-gate))
+    activated = gate * sigmoid_gate
+    low_hidden = low(activated * up)
+    low_gate = low(hidden_grad * up * (sigmoid_gate + activated * (1.0 - sigmoid_gate)))
+    low_up = low(hidden_grad * activated)
+    hidden[...] = low_hidden
+    gate_grad[...] = low_gate
+    up_grad[...] = low_up
+    more_result = dot_nn(low_hidden, w_down[...])
+    more_grad = dot_nt(low_gate, w_gate[...]) + dot_nt(low_up, w_up[...])
+
+    @pl.when(step == 0)
+    def _():
+        result_s[...] = more_result
+        grad_s[...] = more_grad
+
+    @pl.when(step > 0)
+    def _():
+        result_s[...] += more_result
+        grad_s[...] += more_grad
+
+    @pl.when(step == pl.num_programs(0) - 1)
+    def _():
+        rows = results[0].shape[0]
+        for place in range(count):
+            here = slice(place * rows, (place + 1) * rows)
+            results[place][...] = low(result_s[here, :])
+            grads[place][...] = low(grad_s[here, :])
+
+
+NO_COST = pl.CostEstimate(flops=4_000_000_000, bytes_accessed=4096, transcendentals=0)
+ANY = pl.BlockSpec(memory_space=pl.ANY)
+
+
+def project_blocks(pieces, weight, place, length, before):
+    rows, both = pieces[0].shape
+    width, wide = weight.shape
+    count = len(pieces)
+    tall = rows * count
+    tile = 256 if wide % 256 == 0 else 128
+    return pl.pallas_call(
+        functools.partial(project_kernel, count=count),
+        grid=(wide // tile,),
+        out_shape=[
+            jax.ShapeDtypeStruct((length, width), jnp.bfloat16),
+            jax.ShapeDtypeStruct((length, wide), jnp.bfloat16),
+        ],
+        in_specs=[pl.BlockSpec((rows, both), lambda j: (0, 0))] * count
+        + [pl.BlockSpec((width, tile), lambda j: (0, j))]
+        + [ANY] * len(before),
+        out_specs=[
+            pl.BlockSpec((tall, width), lambda j: (place, 0)),
+            pl.BlockSpec((tall, tile), lambda j: (place, j)),
+        ],
+        input_output_aliases={count + 1 + i: i for i in range(len(before))},
+        compiler_params=pltpu.CompilerParams(vmem_limit_bytes=VMEM_LIMIT),
+        cost_estimate=NO_COST,
+    )(*pieces, weight, *before)
+
+
+def feed_blocks(normed, cots, f_in, f_out, place, length, before):
+    count = len(normed)
+    rows, width = normed[0].shape
+    tall, wide = count * rows, f_out.shape[0]
+    tile = min(FEED_TILE, wide)
+    tiles = wide // tile
+    piece = pl.BlockSpec((rows, width), lambda j: (0, 0))
+    kept = pl.BlockSpec((tall, width), lambda j: (place, 0))
+    part = pl.BlockSpec((tall, tile), lambda j: (place, j))
+    outs = pl.pallas_call(
+        functools.partial(feed_kernel, count=count),
+        grid=(tiles,),
+        out_shape=[jax.ShapeDtypeStruct((length, width), jnp.bfloat16)] * 2
+        + [jax.ShapeDtypeStruct((length, wide), jnp.bfloat16)] * 3
+        + [jax.ShapeDtypeStruct((rows, width), jnp.bfloat16)] * (2 * count),
+        in_specs=[piece] * (2 * count)
+        + [
+            pl.BlockSpec((width, tile), lambda j: (0, j)),
+            pl.BlockSpec((width, tile), lambda j: (0, j + tiles)),
+            pl.BlockSpec((tile, width), lambda j: (j, 0)),
+        ]
+        + [ANY] * len(before),
+        out_specs=[kept] * 2 + [part] * 3 + [piece] * (2 * count),
+        scratch_shapes=[pltpu.VMEM((tall, width), jnp.float32)] * 2,
+        input_output_aliases={2 * count + 3 + i: i for i in range(len(before))},
+        compiler_params=pltpu.CompilerParams(vmem_limit_bytes=VMEM_LIMIT),
+        cost_estimate=NO_COST,
+    )(*normed, *cots, f_in, f_in, f_out, *before)
+    return outs[:5], outs[5 : 5 + count], outs[5 + count :]
 
 
 def ring_of(count):
@@ -356,7 +479,14 @@
         for place, index in enumerate(ring):
             places[index] = place
         places = jnp.array(places, jnp.int32)
-        self.order = lax.rem(places - places[lax.axis_index("blk")] + count, count)
+        self.slots = [0] * count
+        self.slots[count // 2] = 1
+        for step in range(1, count // 2):
+            self.slots[count - step], self.slots[step] = 2 * step, 2 * step + 1
+        here = places[lax.axis_index("blk")]
+        self.order = jnp.array(self.slots, jnp.int32)[lax.rem(places - here + count, count)]
+        around = lax.rem(jnp.arange(count, dtype=jnp.int32) + here, count)
+        self.ahead_index = jnp.array(ring, jnp.int32)[around]
 
     def forth(self, values):
         return lax.ppermute(values, "blk", self.ahead)
@@ -364,46 +494,93 @@
     def back(self, values):
         return lax.ppermute(values, "blk", self.behind)
 
-    def gather(self, block):
-        half = self.count // 2
-        middle = block.shape[0] // 2
-        blocks = {0: block}
-        arrival = [0]
-        from_behind = from_ahead = block
-        for step in range(1, half):
-            from_behind = self.forth(from_behind)
-            from_ahead = self.back(from_ahead)
-            blocks[self.count - step] = from_behind
-            blocks[step] = from_ahead
-            arrival += [self.count - step, step]
-        blocks[half] = jnp.concatenate([self.forth(from_behind[:middle]), self.back(from_ahead[middle:])])
-        arrival.append(half)
-        return blocks, arrival
-
-    def scatter(self, partial):
-        half = self.count // 2
-        far = low(partial(half))
-        middle = far.shape[0] // 2
-        forward = self.forth(far[:middle])
-        backward = self.back(far[middle:])
-        for step in range(half - 1, 0, -1):
-            forward, backward = forward.astype(jnp.float32), backward.astype(jnp.float32)
-            if step == half - 1:
-                forward = jnp.pad(forward, ((0, middle), (0, 0)))
-                backward = jnp.pad(backward, ((middle, 0), (0, 0)))
-            forward = self.forth(low(partial(step) + forward))
-            backward = self.back(low(partial(self.count - step) + backward))
-        return partial(0) + forward.astype(jnp.float32) + backward.astype(jnp.float32)
-
-
-def sum_everywhere(values):
-    for axis in ("seq", "blk"):
-        size = lax.axis_size(axis)
-        step = 1
-        while step < size:
-            values = values + lax.ppermute(values, axis, [(i, i ^ step) for i in range(size)])
-            step *= 2
-    return values
+
+class Gather:
+    def __init__(self, ring, block):
+        self.ring = ring
+        self.groups = [(block,)]
+
+    def hop(self, *earlier):
+        ring, half = self.ring, self.ring.count // 2
+        last = self.groups[-1]
+        behind, ahead = after((last[0], last[-1]), *earlier)
+        if len(self.groups) == half:
+            middle = behind.shape[0] // 2
+            behind, ahead = behind[:middle], ahead[middle:]
+        self.groups.append((ring.forth(behind), ring.back(ahead)))
+        return self.groups[-1]
+
+    def place(self, step):
+        return {0: 0, self.ring.count // 2: 1}.get(step, step)
+
+
+class Scatter:
+    def __init__(self, ring, partial, axis=0):
+        self.ring = ring
+        self.partial = partial
+        self.axis = axis
+        self.step = ring.count // 2
+        self.sent = self.moved = self.rider = self.parts = None
+
+    def messages(self, *earlier):
+        half, step = self.ring.count // 2, self.step
+        self.step -= 1
+        if step == half:
+            return after(tuple(self.partial(half)), *earlier)
+        forward, backward = (part.astype(jnp.float32) for part in after(self.moved, *earlier))
+        if step == half - 1:
+            extra = forward.shape[self.axis]
+            forward = jnp.pad(forward, [(0, extra if axis == self.axis else 0) for axis in (0, 1)])
+            backward = jnp.pad(backward, [(extra if axis == self.axis else 0, 0) for axis in (0, 1)])
+        parts = self.parts or (self.partial(step), self.partial(self.ring.count - step))
+        self.parts = None
+        forward, backward = parts[0].astype(jnp.float32) + forward, parts[1].astype(jnp.float32) + backward
+        return low(forward), low(backward)
+
+    def compute(self, *earlier):
+        self.parts = after((low(self.partial(self.step)), low(self.partial(self.ring.count - self.step))), *earlier)
+
+    def prepare(self, *earlier, rider=None):
+        self.sent = self.messages(*earlier)
+        self.rider = rider
+        if rider is not None:
+            self.sent = tuple(
+                jnp.concatenate(pair, axis=1) for pair in zip(self.sent, rider.messages(*earlier))
+            )
+        self.sent = after(self.sent)
+
+    def hop(self, *earlier):
+        if self.sent is None:
+            self.prepare()
+        forward, backward = after(self.sent, *earlier)
+        self.moved = (self.ring.forth(forward), self.ring.back(backward))
+        self.sent = None
+
+    def hold(self, *others):
+        self.moved = after(self.moved, *others)
+        if self.rider is not None:
+            width = self.partial(0).shape[1]
+            self.rider.moved = tuple(part[:, width:] for part in self.moved)
+            self.moved = tuple(part[:, :width] for part in self.moved)
+            self.rider = None
+
+    def total(self):
+        own = self.partial(0).astype(jnp.float32)
+        return own + self.moved[0].astype(jnp.float32) + self.moved[1].astype(jnp.float32)
+
+
+def after(values, *earlier):
+    return lax.optimization_barrier((values, earlier))[0]
+
+
+def sum_axis(values, axis):
+    size = lax.axis_size(axis)
+    terms = [values] + [
+        lax.ppermute(values, axis, [(i, i ^ step) for i in range(size)]) for step in range(1, size)
+    ]
+    while len(terms) > 1:
+        terms = [left + right for left, right in zip(terms[::2], terms[1::2])]
+    return terms[0]
 
 
 def rms_parts(values):
@@ -413,10 +590,6 @@
 
 def rms_back(unit_grad, unit, scale_rows):
     return scale_rows * (unit_grad - unit * jnp.mean(unit_grad * unit, axis=-1, keepdims=True))
-
-
-def joined(blocks):
-    return jnp.concatenate([blocks[d] for d in range(len(blocks))])
 
 
 def sum_over_seq(values, dimension):
@@ -448,73 +621,172 @@
     def whole(weight, axis):
         return lax.all_gather(weight, "seq", axis=axis, tiled=True)
 
-    w_in = whole(attention_in.reshape(attention_in.shape[0], -1), 0)
-    w_out = whole(lax.all_gather(attention_out, "blk", axis=0, tiled=True), 1)
-    f_in = whole(feed_in.reshape(feed_in.shape[0], -1), 0)
-    f_out = whole(feed_out, 1)
-    hidden_here = f_out.shape[0]
-
+    half = count // 2
     tokens_full = tokens.astype(jnp.float32)
     scale_first, unit_first = rms_parts(tokens_full)
-    normed_a, arrival = ring.gather(low(unit_first * gain_attention))
-    proj = joined({d: low(dot_nn(normed_a[d], w_in)) for d in arrival})
+
+    length = rows * count
+    w_in = whole(attention_in.reshape(attention_in.shape[0], -1), 0)
+    gather_a = Gather(
+        ring, jnp.concatenate([low(unit_first * gain_attention), attention_out.reshape(rows, -1)], axis=1)
+    )
+
+    def project(step, kept, *earlier):
+        return project_blocks(
+            after(gather_a.groups[step], *earlier), w_in, gather_a.place(step), length, kept
+        )
+
+    gather_a.hop()
+    f_in = whole(after(feed_in, w_in, gather_a.groups[1]).reshape(feed_in.shape[0], -1), 0)
+    gather_a.hop()
+    kept = project(0, [], gather_a.groups[2])
+    for step in range(3, half + 1):
+        gather_a.hop(*([kept[1]] if step > 3 else []))
+        kept = project(step - 2, kept)
+    kept = project(half - 1, kept)
+    gather_a.groups[half] = after(gather_a.groups[half], kept[1])
+    normed_a, proj = project(half, kept)
+    w_out_rows = jnp.zeros((length, gather_a.groups[0][0].shape[1] - width), jnp.bfloat16)
+    for step, group in enumerate(gather_a.groups):
+        for piece, d, begin in zip(group, (-step % count, step), (0, rows // 2 if step == half else 0)):
+            start = ring.ahead_index[d] * rows + begin
+            w_out_rows = lax.dynamic_update_slice_in_dim(w_out_rows, piece[:, width:], start, 0)
+    w_out = whole(after(w_out_rows.reshape(-1, attention_out.shape[1]), f_in), 1)
+
+    gather_c = Gather(ring, after(cotangent, gather_a.groups[half]))
+    gather_c.hop()
     merged, attended, lse, states, norms, memory_final, norm_final = attend_forward(
         ring.order, splits, mix, proj, memory_start[0], normalizer_start[0], rows
     )
-    merged_mine = lax.all_to_all(merged, "blk", 0, 1, tiled=True)
+    merged_mine = lax.all_to_all(after(merged, gather_c.groups[1]), "blk", 0, 1, tiled=True)
+    f_out = whole(after(feed_out, w_out, merged_mine), 1)
+    while len(gather_c.groups) < half - 1:
+        gather_c.hop(merged_mine)
     middle = tokens_full + dot_nn(merged_mine, w_out)
     scale_second, unit_second = rms_parts(middle)
-
-    cot, _ = ring.gather(cotangent)
-    normed_f, arrival = ring.gather(low(unit_second * gain_feed))
-    hidden, gate_up_grad = {}, {}
-    for d in arrival:
-        gate_up = dot_nn(normed_f[d], f_in)
-        gate, up = gate_up[:, :hidden_here], gate_up[:, hidden_here:]
-        sigmoid_gate = jax.nn.sigmoid(gate)
-        activated = gate * sigmoid_gate
-        hidden[d] = low(activated * up)
-        hidden_grad = dot_nt(cot[d], f_out)
-        gate_grad = hidden_grad * up * sigmoid_gate * (1.0 + gate * (1.0 - sigmoid_gate))
-        gate_up_grad[d] = low(jnp.concatenate([gate_grad, hidden_grad * activated], axis=1))
-    normed_f_grad = ring.scatter(lambda d: dot_nt(gate_up_grad[d], f_in))
+    gather_f = Gather(ring, after(low(unit_second * gain_feed), gather_c.groups[-1]))
+    result_part, normed_f_part = {}, {}
+    kept = []
+
+    def feed(step, kept):
+        kept, results, grads = feed_blocks(
+            gather_f.groups[step], gather_c.groups[step], f_in, f_out, gather_f.place(step), length, kept
+        )
+        if step == half:
+            result_part[half], normed_f_part[half] = results, grads
+        else:
+            for d, result, grad in zip((-step % count, step), results, grads):
+                result_part[d], normed_f_part[d] = result, grad
+        return kept
+
+    for step in range(1, half + 1):
+        gather_f.hop(gather_c.groups[-1], *kept[2:3])
+        if step > 1:
+            kept = feed(step - 1 if step < half else half, kept)
+        if len(gather_c.groups) <= half:
+            gather_c.hop(gather_f.groups[step], *(kept[2:3] if step > 1 else []))
+        if step == 1:
+            kept = feed(0, kept)
+    kept = feed(half - 1, kept)
+    normed_f, cot, hidden, gate_grad, up_grad = kept
+
+    scatter_f = Scatter(ring, lambda d: normed_f_part[d])
+    for _ in range(half - 2):
+        scatter_f.hop()
+    feed_out_local = low(dot_tn(hidden, after(cot, scatter_f.moved)))
+    scatter_f.hop()
+    scatter_f.hold(feed_out_local)
+    feed_gate_local = low(dot_tn(normed_f, after(gate_grad, scatter_f.moved)))
+    feed_out_grad = sum_over_seq(after(feed_out_local, scatter_f.moved), 1)
+    scatter_f.hop()
+    scatter_f.hold(feed_gate_local)
+    normed_f_grad = scatter_f.total()
+    feed_up_local = low(dot_tn(normed_f, after(up_grad, normed_f_grad)))
+    scatter_r = Scatter(ring, lambda d: result_part[d])
+    scatter_r.hop(normed_f_grad)
     gain_feed_part = jnp.sum(normed_f_grad * unit_second, axis=0)
     middle_grad = cotangent.astype(jnp.float32) + rms_back(
         normed_f_grad * gain_feed, unit_second, scale_second
     )
     out_grad = low(middle_grad)
-    combined_grad = lax.all_to_all(low(dot_nt(out_grad, w_out)), "blk", 1, 0, tiled=True)
+    combined_grad = after(low(dot_nt(out_grad, w_out)), scatter_r.moved)
+    attention_out_local = low(dot_tn(merged_mine, out_grad))
+    combined_grad = lax.all_to_all(combined_grad, "blk", 1, 0, tiled=True)
+    combined_grad = after(combined_grad, attention_out_local, feed_up_local)
+    out_sum = sum_over_seq(after(attention_out_local, feed_out_grad, combined_grad), 1)
+    scatter_r.hop(combined_grad)
     proj_grad, gate_rows = attend_backward(
-        ring.order, splits, mix, proj, combined_grad, attended, lse, states, norms, rows
+        ring.order, splits, mix, proj, combined_grad,
+        attended, lse, states, norms, rows,
     )
-    result = middle + ring.scatter(lambda d: dot_nn(hidden[d], f_out))
-
-    normed_a_grad = ring.scatter(lambda d: dot_nt(proj_grad[d * rows : (d + 1) * rows], w_in))
-    token_grad = middle_grad + rms_back(normed_a_grad * gain_attention, unit_first, scale_first)
-
-    feed_out_grad = sum_over_seq(dot_tn(joined(hidden), joined(cot)), 1)
-    feed_in_grad = sum_over_seq(dot_tn(joined(normed_f), joined(gate_up_grad)), 0)
-    attention_out_grad = lax.psum_scatter(
-        sum_over_seq(dot_tn(merged_mine, out_grad), 1), "blk", scatter_dimension=0, tiled=True
-    )
-    attention_in_local = dot_tn(joined(normed_a), proj_grad)
-    attention_in_grad = sum_over_seq(attention_in_local, 0)
-    gain_attention_part = jnp.sum(attention_in_local * w_in.astype(jnp.float32), axis=1) / gain_attention
+    def in_two(values):
+        return values[: values.shape[0] // 2], values[values.shape[0] // 2 :]
+
+    def normed_a_part(d):
+        first = ring.slots[d] * rows
+        if d == half:
+            return [low(dot_nt(part, w_in)) for part in in_two(proj_grad[first : first + rows])]
+        return dot_nt(proj_grad[first : first + rows], w_in)
+
+    proj_grad = after(proj_grad, scatter_r.moved)
+    def attention_out_part(d):
+        high = attention_out.shape[0]
+        part = lax.dynamic_slice_in_dim(out_sum, ring.ahead_index[d] * high, high, 0).reshape(rows, -1)
+        return (part[:, : part.shape[1] // 2], part[:, part.shape[1] // 2 :]) if d == half else part
+
+    scatter_o = Scatter(ring, attention_out_part, axis=1)
+
+    def rider():
+        return scatter_o if scatter_o.step > 0 else None
+
+    scatter_a = Scatter(ring, normed_a_part)
+    scatter_a.hop()
+    scatter_a.hop()
+    scatter_r.prepare(proj_grad, rider=rider())
+    scatter_a.hold(scatter_r.sent)
+    feed_gate_grad = sum_over_seq(after(feed_gate_local, out_sum, scatter_a.moved), 0)
+    scatter_r.hop(scatter_a.moved)
+    attention_in_local = low(dot_tn(normed_a, after(proj_grad, scatter_a.moved)))
+    gain_attention_part = jnp.sum(attention_in_local.astype(jnp.float32) * w_in.astype(jnp.float32), axis=1) / gain_attention
     gate_part = jnp.sum(gate_rows, axis=1) * mix * (1.0 - mix)
     gate_full = lax.dynamic_update_slice_in_dim(
         jnp.zeros(gate_logit.shape, jnp.float32), gate_part, head_first, 0
     )
-    sums = sum_everywhere(jnp.concatenate([gain_attention_part, gain_feed_part, gate_full]))
+    sums = jnp.concatenate([gain_attention_part, gain_feed_part, gate_full])
+    scatter_a.compute()
+    scatter_r.hold(scatter_a.parts, attention_in_local)
+    feed_up_grad = sum_over_seq(after(feed_up_local, feed_gate_grad, scatter_r.moved), 0)
+    while scatter_a.step > 1:
+        scatter_a.prepare(rider=rider())
+        scatter_a.hop(scatter_r.moved)
+        scatter_a.hold()
+        scatter_r.prepare(rider=rider())
+        scatter_r.hop(scatter_a.moved)
+        scatter_a.compute()
+        scatter_r.hold(scatter_a.parts)
+    scatter_a.prepare(rider=rider())
+    attention_in_grad = sum_over_seq(after(attention_in_local, feed_up_grad, scatter_a.sent), 0)
+    sums = sum_axis(after(sums, scatter_a.sent), "seq")
+    scatter_a.hop()
+    result = low(middle + scatter_r.total())
+    feed_in_grad = jnp.stack([feed_gate_grad, feed_up_grad], axis=1).astype(jnp.float32)
+    feed_out_grad = feed_out_grad.astype(jnp.float32)
+    sums = sum_axis(after(sums, result, feed_in_grad, feed_out_grad), "blk")
+    attention_in_grad = attention_in_grad.astype(jnp.float32).reshape(attention_in.shape)
+    scatter_a.hold(sums)
+    attention_out_grad = scatter_o.total().reshape(attention_out.shape)
+    normed_a_grad = scatter_a.total()
+    token_grad = middle_grad + rms_back(normed_a_grad * gain_attention, unit_first, scale_first)
     return (
-        low(result),
+        result,
         token_grad,
         sums[:width],
-        attention_in_grad.astype(jnp.float32).reshape(attention_in.shape),
+        attention_in_grad,
         sums[2 * width :],
         attention_out_grad.astype(jnp.float32),
         sums[width : 2 * width],
-        feed_in_grad.astype(jnp.float32).reshape(feed_in.shape),
-        feed_out_grad.astype(jnp.float32),
+        feed_in_grad,
+        feed_out_grad,
         memory_final[None],
         norm_final[None],
     )

time: 910 us -> 782 us (0.86)
  waiting for transfers between devices: 443 us -> 293 us
  Pallas kernels: 34 us -> 179 us
  matrix products: 235 us -> 90.9 us
  local copies, waits for them, and re-layouts: 73.1 us -> 48.2 us
  blocking collectives: 0 us -> 23.8 us
  other arithmetic: 36.2 us -> 47.2 us
    ppermute x24, waiting for transfers between devices: 192 us -> 25.6 us  [back(): return lax.ppermute(values, 'blk', self.behind)]
    pallas_call x0 -> x10, Pallas kernels: none -> 130 us  [the longest x5 104 us: feed_blocks(): pl.pallas_call(functools.partial(feed_kernel, count=count), grid=(tiles,)...]
    ppermute x24, waiting for transfers between devices: 117 us -> 224 us  [forth(): return lax.ppermute(values, 'blk', self.ahead)]
    dot_general x25 -> x10, matrix products: 107 us -> 28.4 us  [dot_nt(): lax.dot_general(left, right, (((1,), (1,)), ((), ())), preferred_element_...]
    dot_general x25 -> x1, matrix products: 72.4 us -> 6.17 us  [dot_nn(): lax.dot_general(left, right, (((1,), (0,)), ((), ())), preferred_element_...]
    all_gather x1 -> x0, waiting for transfers between devices: 51.8 us -> none  [per_device(): w_out = whole(lax.all_gather(attention_out, 'blk', axis=0, tiled=True), 1)]
    reduce_scatter x1 -> x0, waiting for transfers between devices: 46.2 us -> none  [per_device(): lax.psum_scatter(sum_over_seq(dot_tn(merged_mine, out_grad), 1), 'blk', s...]
    unnamed x235 -> x128, local copies, waits for them, and re-layouts: 50.8 us -> 17 us
  transfers between devices with their start and end apart: 65 -> 68, of which waited for: 30 -> 38; matrix products, arithmetic and copies ran while one was open for 34% -> 21% of each run, Pallas kernels for 4% -> 21%
where the time goes in v2:
time: 782 us; the launch traced here: 772 us
  waiting for transfers between devices  293 us (37%)
  Pallas kernels  179 us (23%)
  matrix products  90.9 us (12%)
  starting transfers between devices  69.2 us (9%)
  local copies, waits for them, and re-layouts  48.2 us (6%)
  other arithmetic  47.2 us (6%)
  blocking collectives  23.8 us (3%)
  between operations  21.2 us (3%)
    ppermute x24, waiting for transfers between devices, forth(): return lax.ppermute(values, 'blk', self.ahead)  224 us
    pallas_call x5, Pallas kernels, feed_blocks(): pl.pallas_call(functools.partial(feed_kernel, count=count), grid=(tiles,)...  104 us
    dot_general x5, matrix products, dot_tn(): lax.dot_general(left, right, (((0,), (0,)), ((), ())), preferred_element_...  56.3 us
    ppermute x24, starting transfers between devices, forth(): return lax.ppermute(values, 'blk', self.ahead)  34.1 us
    dot_general x10, matrix products, dot_nt(): lax.dot_general(left, right, (((1,), (1,)), ((), ())), preferred_element_...  28.4 us
    pallas_call x1, Pallas kernels, attend_backward(): pl.pallas_call(functools.partial(backward_kernel, rows=rows, heads=heads,...  28.3 us
    convert_element_type x20, other arithmetic, low(): return values.astype(jnp.bfloat16)  27.8 us
    pallas_call x5, Pallas kernels, project_blocks(): pl.pallas_call(functools.partial(project_kernel, count=count), grid=(wide...  26.7 us
  transfers between devices with their start and end apart: 68, of which 38 were waited for; matrix products, arithmetic and copies ran while one was open for 21% of the time, Pallas kernels for 21%

profile of v2, /device:TPU:0, one launch (start us, length us, event | category | flops | bytes accessed | tf_op | source)
XLA Modules:
  0.0 771.7 jit_solution(12717004413457987969)
XLA Ops:
  11.0 3.1 collective-permute-start
  15.0 27.9 %collective-permute-done.refs_0_ = bf16[256,2560]{1,0:T(8,128)(2,1)} collective-permute-done((bf16[256,2560]{1,0:T(8,128)(2,1)S(1)}, bf16[256,2560]{1,0:T(8,128)(2,1)}, u32[]{:S(2)}, u32[]{:S(2)}) %collective-permute-start) | collective-permute-done | bytes 1310752 | tf_op jit(solution)/shard_map/ppermute | solution.py:492
  49.1 27.0 %collective-permute-done.2.refs_0_ = bf16[256,2560]{1,0:T(8,128)(2,1)} collective-permute-done((bf16[256,2560]{1,0:T(8,128)(2,1)}, bf16[256,2560]{1,0:T(8,128)(2,1)}, u32[]{:S(2)}, u32[]{:S(2)}) %collective-permute-start.2) | collective-permute-done | bytes 1310752 | tf_op jit(solution)/shard_map/ppermute | solution.py:492
  90.7 15.1 %collective-permute-done.4.refs_0_ = bf16[256,2560]{1,0:T(8,128)(2,1)} collective-permute-done((bf16[256,2560]{1,0:T(8,128)(2,1)}, bf16[256,2560]{1,0:T(8,128)(2,1)}, u32[]{:S(2)}, u32[]{:S(2)}) %collective-permute-start.4) | collective-permute-done | bytes 1310752 | tf_op jit(solution)/shard_map/ppermute | solution.py:492
  109.1 4.6 shard_map.230
  113.6 5.7 shard_map.231
  125.3 5.7 shard_map.232
  131.0 5.7 shard_map.233
  146.6 5.1 shard_map.234
  151.7 20.1 %shard_map.235 = (bf16[2048,256]{1,0:T(8,128)(2,1)}, f32[2048,256]{1,0:T(8,128)}, f32[4,2,512]{2,1,0:T(2,128)}, f32[2,2,128,128]{3,2,1,0:T(8,128)}, f32[2,2,128]...) custom-call(s32[8]{0:T(128)} %gather_fusion, s32[1]{0:T(128)} %bitcast.54.splits, f32[2]{0:T(128)} %add_divide_fusion.mix, ...), custom_call_target="tpu_custom_call" | custom-call | flops 4000000000 | bytes 4096 | tf_op jit(solution)/shard_map/pallas_call | solution.py:301
  173.3 23.8 %all_to_all.38 = bf16[8,256,256]{1,2,0:T(8,128)(2,1)} all-to-all(bf16[8,256,256]{1,2,0:T(8,128)(2,1)S(1)} %copy.61), channel_id=1, replica_groups=mesh['seq'=4,'blk'=8] {'blk'}, dimensions={0} | all-to-all | bytes 2097152 | tf_op jit(solution)/shard_map/all_to_all | solution.py:661
  200.7 6.2 multiply_reduce_fusion.3
  207.2 17.0 %collective-permute-done.10.refs_2_ = bf16[256,2048]{1,0:T(8,128)(2,1)} collective-permute-done((bf16[256,2048]{1,0:T(8,128)(2,1)}, bf16[256,2048]{1,0:T(8,128)(2,1)}, u32[]{:S(2)}, u32[]{:S(2)}) %collective-permute-start.10) | collective-permute-done | bytes 1048608 | tf_op jit(solution)/shard_map/ppermute | solution.py:492
  227.6 22.2 %collective-permute-done.12.refs_0_ = bf16[256,2048]{1,0:T(8,128)(2,1)S(1)} collective-permute-done((bf16[256,2048]{1,0:T(8,128)(2,1)S(1)}, bf16[256,2048]{1,0:T(8,128)(2,1)S(1)}, u32[]{:S(2)}, u32[]{:S(2)}) %collective-permute-start.12) | collective-permute-done | bytes 1048608 | tf_op jit(solution)/shard_map/ppermute | solution.py:492
  253.0 14.6 %shard_map.236 = (bf16[2048,2048]{1,0:T(8,128)(2,1)}, bf16[2048,2048]{1,0:T(8,128)(2,1)}, bf16[2048,1024]{1,0:T(8,128)(2,1)}, bf16[2048,1024]{1,0:T(8,128)(2,1)}...) custom-call(bf16[256,2048]{1,0:T(8,128)(2,1)} %copy-done.14, ...), custom_call_target="tpu_custom_call" | custom-call | flops 4000000000 | bytes 4096 | tf_op jit(solution)/shard_map/pallas_call | solution.py:440
  267.6 6.8 collective-permute-done.14.refs_2_
  277.6 24.8 %shard_map.237 = (bf16[2048,2048]{1,0:T(8,128)(2,1)}, bf16[2048,2048]{1,0:T(8,128)(2,1)}, bf16[2048,1024]{1,0:T(8,128)(2,1)}, bf16[2048,1024]{1,0:T(8,128)(2,1)}...) custom-call(bf16[256,2048]{1,0:T(8,128)(2,1)} %copy-done.47, ...), custom_call_target="tpu_custom_call", output_to_operand_aliasing={{0}: (7, {}), {1}: (8, {}), {2}: (9, {}), {3}: (10, {}), {4... | custom-call | flops 4000000000 | bytes 4096 | tf_op jit(solution)/shard_map/pallas_call | solution.py:440
  307.1 6.9 collective-permute-done.18.refs_2_
  319.6 24.8 %shard_map.238 = (bf16[2048,2048]{1,0:T(8,128)(2,1)}, bf16[2048,2048]{1,0:T(8,128)(2,1)}, bf16[2048,1024]{1,0:T(8,128)(2,1)}, bf16[2048,1024]{1,0:T(8,128)(2,1)}...) custom-call(bf16[256,2048]{1,0:T(8,128)(2,1)} %copy-done.46, ...), custom_call_target="tpu_custom_call", output_to_operand_aliasing={{0}: (7, {}), {1}: (8, {}), {2}: (9, {}), {3}: (10, {}), {4... | custom-call | flops 4000000000 | bytes 4096 | tf_op jit(solution)/shard_map/pallas_call | solution.py:440
  347.7 6.0 collective-permute-done.22.refs_0_
  356.6 14.6 %shard_map.239 = (bf16[2048,2048]{1,0:T(8,128)(2,1)}, bf16[2048,2048]{1,0:T(8,128)(2,1)}, bf16[2048,1024]{1,0:T(8,128)(2,1)}, bf16[2048,1024]{1,0:T(8,128)(2,1)}...) custom-call(bf16[128,2048]{1,0:T(8,128)(2,1)} %copy-done.51, ...), custom_call_target="tpu_custom_call", output_to_operand_aliasing={{0}: (7, {}), {1}: (8, {}), {2}: (9, {}), {3}: (10, {}), {4... | custom-call | flops 4000000000 | bytes 4096 | tf_op jit(solution)/shard_map/pallas_call | solution.py:440
  373.5 24.8 %shard_map.240 = (bf16[2048,2048]{1,0:T(8,128)(2,1)}, bf16[2048,2048]{1,0:T(8,128)(2,1)}, bf16[2048,1024]{1,0:T(8,128)(2,1)}, bf16[2048,1024]{1,0:T(8,128)(2,1)}...) custom-call(bf16[256,2048]{1,0:T(8,128)(2,1)} %copy-done.20, ...), custom_call_target="tpu_custom_call", output_to_operand_aliasing={{0}: (7, {}), {1}: (8, {}), {2}: (9, {}), {3}: (10, {}), {4... | custom-call | flops 4000000000 | bytes 4096 | tf_op jit(solution)/shard_map/pallas_call | solution.py:440
  402.2 17.5 %collective-permute-done.26 = bf16[256,2048]{1,0:T(8,128)(2,1)S(1)} collective-permute-done((bf16[256,2048]{1,0:T(8,128)(2,1)S(1)}, bf16[256,2048]{1,0:T(8,128)(2,1)S(1)}, u32[]{:S(2)}, u32[]{:S(2)}) %collective-permute-start.26) | collective-permute-done | bytes 1048608 | tf_op jit(solution)/shard_map/ppermute | solution.py:492
  426.7 12.4 %convolution_convert_fusion.1 = bf16[1024,2048]{1,0:T(8,128)(2,1)} fusion(bf16[2048,1024]{1,0:T(8,128)(2,1)} %get-tuple-element.297, bf16[2048,2048]{1,0:T(8,128)(2,1)S(1)} %copy-done.2), kind=kOutput, calls=%fused_computation.4 | convolution fusion | flops 8592031744 | bytes 16777216 | tf_op jit(solution)/shard_map/dot_general | solution.py:29
  450.3 13.0 %convolution_convert_fusion.3 = bf16[2048,1024]{1,0:T(8,128)(2,1)} fusion(bf16[2048,2048]{1,0:T(8,128)(2,1)} %get-tuple-element.307, bf16[2048,1024]{1,0:T(8,128)(2,1)S(1)} %copy-done.4), kind=kOutput, calls=%fused_computation.6 | convolution fusion | flops 8592031744 | bytes 16777216 | tf_op jit(solution)/shard_map/dot_general | solution.py:29
  463.3 3.4 collective-permute-done.30
  468.7 2.9 multiply_reduce_fusion.1
  474.3 6.5 convolution_convert_fusion.9
  480.9 5.7 convolution_convert_fusion
  488.3 3.6 all-to-all-start.1
  491.9 14.0 %convolution_convert_fusion.2 = bf16[2048,1024]{1,0:T(8,128)(2,1)} fusion(bf16[2048,2048]{1,0:T(8,128)(2,1)} %get-tuple-element.307, bf16[2048,1024]{1,0:T(8,128)(2,1)} %get-tuple-element.321), kind=kOutput, calls=%fused_computation.5 | convolution fusion | flops 8592031744 | bytes 16777216 | tf_op jit(solution)/shard_map/dot_general | solution.py:29
  505.9 5.0 all-to-all-done.1
  519.1 28.3 %shard_map.241 = (bf16[2048,768]{1,0:T(8,128)(2,1)}, f32[2,128]{1,0:T(2,128)}) custom-call(s32[8]{0:T(128)} %gather_fusion, s32[1]{0:T(128)} %bitcast.55.splits, f32[2]{0:T(128)} %add_divide_fusion.mix, bf16[2048,768]{1,0:T(8,128)(2,1)} %get-tuple-element.227.proj, bf16[2048,256]{1,0:T(8,128)(2,1)} %bitcast.62, f32[2048,256]{1,0:T(8,128)} %get-tuple-element.325.attended, ...), custom_call_target="tpu_custom_call" | custom-call | flops 4000000000 | bytes 4096 | tf_op jit(solution)/shard_map/pallas_call | solution.py:322
  556.4 9.1 %collective-permute-done.36 = bf16[128,2048]{1,0:T(8,128)(2,1)S(1)} collective-permute-done((bf16[128,2048]{1,0:T(8,128)(2,1)S(1)}, bf16[128,2048]{1,0:T(8,128)(2,1)S(1)}, u32[]{:S(2)}, u32[]{:S(2)}) %collective-permute-start.36) | collective-permute-done | bytes 524320 | tf_op jit(solution)/shard_map/ppermute | solution.py:492
  565.5 3.0 fusion.6
  568.5 3.1 fusion.5
  576.2 6.6 reduce-scatter.8.cloned.1.call-done
  588.4 3.1 convolution_convert_fusion.7
  595.8 11.2 %multiply_reduce_fusion = (f32[2048]{0:T(1024)S(1)}, bf16[2048,768]{1,0:T(8,128)(2,1)}) fusion(bf16[2048,768]{1,0:T(8,128)(2,1)S(1)} %copy-done.3, bf16[2048,2048]{1,0:T(8,128)(2,1)} %get-tuple-element.352, bf16[2048,768]{1,0:T(8,128)(2,1)S(1)} %copy-done.53), kind=kOutput, calls=%fused_computation.3 | convolution fusion | flops 6450313216 | bytes 17833984 | tf_op jit(solution)/shard_map/dot_general | solution.py:29
  607.0 13.6 %collective-permute-done.40 = bf16[256,2304]{1,0:T(8,128)(2,1)} collective-permute-done((bf16[256,2304]{1,0:T(8,128)(2,1)S(1)}, bf16[256,2304]{1,0:T(8,128)(2,1)}, u32[]{:S(2)}, u32[]{:S(2)}) %collective-permute-start.40) | collective-permute-done | bytes 1179680 | tf_op jit(solution)/shard_map/ppermute | solution.py:492
  626.3 5.7 reduce-scatter.10.cloned.1.call-done
  632.1 3.2 add_convert_fusion.4
  641.6 25.5 %collective-permute-done.42 = bf16[256,2560]{1,0:T(8,128)(2,1)S(1)} collective-permute-done((bf16[256,2560]{1,0:T(8,128)(2,1)S(1)}, bf16[256,2560]{1,0:T(8,128)(2,1)S(1)}, u32[]{:S(2)}, u32[]{:S(2)}) %collective-permute-start.42) | collective-permute-done | bytes 1310752 | tf_op jit(solution)/shard_map/ppermute | solution.py:492
  675.6 23.7 %collective-permute-done.44 = bf16[256,2560]{1,0:T(8,128)(2,1)S(1)} collective-permute-done((bf16[256,2560]{1,0:T(8,128)(2,1)S(1)}, bf16[256,2560]{1,0:T(8,128)(2,1)S(1)}, u32[]{:S(2)}, u32[]{:S(2)}) %collective-permute-start.44) | collective-permute-done | bytes 1310752 | tf_op jit(solution)/shard_map/ppermute | solution.py:492
  704.2 3.0 convert_element_type.395
  711.4 3.4 add_convert_fusion.2
  718.8 22.3 %collective-permute-done.51 = f32[4112]{0:T(1024)S(1)} collective-permute-done((f32[4112]{0:T(1024)S(1)}, f32[4112]{0:T(1024)S(1)}, u32[]{:S(2)}, u32[]{:S(2)}) %collective-permute-start.51) | collective-permute-done | bytes 16480 | tf_op jit(solution)/shard_map/ppermute | solution.py:579
  749.2 5.2 copy.66
  (346 shorter events, 184.0 us)
Async XLA Ops:
  7.2 37.2 %all-gather.5.cloned.1.call-start = ((), (), s32[]{:S(2)}) async-start(), calls=%async_computation.7 | async-start | bytes 3932160 | tf_op jit(solution)/shard_map/all_gather | solution.py:622
  9.9 130.2 %all-gather.7.cloned.1.call-start = ((), (), s32[]{:S(2)}) async-start(), calls=%async_computation.8 | async-start | bytes 10485760 | tf_op jit(solution)/shard_map/all_gather | solution.py:622
  11.0 31.9 %collective-permute-start = (bf16[256,2560]{1,0:T(8,128)(2,1)S(1)}, bf16[256,2560]{1,0:T(8,128)(2,1)}, u32[]{:S(2)}, u32[]{:S(2)}) collective-permute-start(bf16[256,2560]{1,0:T(8,128)(2,1)S(1)} %pad_maximum_fusion.refs_0_), channel_id=1, source_target_pairs={{0,2},{2,4},{4,6},{6,7},{7,5},{5,3},{3,1},{1,0},{8,10},{10,12},{12... | collective-permute-start | bytes 3932168 | tf_op jit(solution)/shard_map/ppermute | solution.py:492
  14.0 30.3 %collective-permute-start.1 = (bf16[256,2560]{1,0:T(8,128)(2,1)S(1)}, bf16[256,2560]{1,0:T(8,128)(2,1)}, u32[]{:S(2)}, u32[]{:S(2)}) collective-permute-start(bf16[256,2560]{1,0:T(8,128)(2,1)S(1)} %pad_maximum_fusion.refs_0_), channel_id=1, source_target_pairs={{2,0},{4,2},{6,4},{7,6},{5,7},{3,5},{1,3},{0,1},{10,8},{12,10},{14... | collective-permute-start | bytes 3932168 | tf_op jit(solution)/shard_map/ppermute | solution.py:495
  46.4 152.0 %all-gather.9.cloned.1.call-start = ((), (), s32[]{:S(2)}) async-start(), calls=%async_computation.9 | async-start | bytes 10485760 | tf_op jit(solution)/shard_map/all_gather | solution.py:622
  46.4 29.7 %collective-permute-start.2 = (bf16[256,2560]{1,0:T(8,128)(2,1)}, bf16[256,2560]{1,0:T(8,128)(2,1)}, u32[]{:S(2)}, u32[]{:S(2)}) collective-permute-start(bf16[256,2560]{1,0:T(8,128)(2,1)} %collective-permute-done.refs_0_), channel_id=1, source_target_pairs={{0,2},{2,4},{4,6},{6,7},{7,5},{5,3},{3,1},{1,0},{8,10},{10,12},{12... | collective-permute-start | bytes 3932168 | tf_op jit(solution)/shard_map/ppermute | solution.py:492
  48.0 29.4 %collective-permute-start.3 = (bf16[256,2560]{1,0:T(8,128)(2,1)}, bf16[256,2560]{1,0:T(8,128)(2,1)}, u32[]{:S(2)}, u32[]{:S(2)}) collective-permute-start(bf16[256,2560]{1,0:T(8,128)(2,1)} %collective-permute-done.1.refs_1_), channel_id=1, source_target_pairs={{2,0},{4,2},{6,4},{7,6},{5,7},{3,5},{1,3},{0,1},{10,8},{12,10},{14... | collective-permute-start | bytes 3932168 | tf_op jit(solution)/shard_map/ppermute | solution.py:495
  77.4 28.4 %collective-permute-start.4 = (bf16[256,2560]{1,0:T(8,128)(2,1)}, bf16[256,2560]{1,0:T(8,128)(2,1)}, u32[]{:S(2)}, u32[]{:S(2)}) collective-permute-start(bf16[256,2560]{1,0:T(8,128)(2,1)} %collective-permute-done.2.refs_0_), channel_id=1, source_target_pairs={{0,2},{2,4},{4,6},{6,7},{7,5},{5,3},{3,1},{1,0},{8,10},{10,12},{12... | collective-permute-start | bytes 3932168 | tf_op jit(solution)/shard_map/ppermute | solution.py:492
  79.0 28.2 %collective-permute-start.5 = (bf16[256,2560]{1,0:T(8,128)(2,1)}, bf16[256,2560]{1,0:T(8,128)(2,1)}, u32[]{:S(2)}, u32[]{:S(2)}) collective-permute-start(bf16[256,2560]{1,0:T(8,128)(2,1)} %collective-permute-done.3.refs_1_), channel_id=1, source_target_pairs={{2,0},{4,2},{6,4},{7,6},{5,7},{3,5},{1,3},{0,1},{10,8},{12,10},{14... | collective-permute-start | bytes 3932168 | tf_op jit(solution)/shard_map/ppermute | solution.py:495
  141.4 111.6 %all-gather.11.cloned.1.call-start = ((), (), s32[]{:S(2)}) async-start(), calls=%async_computation.10 | async-start | bytes 5242880 | tf_op jit(solution)/shard_map/all_gather | solution.py:622
  141.4 30.3 %collective-permute-start.8 = (bf16[256,2048]{1,0:T(8,128)(2,1)}, bf16[256,2048]{1,0:T(8,128)(2,1)}, u32[]{:S(2)}, u32[]{:S(2)}) collective-permute-start(bf16[256,2048]{1,0:T(8,128)(2,1)} %refs_1_), channel_id=1, source_target_pairs={{0,2},{2,4},{4,6},{6,7},{7,5},{5,3},{3,1},{1,0},{8,10},{10,12},{12... | collective-permute-start | bytes 3145736 | tf_op jit(solution)/shard_map/ppermute | solution.py:492
  143.2 28.5 %collective-permute-start.9 = (bf16[256,2048]{1,0:T(8,128)(2,1)}, bf16[256,2048]{1,0:T(8,128)(2,1)}, u32[]{:S(2)}, u32[]{:S(2)}) collective-permute-start(bf16[256,2048]{1,0:T(8,128)(2,1)} %refs_1_), channel_id=1, source_target_pairs={{2,0},{4,2},{6,4},{7,6},{5,7},{3,5},{1,3},{0,1},{10,8},{12,10},{14... | collective-permute-start | bytes 3145736 | tf_op jit(solution)/shard_map/ppermute | solution.py:495
  198.4 312.5 %reduce-scatter.6.cloned.1.call-start = ((), (), s32[]{:S(2)}) async-start(), calls=%async_computation.11 | async-start | bytes 5242880 | tf_op jit(solution)/shard_map/reduce_scatter | solution.py:596
  198.5 25.7 %collective-permute-start.10 = (bf16[256,2048]{1,0:T(8,128)(2,1)}, bf16[256,2048]{1,0:T(8,128)(2,1)}, u32[]{:S(2)}, u32[]{:S(2)}) collective-permute-start(bf16[256,2048]{1,0:T(8,128)(2,1)} %collective-permute-done.8.refs_2_), channel_id=1, source_target_pairs={{0,2},{2,4},{4,6},{6,7},{7,5},{5,3},{3,1},{1,0},{8,10},{10,12},{12... | collective-permute-start | bytes 3145736 | tf_op jit(solution)/shard_map/ppermute | solution.py:492
  200.0 25.5 %collective-permute-start.11 = (bf16[256,2048]{1,0:T(8,128)(2,1)}, bf16[256,2048]{1,0:T(8,128)(2,1)}, u32[]{:S(2)}, u32[]{:S(2)}) collective-permute-start(bf16[256,2048]{1,0:T(8,128)(2,1)} %collective-permute-done.9.refs_3_), channel_id=1, source_target_pairs={{2,0},{4,2},{6,4},{7,6},{5,7},{3,5},{1,3},{0,1},{10,8},{12,10},{14... | collective-permute-start | bytes 3145736 | tf_op jit(solution)/shard_map/ppermute | solution.py:495
  225.6 24.2 %collective-permute-start.12 = (bf16[256,2048]{1,0:T(8,128)(2,1)S(1)}, bf16[256,2048]{1,0:T(8,128)(2,1)S(1)}, u32[]{:S(2)}, u32[]{:S(2)}) collective-permute-start(bf16[256,2048]{1,0:T(8,128)(2,1)S(1)} %multiply_convert_fusion.refs_0_), channel_id=1, source_target_pairs={{0,2},{2,4},{4,6},{6,7},{7,5},{5,3},{3,1},{1,0},{8,10},{10,12},{12... | collective-permute-start | bytes 3145736 | tf_op jit(solution)/shard_map/ppermute | solution.py:492
  227.0 23.9 %collective-permute-start.13 = (bf16[256,2048]{1,0:T(8,128)(2,1)S(1)}, bf16[256,2048]{1,0:T(8,128)(2,1)S(1)}, u32[]{:S(2)}, u32[]{:S(2)}) collective-permute-start(bf16[256,2048]{1,0:T(8,128)(2,1)S(1)} %multiply_convert_fusion.refs_0_), channel_id=1, source_target_pairs={{2,0},{4,2},{6,4},{7,6},{5,7},{3,5},{1,3},{0,1},{10,8},{12,10},{14... | collective-permute-start | bytes 3145736 | tf_op jit(solution)/shard_map/ppermute | solution.py:495
  251.0 23.4 %collective-permute-start.14 = (bf16[256,2048]{1,0:T(8,128)(2,1)}, bf16[256,2048]{1,0:T(8,128)(2,1)}, u32[]{:S(2)}, u32[]{:S(2)}) collective-permute-start(bf16[256,2048]{1,0:T(8,128)(2,1)} %collective-permute-done.10.refs_2_), channel_id=1, source_target_pairs={{0,2},{2,4},{4,6},{6,7},{7,5},{5,3},{3,1},{1,0},{8,10},{10,12},{12... | collective-permute-start | bytes 3145736 | tf_op jit(solution)/shard_map/ppermute | solution.py:492
  252.4 23.1 %collective-permute-start.15 = (bf16[256,2048]{1,0:T(8,128)(2,1)}, bf16[256,2048]{1,0:T(8,128)(2,1)}, u32[]{:S(2)}, u32[]{:S(2)}) collective-permute-start(bf16[256,2048]{1,0:T(8,128)(2,1)} %collective-permute-done.11.refs_3_), channel_id=1, source_target_pairs={{2,0},{4,2},{6,4},{7,6},{5,7},{3,5},{1,3},{0,1},{10,8},{12,10},{14... | collective-permute-start | bytes 3145736 | tf_op jit(solution)/shard_map/ppermute | solution.py:495
  275.5 26.9 %collective-permute-start.16 = (bf16[256,2048]{1,0:T(8,128)(2,1)}, bf16[256,2048]{1,0:T(8,128)(2,1)S(1)}, u32[]{:S(2)}, u32[]{:S(2)}) collective-permute-start(bf16[256,2048]{1,0:T(8,128)(2,1)} %copy-done.47), channel_id=1, source_target_pairs={{0,2},{2,4},{4,6},{6,7},{7,5},{5,3},{3,1},{1,0},{8,10},{10,12},{12... | collective-permute-start | bytes 3145736 | tf_op jit(solution)/shard_map/ppermute | solution.py:492
  277.0 25.4 %collective-permute-start.17 = (bf16[256,2048]{1,0:T(8,128)(2,1)}, bf16[256,2048]{1,0:T(8,128)(2,1)}, u32[]{:S(2)}, u32[]{:S(2)}) collective-permute-start(bf16[256,2048]{1,0:T(8,128)(2,1)} %copy-done.48), channel_id=1, source_target_pairs={{2,0},{4,2},{6,4},{7,6},{5,7},{3,5},{1,3},{0,1},{10,8},{12,10},{14... | collective-permute-start | bytes 3145736 | tf_op jit(solution)/shard_map/ppermute | solution.py:495
  317.2 27.2 %collective-permute-start.20 = (bf16[256,2048]{1,0:T(8,128)(2,1)}, bf16[256,2048]{1,0:T(8,128)(2,1)S(1)}, u32[]{:S(2)}, u32[]{:S(2)}) collective-permute-start(bf16[256,2048]{1,0:T(8,128)(2,1)} %copy-done.46), channel_id=1, source_target_pairs={{0,2},{2,4},{4,6},{6,7},{7,5},{5,3},{3,1},{1,0},{8,10},{10,12},{12... | collective-permute-start | bytes 3145736 | tf_op jit(solution)/shard_map/ppermute | solution.py:492
  318.8 25.6 %collective-permute-start.21 = (bf16[256,2048]{1,0:T(8,128)(2,1)}, bf16[256,2048]{1,0:T(8,128)(2,1)}, u32[]{:S(2)}, u32[]{:S(2)}) collective-permute-start(bf16[256,2048]{1,0:T(8,128)(2,1)} %collective-permute-done.17.refs_1_), channel_id=1, source_target_pairs={{2,0},{4,2},{6,4},{7,6},{5,7},{3,5},{1,3},{0,1},{10,8},{12,10},{14... | collective-permute-start | bytes 3145736 | tf_op jit(solution)/shard_map/ppermute | solution.py:495
  371.2 27.1 %collective-permute-start.24 = (bf16[128,2048]{1,0:T(8,128)(2,1)}, bf16[128,2048]{1,0:T(8,128)(2,1)S(1)}, u32[]{:S(2)}, u32[]{:S(2)}) collective-permute-start(bf16[128,2048]{1,0:T(8,128)(2,1)} %get-tuple-element.285), channel_id=1, source_target_pairs={{0,2},{2,4},{4,6},{6,7},{7,5},{5,3},{3,1},{1,0},{8,10},{10,12},{12... | collective-permute-start | bytes 1572872 | tf_op jit(solution)/shard_map/ppermute | solution.py:492
  372.9 25.4 %collective-permute-start.25 = (bf16[128,2048]{1,0:T(8,128)(2,1)}, bf16[128,2048]{1,0:T(8,128)(2,1)S(1)}, u32[]{:S(2)}, u32[]{:S(2)}) collective-permute-start(bf16[128,2048]{1,0:T(8,128)(2,1)} %get-tuple-element.286), channel_id=1, source_target_pairs={{2,0},{4,2},{6,4},{7,6},{5,7},{3,5},{1,3},{0,1},{10,8},{12,10},{14... | collective-permute-start | bytes 1572872 | tf_op jit(solution)/shard_map/ppermute | solution.py:495
  400.1 19.5 %collective-permute-start.26 = (bf16[256,2048]{1,0:T(8,128)(2,1)S(1)}, bf16[256,2048]{1,0:T(8,128)(2,1)S(1)}, u32[]{:S(2)}, u32[]{:S(2)}) collective-permute-start(bf16[256,2048]{1,0:T(8,128)(2,1)S(1)} %add_convert_fusion.16), channel_id=1, source_target_pairs={{0,2},{2,4},{4,6},{6,7},{7,5},{5,3},{3,1},{1,0},{8,10},{10,12},{12... | collective-permute-start | bytes 3145736 | tf_op jit(solution)/shard_map/ppermute | solution.py:492
  401.8 20.0 %collective-permute-start.27 = (bf16[256,2048]{1,0:T(8,128)(2,1)S(1)}, bf16[256,2048]{1,0:T(8,128)(2,1)S(1)}, u32[]{:S(2)}, u32[]{:S(2)}) collective-permute-start(bf16[256,2048]{1,0:T(8,128)(2,1)S(1)} %add_convert_fusion.15), channel_id=1, source_target_pairs={{2,0},{4,2},{6,4},{7,6},{5,7},{3,5},{1,3},{0,1},{10,8},{12,10},{14... | collective-permute-start | bytes 3145736 | tf_op jit(solution)/shard_map/ppermute | solution.py:495
  425.2 18.2 %collective-permute-start.29 = (bf16[256,2048]{1,0:T(8,128)(2,1)}, bf16[256,2048]{1,0:T(8,128)(2,1)}, u32[]{:S(2)}, u32[]{:S(2)}) collective-permute-start(bf16[256,2048]{1,0:T(8,128)(2,1)} %add_convert_fusion.13), channel_id=1, source_target_pairs={{2,0},{4,2},{6,4},{7,6},{5,7},{3,5},{1,3},{0,1},{10,8},{12,10},{14... | collective-permute-start | bytes 3145736 | tf_op jit(solution)/shard_map/ppermute | solution.py:495
  447.8 18.9 %collective-permute-start.30 = (bf16[256,2048]{1,0:T(8,128)(2,1)S(1)}, bf16[256,2048]{1,0:T(8,128)(2,1)}, u32[]{:S(2)}, u32[]{:S(2)}) collective-permute-start(bf16[256,2048]{1,0:T(8,128)(2,1)S(1)} %add_convert_fusion.12), channel_id=1, source_target_pairs={{0,2},{2,4},{4,6},{6,7},{7,5},{5,3},{3,1},{1,0},{8,10},{10,12},{12... | collective-permute-start | bytes 3145736 | tf_op jit(solution)/shard_map/ppermute | solution.py:492
  448.8 19.9 %collective-permute-start.31 = (bf16[256,2048]{1,0:T(8,128)(2,1)}, bf16[256,2048]{1,0:T(8,128)(2,1)}, u32[]{:S(2)}, u32[]{:S(2)}) collective-permute-start(bf16[256,2048]{1,0:T(8,128)(2,1)} %add_convert_fusion.11), channel_id=1, source_target_pairs={{2,0},{4,2},{6,4},{7,6},{5,7},{3,5},{1,3},{0,1},{10,8},{12,10},{14... | collective-permute-start | bytes 3145736 | tf_op jit(solution)/shard_map/ppermute | solution.py:495
  488.3 22.6 %all-to-all-start.1 = ((bf16[256,8,256]{2,0,1:T(8,128)(2,1)}), bf16[256,8,256]{2,0,1:T(8,128)(2,1)S(1)}, u32[]{:S(2)}, u32[]{:S(2)}) async-start(bf16[256,8,256]{2,0,1:T(8,128)(2,1)} %bitcast.53), calls=%async_computation.1 | async-start | bytes 2097152 | tf_op jit(solution)/shard_map/all_to_all | solution.py:714
  491.9 90.9 %reduce-scatter.8.cloned.1.call-start = ((), (), s32[]{:S(2)}) async-start(), calls=%async_computation.12 | async-start | bytes 10485760 | tf_op jit(solution)/shard_map/reduce_scatter | solution.py:596
  512.0 120.0 %reduce-scatter.10.cloned.1.call-start = ((), (), s32[]{:S(2)}) async-start(), calls=%async_computation.13 | async-start | bytes 5242880 | tf_op jit(solution)/shard_map/reduce_scatter | solution.py:596
  516.9 30.5 %collective-permute-start.34 = (bf16[256,2048]{1,0:T(8,128)(2,1)}, bf16[256,2048]{1,0:T(8,128)(2,1)}, u32[]{:S(2)}, u32[]{:S(2)}) collective-permute-start(bf16[256,2048]{1,0:T(8,128)(2,1)} %add_convert_fusion.10), channel_id=1, source_target_pairs={{0,2},{2,4},{4,6},{6,7},{7,5},{5,3},{3,1},{1,0},{8,10},{10,12},{12... | collective-permute-start | bytes 3145736 | tf_op jit(solution)/shard_map/ppermute | solution.py:492
  516.9 30.5 %collective-permute-start.35 = (bf16[256,2048]{1,0:T(8,128)(2,1)}, bf16[256,2048]{1,0:T(8,128)(2,1)}, u32[]{:S(2)}, u32[]{:S(2)}) collective-permute-start(bf16[256,2048]{1,0:T(8,128)(2,1)} %add_convert_fusion.9), channel_id=1, source_target_pairs={{2,0},{4,2},{6,4},{7,6},{5,7},{3,5},{1,3},{0,1},{10,8},{12,10},{14... | collective-permute-start | bytes 3145736 | tf_op jit(solution)/shard_map/ppermute | solution.py:495
  588.3 114.9 %reduce-scatter.12.cloned.1.call-start = ((), (), s32[]{:S(2)}) async-start(), calls=%async_computation.14 | async-start | bytes 5242880 | tf_op jit(solution)/shard_map/reduce_scatter | solution.py:596
  593.5 27.1 %collective-permute-start.40 = (bf16[256,2304]{1,0:T(8,128)(2,1)S(1)}, bf16[256,2304]{1,0:T(8,128)(2,1)}, u32[]{:S(2)}, u32[]{:S(2)}) collective-permute-start(bf16[256,2304]{1,0:T(8,128)(2,1)S(1)} %copy-done.29), channel_id=1, source_target_pairs={{0,2},{2,4},{4,6},{6,7},{7,5},{5,3},{3,1},{1,0},{8,10},{10,12},{12... | collective-permute-start | bytes 3538952 | tf_op jit(solution)/shard_map/ppermute | solution.py:492
  595.3 26.4 %collective-permute-start.41 = (bf16[256,2304]{1,0:T(8,128)(2,1)S(1)}, bf16[256,2304]{1,0:T(8,128)(2,1)S(1)}, u32[]{:S(2)}, u32[]{:S(2)}) collective-permute-start(bf16[256,2304]{1,0:T(8,128)(2,1)S(1)} %copy-done.26), channel_id=1, source_target_pairs={{2,0},{4,2},{6,4},{7,6},{5,7},{3,5},{1,3},{0,1},{10,8},{12,10},{14... | collective-permute-start | bytes 3538952 | tf_op jit(solution)/shard_map/ppermute | solution.py:495
  632.0 129.7 %reduce-scatter.14.cloned.1.call-start = ((), (), s32[]{:S(2)}) async-start(), calls=%async_computation.15 | async-start | bytes 3932160 | tf_op jit(solution)/shard_map/reduce_scatter | solution.py:596
  636.6 30.5 %collective-permute-start.42 = (bf16[256,2560]{1,0:T(8,128)(2,1)S(1)}, bf16[256,2560]{1,0:T(8,128)(2,1)S(1)}, u32[]{:S(2)}, u32[]{:S(2)}) collective-permute-start(bf16[256,2560]{1,0:T(8,128)(2,1)S(1)} %pad_maximum_fusion.1), channel_id=1, source_target_pairs={{0,2},{2,4},{4,6},{6,7},{7,5},{5,3},{3,1},{1,0},{8,10},{10,12},{12... | collective-permute-start | bytes 3932168 | tf_op jit(solution)/shard_map/ppermute | solution.py:492
  638.1 30.2 %collective-permute-start.43 = (bf16[256,2560]{1,0:T(8,128)(2,1)S(1)}, bf16[256,2560]{1,0:T(8,128)(2,1)S(1)}, u32[]{:S(2)}, u32[]{:S(2)}) collective-permute-start(bf16[256,2560]{1,0:T(8,128)(2,1)S(1)} %pad_maximum_fusion.2), channel_id=1, source_target_pairs={{2,0},{4,2},{6,4},{7,6},{5,7},{3,5},{1,3},{0,1},{10,8},{12,10},{14... | collective-permute-start | bytes 3932168 | tf_op jit(solution)/shard_map/ppermute | solution.py:495
  669.8 29.5 %collective-permute-start.44 = (bf16[256,2560]{1,0:T(8,128)(2,1)S(1)}, bf16[256,2560]{1,0:T(8,128)(2,1)S(1)}, u32[]{:S(2)}, u32[]{:S(2)}) collective-permute-start(bf16[256,2560]{1,0:T(8,128)(2,1)S(1)} %pad_maximum_fusion.3), channel_id=1, source_target_pairs={{0,2},{2,4},{4,6},{6,7},{7,5},{5,3},{3,1},{1,0},{8,10},{10,12},{12... | collective-permute-start | bytes 3932168 | tf_op jit(solution)/shard_map/ppermute | solution.py:492
  671.3 29.1 %collective-permute-start.45 = (bf16[256,2560]{1,0:T(8,128)(2,1)S(1)}, bf16[256,2560]{1,0:T(8,128)(2,1)S(1)}, u32[]{:S(2)}, u32[]{:S(2)}) collective-permute-start(bf16[256,2560]{1,0:T(8,128)(2,1)S(1)} %pad_maximum_fusion.4), channel_id=1, source_target_pairs={{2,0},{4,2},{6,4},{7,6},{5,7},{3,5},{1,3},{0,1},{10,8},{12,10},{14... | collective-permute-start | bytes 3932168 | tf_op jit(solution)/shard_map/ppermute | solution.py:495
  709.1 45.8 %collective-permute-start.46 = (bf16[256,2560]{1,0:T(8,128)(2,1)}, bf16[256,2560]{1,0:T(8,128)(2,1)S(1)}, u32[]{:S(2)}, u32[]{:S(2)}) collective-permute-start(bf16[256,2560]{1,0:T(8,128)(2,1)} %pad_maximum_fusion.5), channel_id=1, source_target_pairs={{0,2},{2,4},{4,6},{6,7},{7,5},{5,3},{3,1},{1,0},{8,10},{10,12},{12... | collective-permute-start | bytes 3932168 | tf_op jit(solution)/shard_map/ppermute | solution.py:492
  710.6 44.4 %collective-permute-start.47 = (bf16[256,2560]{1,0:T(8,128)(2,1)}, bf16[256,2560]{1,0:T(8,128)(2,1)S(1)}, u32[]{:S(2)}, u32[]{:S(2)}) collective-permute-start(bf16[256,2560]{1,0:T(8,128)(2,1)} %pad_maximum_fusion.6), channel_id=1, source_target_pairs={{2,0},{4,2},{6,4},{7,6},{5,7},{3,5},{1,3},{0,1},{10,8},{12,10},{14... | collective-permute-start | bytes 3932168 | tf_op jit(solution)/shard_map/ppermute | solution.py:495
  715.2 25.8 %collective-permute-start.51 = (f32[4112]{0:T(1024)S(1)}, f32[4112]{0:T(1024)S(1)}, u32[]{:S(2)}, u32[]{:S(2)}) collective-permute-start(f32[4112]{0:T(1024)S(1)} %add_add_fusion.1), channel_id=1, source_target_pairs={{0,1},{1,0},{2,3},{3,2},{4,5},{5,4},{6,7},{7,6},{8,9},{9,8},{10,11... | collective-permute-start | bytes 49352 | tf_op jit(solution)/shard_map/ppermute | solution.py:579
  715.9 26.5 %collective-permute-start.52 = (f32[4112]{0:T(1024)S(1)}, f32[4112]{0:T(1024)S(1)}, u32[]{:S(2)}, u32[]{:S(2)}) collective-permute-start(f32[4112]{0:T(1024)S(1)} %add_add_fusion.1), channel_id=1, source_target_pairs={{0,2},{1,3},{2,0},{3,1},{4,6},{5,7},{6,4},{7,5},{8,10},{9,11},{10,... | collective-permute-start | bytes 49352 | tf_op jit(solution)/shard_map/ppermute | solution.py:579
  717.2 28.0 %collective-permute-start.53 = (f32[4112]{0:T(1024)S(1)}, f32[4112]{0:T(1024)S(1)}, u32[]{:S(2)}, u32[]{:S(2)}) collective-permute-start(f32[4112]{0:T(1024)S(1)} %add_add_fusion.1), channel_id=1, source_target_pairs={{0,3},{1,2},{2,1},{3,0},{4,7},{5,6},{6,5},{7,4},{8,11},{9,10},{10,... | collective-permute-start | bytes 49352 | tf_op jit(solution)/shard_map/ppermute | solution.py:579
  (85 other events, 1040.3 us)
Sparse Core Ops, SparseCore 0:
  10.2 31.2 all-gather.4
  46.5 59.2 all-gather.6
  141.5 56.8 all-gather.8
  199.8 34.4 all-gather.10
  443.5 41.1 reduce-scatter.5
  512.1 70.6 reduce-scatter.7
  588.4 43.5 reduce-scatter.9
  635.2 44.4 reduce-scatter.11
  703.3 36.7 reduce-scatter.13

commit v3 on v2

--- a/solution.py
+++ b/solution.py
@@ -341,15 +341,42 @@
 
 def project_kernel(*refs, count):
     pieces, weight = refs[:count], refs[count]
-    normed_all, proj_all = refs[-2:]
-    rows, width = pieces[0].shape[0], normed_all.shape[1]
+    normed_all, extra_all, proj_all = refs[-3:]
+    width = normed_all.shape[1]
 
     @pl.when(pl.program_id(0) == 0)
     def _():
-        for place, piece in enumerate(pieces):
-            normed_all[place * rows : (place + 1) * rows, :] = piece[:, :width]
+        begin = 0
+        for piece in pieces:
+            here = slice(begin, begin + piece.shape[0])
+            normed_all[here, :] = piece[:, :width]
+            extra_all[here, :] = piece[:, width:]
+            begin += piece.shape[0]
 
     proj_all[...] = low(dot_nn(normed_all[...], weight[...]))
+
+
+def widen_kernel(*refs):
+    out, parts = refs[-1], refs[:-1]
+    columns = out.shape[2]
+    place = 0
+    for part in parts:
+        for begin in range(0, part.shape[1], columns):
+            out[:, place, :] = part[:, begin : begin + columns].astype(jnp.float32)
+            place += 1
+
+
+def widen(parts, shape):
+    rows = shape[0]
+    tall = min(rows, 128)
+    return pl.pallas_call(
+        widen_kernel,
+        grid=(rows // tall,),
+        out_shape=jax.ShapeDtypeStruct(shape, jnp.float32),
+        in_specs=[pl.BlockSpec((tall, part.shape[1]), lambda i: (i, 0)) for part in parts],
+        out_specs=pl.BlockSpec((tall, *shape[1:]), lambda i: (i, 0, 0)),
+        cost_estimate=NO_COST,
+    )(*parts)
 
 
 def feed_kernel(*refs, count):
@@ -403,23 +430,25 @@
 
 
 def project_blocks(pieces, weight, place, length, before):
-    rows, both = pieces[0].shape
+    both = pieces[0].shape[1]
     width, wide = weight.shape
     count = len(pieces)
-    tall = rows * count
+    tall = sum(piece.shape[0] for piece in pieces)
     tile = 256 if wide % 256 == 0 else 128
     return pl.pallas_call(
         functools.partial(project_kernel, count=count),
         grid=(wide // tile,),
         out_shape=[
             jax.ShapeDtypeStruct((length, width), jnp.bfloat16),
+            jax.ShapeDtypeStruct((length, both - width), jnp.bfloat16),
             jax.ShapeDtypeStruct((length, wide), jnp.bfloat16),
         ],
-        in_specs=[pl.BlockSpec((rows, both), lambda j: (0, 0))] * count
+        in_specs=[pl.BlockSpec(piece.shape, lambda j: (0, 0)) for piece in pieces]
         + [pl.BlockSpec((width, tile), lambda j: (0, j))]
         + [ANY] * len(before),
         out_specs=[
             pl.BlockSpec((tall, width), lambda j: (place, 0)),
+            pl.BlockSpec((tall, both - width), lambda j: (place, 0)),
             pl.BlockSpec((tall, tile), lambda j: (place, j)),
         ],
         input_output_aliases={count + 1 + i: i for i in range(len(before))},
@@ -521,13 +550,15 @@
         self.axis = axis
         self.step = ring.count // 2
         self.sent = self.moved = self.rider = self.parts = None
+        self.begin = 0
+        self.fresh = True
 
     def messages(self, *earlier):
         half, step = self.ring.count // 2, self.step
         self.step -= 1
         if step == half:
             return after(tuple(self.partial(half)), *earlier)
-        forward, backward = (part.astype(jnp.float32) for part in after(self.moved, *earlier))
+        forward, backward = self.came(*earlier)
         if step == half - 1:
             extra = forward.shape[self.axis]
             forward = jnp.pad(forward, [(0, extra if axis == self.axis else 0) for axis in (0, 1)])
@@ -540,8 +571,15 @@
     def compute(self, *earlier):
         self.parts = after((low(self.partial(self.step)), low(self.partial(self.ring.count - self.step))), *earlier)
 
+    def came(self, *earlier):
+        width = self.partial(0).shape[1]
+        return [
+            part[:, self.begin : self.begin + width].astype(jnp.float32) for part in after(self.moved, *earlier)
+        ]
+
     def prepare(self, *earlier, rider=None):
         self.sent = self.messages(*earlier)
+        self.fresh = False
         self.rider = rider
         if rider is not None:
             self.sent = tuple(
@@ -550,23 +588,21 @@
         self.sent = after(self.sent)
 
     def hop(self, *earlier):
-        if self.sent is None:
+        if self.fresh:
             self.prepare()
-        forward, backward = after(self.sent, *earlier)
+        self.fresh = True
+        forward, backward = self.sent = after(self.sent, *earlier)
         self.moved = (self.ring.forth(forward), self.ring.back(backward))
-        self.sent = None
 
     def hold(self, *others):
         self.moved = after(self.moved, *others)
         if self.rider is not None:
-            width = self.partial(0).shape[1]
-            self.rider.moved = tuple(part[:, width:] for part in self.moved)
-            self.moved = tuple(part[:, :width] for part in self.moved)
+            self.rider.moved, self.rider.begin = self.moved, self.partial(0).shape[1]
             self.rider = None
 
     def total(self):
-        own = self.partial(0).astype(jnp.float32)
-        return own + self.moved[0].astype(jnp.float32) + self.moved[1].astype(jnp.float32)
+        forward, backward = self.came()
+        return self.partial(0).astype(jnp.float32) + forward + backward
 
 
 def after(values, *earlier):
@@ -581,6 +617,11 @@
     while len(terms) > 1:
         terms = [left + right for left, right in zip(terms[::2], terms[1::2])]
     return terms[0]
+
+
+def swap_sum(values, axis, step, *earlier):
+    size = lax.axis_size(axis)
+    return values + after(lax.ppermute(values, axis, [(i, i ^ step) for i in range(size)]), *earlier)
 
 
 def rms_parts(values):
@@ -631,27 +672,18 @@
         ring, jnp.concatenate([low(unit_first * gain_attention), attention_out.reshape(rows, -1)], axis=1)
     )
 
-    def project(step, kept, *earlier):
-        return project_blocks(
-            after(gather_a.groups[step], *earlier), w_in, gather_a.place(step), length, kept
-        )
-
     gather_a.hop()
     f_in = whole(after(feed_in, w_in, gather_a.groups[1]).reshape(feed_in.shape[0], -1), 0)
-    gather_a.hop()
-    kept = project(0, [], gather_a.groups[2])
-    for step in range(3, half + 1):
-        gather_a.hop(*([kept[1]] if step > 3 else []))
-        kept = project(step - 2, kept)
-    kept = project(half - 1, kept)
-    gather_a.groups[half] = after(gather_a.groups[half], kept[1])
-    normed_a, proj = project(half, kept)
-    w_out_rows = jnp.zeros((length, gather_a.groups[0][0].shape[1] - width), jnp.bfloat16)
-    for step, group in enumerate(gather_a.groups):
-        for piece, d, begin in zip(group, (-step % count, step), (0, rows // 2 if step == half else 0)):
-            start = ring.ahead_index[d] * rows + begin
-            w_out_rows = lax.dynamic_update_slice_in_dim(w_out_rows, piece[:, width:], start, 0)
-    w_out = whole(after(w_out_rows.reshape(-1, attention_out.shape[1]), f_in), 1)
+    kept = []
+    for step in range(2, half + 1):
+        gather_a.hop(*kept[2:3])
+        if step > 2:
+            kept = project_blocks(gather_a.groups[step - 2], w_in, step - 2, length, kept)
+    kept = project_blocks(gather_a.groups[half - 1], w_in, half - 1, length, kept)
+    gather_a.groups[half] = after(gather_a.groups[half], kept[2])
+    normed_a, extra, proj = project_blocks(gather_a.groups[0] + gather_a.groups[half], w_in, 0, length, kept)
+    extra = extra.reshape(count, *attention_out.shape)[ring.order].reshape(-1, attention_out.shape[1])
+    w_out = whole(after(extra, f_in), 1)
 
     gather_c = Gather(ring, after(cotangent, gather_a.groups[half]))
     gather_c.hop()
@@ -691,29 +723,34 @@
     normed_f, cot, hidden, gate_grad, up_grad = kept
 
     scatter_f = Scatter(ring, lambda d: normed_f_part[d])
-    for _ in range(half - 2):
+    scatter_r = Scatter(ring, lambda d: result_part[d])
+    scatter_f.hop()
+    scatter_r.hop(scatter_f.sent)
+    scatter_f.hop(scatter_r.moved)
+    for _ in range(half - 4):
         scatter_f.hop()
-    feed_out_local = low(dot_tn(hidden, after(cot, scatter_f.moved)))
-    scatter_f.hop()
+    feed_out_local = low(dot_tn(hidden, after(cot, scatter_f.sent)))
     scatter_f.hold(feed_out_local)
-    feed_gate_local = low(dot_tn(normed_f, after(gate_grad, scatter_f.moved)))
     feed_out_grad = sum_over_seq(after(feed_out_local, scatter_f.moved), 1)
     scatter_f.hop()
+    feed_gate_local = low(dot_tn(normed_f, after(gate_grad, scatter_f.sent)))
     scatter_f.hold(feed_gate_local)
+    scatter_f.hop()
+    feed_up_local = low(dot_tn(normed_f, after(up_grad, scatter_f.sent)))
+    scatter_f.hold(feed_up_local)
     normed_f_grad = scatter_f.total()
-    feed_up_local = low(dot_tn(normed_f, after(up_grad, normed_f_grad)))
-    scatter_r = Scatter(ring, lambda d: result_part[d])
-    scatter_r.hop(normed_f_grad)
+    feed_gate_grad = sum_over_seq(after(feed_gate_local, feed_out_grad, normed_f_grad), 0)
+    scatter_r.prepare()
     gain_feed_part = jnp.sum(normed_f_grad * unit_second, axis=0)
     middle_grad = cotangent.astype(jnp.float32) + rms_back(
         normed_f_grad * gain_feed, unit_second, scale_second
     )
     out_grad = low(middle_grad)
-    combined_grad = after(low(dot_nt(out_grad, w_out)), scatter_r.moved)
-    attention_out_local = low(dot_tn(merged_mine, out_grad))
+    combined_grad = low(dot_nt(out_grad, w_out))
+    attention_out_local = low(dot_tn(merged_mine, after(out_grad, feed_up_local)))
     combined_grad = lax.all_to_all(combined_grad, "blk", 1, 0, tiled=True)
-    combined_grad = after(combined_grad, attention_out_local, feed_up_local)
-    out_sum = sum_over_seq(after(attention_out_local, feed_out_grad, combined_grad), 1)
+    combined_grad = after(combined_grad, attention_out_local, scatter_r.sent)
+    out_sum = sum_over_seq(after(attention_out_local, feed_gate_grad, combined_grad), 1)
     scatter_r.hop(combined_grad)
     proj_grad, gate_rows = attend_backward(
         ring.order, splits, mix, proj, combined_grad,
@@ -741,10 +778,12 @@
 
     scatter_a = Scatter(ring, normed_a_part)
     scatter_a.hop()
+    scatter_a.compute(scatter_a.sent)
+    scatter_a.hold(scatter_a.parts)
     scatter_a.hop()
-    scatter_r.prepare(proj_grad, rider=rider())
+    scatter_r.prepare(scatter_a.sent, rider=rider())
     scatter_a.hold(scatter_r.sent)
-    feed_gate_grad = sum_over_seq(after(feed_gate_local, out_sum, scatter_a.moved), 0)
+    feed_up_grad = sum_over_seq(after(feed_up_local, out_sum, scatter_a.moved), 0)
     scatter_r.hop(scatter_a.moved)
     attention_in_local = low(dot_tn(normed_a, after(proj_grad, scatter_a.moved)))
     gain_attention_part = jnp.sum(attention_in_local.astype(jnp.float32) * w_in.astype(jnp.float32), axis=1) / gain_attention
@@ -753,26 +792,34 @@
         jnp.zeros(gate_logit.shape, jnp.float32), gate_part, head_first, 0
     )
     sums = jnp.concatenate([gain_attention_part, gain_feed_part, gate_full])
-    scatter_a.compute()
-    scatter_r.hold(scatter_a.parts, attention_in_local)
-    feed_up_grad = sum_over_seq(after(feed_up_local, feed_gate_grad, scatter_r.moved), 0)
+    scatter_a.compute(scatter_a.moved)
+    sums = sum_axis(sums, "seq")
+    scatter_r.hold(scatter_a.parts, attention_in_local, sums)
+    swaps = [1 << bit for bit in range(count.bit_length() - 1)]
     while scatter_a.step > 1:
         scatter_a.prepare(rider=rider())
         scatter_a.hop(scatter_r.moved)
-        scatter_a.hold()
+        if swaps:
+            sums = swap_sum(after(sums, scatter_a.sent), "blk", swaps.pop())
+        scatter_a.hold(sums)
         scatter_r.prepare(rider=rider())
         scatter_r.hop(scatter_a.moved)
-        scatter_a.compute()
-        scatter_r.hold(scatter_a.parts)
+        scatter_a.compute(scatter_r.sent)
+        if swaps:
+            sums = swap_sum(after(sums, scatter_r.sent), "blk", swaps.pop())
+        scatter_r.hold(scatter_a.parts, sums)
     scatter_a.prepare(rider=rider())
     attention_in_grad = sum_over_seq(after(attention_in_local, feed_up_grad, scatter_a.sent), 0)
-    sums = sum_axis(after(sums, scatter_a.sent), "seq")
     scatter_a.hop()
-    result = low(middle + scatter_r.total())
-    feed_in_grad = jnp.stack([feed_gate_grad, feed_up_grad], axis=1).astype(jnp.float32)
+    sums = after(sums, scatter_a.sent)
+    while len(swaps) > 1:
+        sums = swap_sum(sums, "blk", swaps.pop())
+    feed_in_grad = widen(after((feed_gate_grad, feed_up_grad), scatter_a.sent), feed_in.shape)
+    result, feed_out_grad = after((low(middle + scatter_r.total()), feed_out_grad), scatter_a.sent)
     feed_out_grad = feed_out_grad.astype(jnp.float32)
-    sums = sum_axis(after(sums, result, feed_in_grad, feed_out_grad), "blk")
-    attention_in_grad = attention_in_grad.astype(jnp.float32).reshape(attention_in.shape)
+    attention_in_grad = widen((attention_in_grad,), attention_in.shape)
+    while swaps:
+        sums = swap_sum(sums, "blk", swaps.pop(), result, feed_in_grad, feed_out_grad, attention_in_grad)
     scatter_a.hold(sums)
     attention_out_grad = scatter_o.total().reshape(attention_out.shape)
     normed_a_grad = scatter_a.total()

time: 782 us -> 762 us (0.974)
  other arithmetic: 47.2 us -> 62.4 us
  local copies, waits for them, and re-layouts: 48.2 us -> 36.9 us
    ppermute x24, waiting for transfers between devices: 224 us -> 155 us  [forth(): return lax.ppermute(values, 'blk', self.ahead)]
    ppermute x0 -> x3, waiting for transfers between devices: none -> 56.3 us  [swap_sum(): lax.ppermute(values, axis, [(i, i ^ step) for i in range(size)])]
    ppermute x10 -> x3, waiting for transfers between devices: 23.7 us -> 0.01 us  [sum_axis(): lax.ppermute(values, axis, [(i, i ^ step) for i in range(size)])]
    reduce_scatter x5, waiting for transfers between devices: 12.3 us -> 33.1 us  [sum_over_seq(): lax.psum_scatter(low(values), 'seq', scatter_dimension=dimension, tiled=T...]
    convert_element_type x20 -> x23, other arithmetic: 27.8 us -> 40.2 us  [low(): return values.astype(jnp.bfloat16)]
    ppermute x10 -> x3, starting transfers between devices: 12.2 us -> 1.93 us  [sum_axis(): lax.ppermute(values, axis, [(i, i ^ step) for i in range(size)])]
    pallas_call x0 -> x2, Pallas kernels: none -> 8.15 us  [widen(): pl.pallas_call(widen_kernel, grid=(rows // tall,), out_shape=jax.ShapeDty...]
    pallas_call x5 -> x4, Pallas kernels: 26.7 us -> 23.5 us  [project_blocks(): pl.pallas_call(functools.partial(project_kernel, count=count), grid=(wide...]
  transfers between devices with their start and end apart: 68 -> 64, of which waited for: 38 -> 38; matrix products, arithmetic and copies ran while one was open for 21% -> 22% of each run, Pallas kernels for 21% -> 21%
where the time goes in v3:
time: 762 us; the launch traced here: 752 us
  waiting for transfers between devices  286 us (38%)
  Pallas kernels  172 us (23%)
  matrix products  88.6 us (12%)
  other arithmetic  62.4 us (8%)
  starting transfers between devices  61.5 us (8%)
  local copies, waits for them, and re-layouts  36.9 us (5%)
  blocking collectives  24 us (3%)
  between operations  21.2 us (3%)
    ppermute x24, waiting for transfers between devices, forth(): return lax.ppermute(values, 'blk', self.ahead)  155 us
    pallas_call x5, Pallas kernels, feed_blocks(): pl.pallas_call(functools.partial(feed_kernel, count=count), grid=(tiles,)...  104 us
    dot_general x5, matrix products, dot_tn(): lax.dot_general(left, right, (((0,), (0,)), ((), ())), preferred_element_...  56.4 us
    ppermute x3, waiting for transfers between devices, swap_sum(): lax.ppermute(values, axis, [(i, i ^ step) for i in range(size)])  56.3 us
    convert_element_type x23, other arithmetic, low(): return values.astype(jnp.bfloat16)  40.2 us
    ppermute x24, starting transfers between devices, forth(): return lax.ppermute(values, 'blk', self.ahead)  36.6 us
    reduce_scatter x5, waiting for transfers between devices, sum_over_seq(): lax.psum_scatter(low(values), 'seq', scatter_dimension=dimension, tiled=T...  33.1 us
    dot_general x10, matrix products, dot_nt(): lax.dot_general(left, right, (((1,), (1,)), ((), ())), preferred_element_...  26 us
  transfers between devices with their start and end apart: 64, of which 38 were waited for; matrix products, arithmetic and copies ran while one was open for 22% of the time, Pallas kernels for 21%

profile of v3, /device:TPU:0, one launch (start us, length us, event | category | flops | bytes accessed | tf_op | source)
XLA Modules:
  0.0 751.9 jit_solution(10549325208837024247)
XLA Ops:
  11.3 3.1 collective-permute-start
  14.4 28.7 %collective-permute-done.refs_0_ = bf16[256,2560]{1,0:T(8,128)(2,1)S(1)} collective-permute-done((bf16[256,2560]{1,0:T(8,128)(2,1)S(1)}, bf16[256,2560]{1,0:T(8,128)(2,1)S(1)}, u32[]{:S(2)}, u32[]{:S(2)}) %collective-permute-start) | collective-permute-done | bytes 1310752 | tf_op jit(solution)/shard_map/ppermute | solution.py:521
  44.7 3.5 copy.67
  51.6 27.6 %collective-permute-done.2.refs_0_ = bf16[256,2560]{1,0:T(8,128)(2,1)} collective-permute-done((bf16[256,2560]{1,0:T(8,128)(2,1)S(1)}, bf16[256,2560]{1,0:T(8,128)(2,1)}, u32[]{:S(2)}, u32[]{:S(2)}) %collective-permute-start.2) | collective-permute-done | bytes 1310752 | tf_op jit(solution)/shard_map/ppermute | solution.py:521
  84.6 5.9 shard_map.230
  90.5 18.5 %collective-permute-done.4.refs_0_ = bf16[256,2560]{1,0:T(8,128)(2,1)S(1)} collective-permute-done((bf16[256,2560]{1,0:T(8,128)(2,1)}, bf16[256,2560]{1,0:T(8,128)(2,1)S(1)}, u32[]{:S(2)}, u32[]{:S(2)}) %collective-permute-start.4) | collective-permute-done | bytes 1310752 | tf_op jit(solution)/shard_map/ppermute | solution.py:521
  115.3 5.9 shard_map.231
  121.2 5.9 shard_map.232
  128.3 5.9 shard_map.233
  134.2 3.6 gather_fusion.1
  142.3 15.3 %shard_map.234 = (bf16[2048,256]{1,0:T(8,128)(2,1)}, f32[2048,256]{1,0:T(8,128)}, f32[4,2,512]{2,1,0:T(2,128)}, f32[2,2,128,128]{3,2,1,0:T(8,128)}, f32[2,2,128]...) custom-call(s32[8]{0:T(128)} %copy-done.65, s32[1]{0:T(128)} %bitcast.59.splits, f32[2]{0:T(128)} %add_divide_fusion.mix, ...), custom_call_target="tpu_custom_call" | custom-call | flops 4000000000 | bytes 4096 | tf_op jit(solution)/shard_map/pallas_call | solution.py:301
  162.8 24.0 %all_to_all.38 = bf16[8,256,256]{1,2,0:T(8,128)(2,1)} all-to-all(bf16[8,256,256]{1,2,0:T(8,128)(2,1)S(1)} %copy.61), channel_id=1, replica_groups=mesh['seq'=4,'blk'=8] {'blk'}, dimensions={0} | all-to-all | bytes 2097152 | tf_op jit(solution)/shard_map/all_to_all | solution.py:693
  186.7 8.6 %all-gather.9.cloned.1.call-done = bf16[2048,2048]{1,0:T(8,128)(2,1)} async-done(((bf16[2048,512]{1,0:T(8,128)(2,1)}), bf16[2048,2048]{1,0:T(8,128)(2,1)}) %all-gather.9.cloned.1.call-update) | async-done | bytes 8388624 | tf_op jit(solution)/shard_map/all_gather | solution.py:663
  197.7 6.2 multiply_reduce_fusion.3
  204.2 17.0 %collective-permute-done.10.refs_2_ = bf16[256,2048]{1,0:T(8,128)(2,1)} collective-permute-done((bf16[256,2048]{1,0:T(8,128)(2,1)}, bf16[256,2048]{1,0:T(8,128)(2,1)}, u32[]{:S(2)}, u32[]{:S(2)}) %collective-permute-start.10) | collective-permute-done | bytes 1048608 | tf_op jit(solution)/shard_map/ppermute | solution.py:521
  224.6 22.2 %collective-permute-done.12.refs_0_ = bf16[256,2048]{1,0:T(8,128)(2,1)S(1)} collective-permute-done((bf16[256,2048]{1,0:T(8,128)(2,1)S(1)}, bf16[256,2048]{1,0:T(8,128)(2,1)S(1)}, u32[]{:S(2)}, u32[]{:S(2)}) %collective-permute-start.12) | collective-permute-done | bytes 1048608 | tf_op jit(solution)/shard_map/ppermute | solution.py:521
  250.0 14.6 %shard_map.235 = (bf16[2048,2048]{1,0:T(8,128)(2,1)}, bf16[2048,2048]{1,0:T(8,128)(2,1)}, bf16[2048,1024]{1,0:T(8,128)(2,1)}, bf16[2048,1024]{1,0:T(8,128)(2,1)}...) custom-call(bf16[256,2048]{1,0:T(8,128)(2,1)} %copy-done.17, ...), custom_call_target="tpu_custom_call" | custom-call | flops 4000000000 | bytes 4096 | tf_op jit(solution)/shard_map/pallas_call | solution.py:469
  264.6 6.7 collective-permute-done.14.refs_2_
  274.6 24.8 %shard_map.236 = (bf16[2048,2048]{1,0:T(8,128)(2,1)}, bf16[2048,2048]{1,0:T(8,128)(2,1)}, bf16[2048,1024]{1,0:T(8,128)(2,1)}, bf16[2048,1024]{1,0:T(8,128)(2,1)}...) custom-call(bf16[256,2048]{1,0:T(8,128)(2,1)} %copy-done.47, ...), custom_call_target="tpu_custom_call", output_to_operand_aliasing={{0}: (7, {}), {1}: (8, {}), {2}: (9, {}), {3}: (10, {}), {4... | custom-call | flops 4000000000 | bytes 4096 | tf_op jit(solution)/shard_map/pallas_call | solution.py:469
  304.1 6.9 collective-permute-done.18.refs_2_
  316.6 24.8 %shard_map.237 = (bf16[2048,2048]{1,0:T(8,128)(2,1)}, bf16[2048,2048]{1,0:T(8,128)(2,1)}, bf16[2048,1024]{1,0:T(8,128)(2,1)}, bf16[2048,1024]{1,0:T(8,128)(2,1)}...) custom-call(bf16[256,2048]{1,0:T(8,128)(2,1)} %copy-done.46, ...), custom_call_target="tpu_custom_call", output_to_operand_aliasing={{0}: (7, {}), {1}: (8, {}), {2}: (9, {}), {3}: (10, {}), {4... | custom-call | flops 4000000000 | bytes 4096 | tf_op jit(solution)/shard_map/pallas_call | solution.py:469
  344.7 6.0 collective-permute-done.22.refs_0_
  353.7 14.6 %shard_map.238 = (bf16[2048,2048]{1,0:T(8,128)(2,1)}, bf16[2048,2048]{1,0:T(8,128)(2,1)}, bf16[2048,1024]{1,0:T(8,128)(2,1)}, bf16[2048,1024]{1,0:T(8,128)(2,1)}...) custom-call(bf16[128,2048]{1,0:T(8,128)(2,1)} %copy-done.52, ...), custom_call_target="tpu_custom_call", output_to_operand_aliasing={{0}: (7, {}), {1}: (8, {}), {2}: (9, {}), {3}: (10, {}), {4... | custom-call | flops 4000000000 | bytes 4096 | tf_op jit(solution)/shard_map/pallas_call | solution.py:469
  372.5 24.9 %shard_map.239 = (bf16[2048,2048]{1,0:T(8,128)(2,1)}, bf16[2048,2048]{1,0:T(8,128)(2,1)}, bf16[2048,1024]{1,0:T(8,128)(2,1)}, bf16[2048,1024]{1,0:T(8,128)(2,1)}...) custom-call(bf16[256,2048]{1,0:T(8,128)(2,1)} %copy-done.23, ...), custom_call_target="tpu_custom_call", output_to_operand_aliasing={{0}: (7, {}), {1}: (8, {}), {2}: (9, {}), {3}: (10, {}), {4... | custom-call | flops 4000000000 | bytes 4096 | tf_op jit(solution)/shard_map/pallas_call | solution.py:469
  404.0 13.1 %convolution_convert_fusion.1 = bf16[1024,2048]{1,0:T(8,128)(2,1)} fusion(bf16[2048,1024]{1,0:T(8,128)(2,1)S(1)} %copy-done.6, bf16[2048,2048]{1,0:T(8,128)(2,1)} %get-tuple-element.309), kind=kOutput, calls=%fused_computation.5 | convolution fusion | flops 8592031744 | bytes 16777216 | tf_op jit(solution)/shard_map/dot_general | solution.py:29
  427.9 13.1 %convolution_convert_fusion.3 = bf16[2048,1024]{1,0:T(8,128)(2,1)} fusion(bf16[2048,2048]{1,0:T(8,128)(2,1)} %get-tuple-element.317, bf16[2048,1024]{1,0:T(8,128)(2,1)S(1)} %copy-done.7), kind=kOutput, calls=%fused_computation.7 | convolution fusion | flops 8592031744 | bytes 16777216 | tf_op jit(solution)/shard_map/dot_general | solution.py:29
  443.9 3.1 add_convert_fusion.11
  452.0 12.9 %convolution_convert_fusion.2 = bf16[2048,1024]{1,0:T(8,128)(2,1)} fusion(bf16[2048,2048]{1,0:T(8,128)(2,1)} %get-tuple-element.317, bf16[2048,1024]{1,0:T(8,128)(2,1)S(1)} %copy-done.8), kind=kOutput, calls=%fused_computation.6 | convolution fusion | flops 8592031744 | bytes 16777216 | tf_op jit(solution)/shard_map/dot_general | solution.py:29
  466.2 3.5 multiply_reduce_fusion.1
  473.3 7.4 convolution_convert_fusion.11
  481.8 3.7 all-to-all-start.1
  489.2 5.7 convolution_convert_fusion
  494.9 10.3 %all-to-all-done.1 = bf16[256,8,256]{2,0,1:T(8,128)(2,1)S(1)} async-done(((bf16[256,8,256]{2,0,1:T(8,128)(2,1)}), bf16[256,8,256]{2,0,1:T(8,128)(2,1)S(1)}, u32[]{:S(2)}, u32[]{:S(2)}) %all-to-all-start.1) | async-done | bytes 1048608 | tf_op jit(solution)/shard_map/all_to_all | solution.py:751
  505.2 6.4 reduce-scatter.8.cloned.1.call-done.refs_0_
  516.5 21.0 %shard_map.240 = (bf16[2048,768]{1,0:T(8,128)(2,1)}, f32[2,128]{1,0:T(2,128)}) custom-call(s32[8]{0:T(128)} %copy-done.65, s32[1]{0:T(128)} %bitcast.60.splits, f32[2]{0:T(128)} %add_divide_fusion.mix, bf16[2048,768]{1,0:T(8,128)(2,1)} %get-tuple-element.232.proj, bf16[2048,256]{1,0:T(8,128)(2,1)} %bitcast.68, f32[2048,256]{1,0:T(8,128)} %get-tuple-element.337.attended, ...), custom_call_target="tpu_custom_call" | custom-call | flops 4000000000 | bytes 4096 | tf_op jit(solution)/shard_map/pallas_call | solution.py:322
  548.5 6.4 collective-permute-done.36
  565.8 20.1 %reduce-scatter.10.cloned.1.call-done = bf16[2048,512]{1,0:T(8,128)(2,1)} async-done(((bf16[2048,2048]{1,0:T(8,128)(2,1)}), bf16[2048,512]{1,0:T(8,128)(2,1)}) %reduce-scatter.10.cloned.1.call-update) | async-done | bytes 2097168 | tf_op jit(solution)/shard_map/reduce_scatter | solution.py:637
  597.8 11.7 %multiply_reduce_fusion = (f32[2048]{0:T(1024)S(1)}, bf16[2048,768]{1,0:T(8,128)(2,1)}) fusion(bf16[2048,768]{1,0:T(8,128)(2,1)S(1)} %copy-done.2, bf16[2048,2048]{1,0:T(8,128)(2,1)} %get-tuple-element.369, bf16[2048,768]{1,0:T(8,128)(2,1)S(1)} %copy-done.57), kind=kOutput, calls=%fused_computation.4 | convolution fusion | flops 6450313216 | bytes 17833984 | tf_op jit(solution)/shard_map/dot_general | solution.py:29
  611.4 3.6 add_convert_fusion.4
  615.1 8.4 %collective-permute-done.40 = bf16[256,2304]{1,0:T(8,128)(2,1)S(1)} collective-permute-done((bf16[256,2304]{1,0:T(8,128)(2,1)S(1)}, bf16[256,2304]{1,0:T(8,128)(2,1)S(1)}, u32[]{:S(2)}, u32[]{:S(2)}) %collective-permute-start.40) | collective-permute-done | bytes 1179680 | tf_op jit(solution)/shard_map/ppermute | solution.py:521
  629.3 6.7 reduce-scatter.12.cloned.1.call-done.refs_1_
  650.4 22.8 %collective-permute-done.47 = f32[4112]{0:T(1024)S(1)} collective-permute-done((f32[4112]{0:T(1024)S(1)}, f32[4112]{0:T(1024)S(1)}, u32[]{:S(2)}, u32[]{:S(2)}) %collective-permute-start.47) | collective-permute-done | bytes 16480 | tf_op jit(solution)/shard_map/ppermute | solution.py:624
  683.3 21.8 %collective-permute-done.50 = f32[4112]{0:T(1024)S(1)} collective-permute-done((f32[4112]{0:T(1024)S(1)}, f32[4112]{0:T(1024)S(1)}, u32[]{:S(2)}, u32[]{:S(2)}) %collective-permute-start.50) | collective-permute-done | bytes 16480 | tf_op jit(solution)/shard_map/ppermute | solution.py:624
  713.1 4.4 shard_map.241
  717.6 3.7 shard_map.242
  721.3 3.1 copy.64
  724.4 11.7 %collective-permute-done.53 = f32[4112]{0:T(1024)S(1)} collective-permute-done((f32[4112]{0:T(1024)S(1)}, f32[4112]{0:T(1024)S(1)}, u32[]{:S(2)}, u32[]{:S(2)}) %collective-permute-start.53) | collective-permute-done | bytes 16480 | tf_op jit(solution)/shard_map/ppermute | solution.py:624
  737.3 3.1 fusion.6
  (336 shorter events, 178.1 us)
Async XLA Ops:
  7.2 37.5 %all-gather.5.cloned.1.call-start = ((), (), s32[]{:S(2)}) async-start(), calls=%async_computation.7 | async-start | bytes 3932160 | tf_op jit(solution)/shard_map/all_gather | solution.py:663
  9.9 127.8 %all-gather.7.cloned.1.call-start = ((), (), s32[]{:S(2)}) async-start(), calls=%async_computation.8 | async-start | bytes 10485760 | tf_op jit(solution)/shard_map/all_gather | solution.py:663
  11.3 31.8 %collective-permute-start = (bf16[256,2560]{1,0:T(8,128)(2,1)S(1)}, bf16[256,2560]{1,0:T(8,128)(2,1)S(1)}, u32[]{:S(2)}, u32[]{:S(2)}) collective-permute-start(bf16[256,2560]{1,0:T(8,128)(2,1)S(1)} %pad_maximum_fusion.refs_0_), channel_id=1, source_target_pairs={{0,2},{2,4},{4,6},{6,7},{7,5},{5,3},{3,1},{1,0},{8,10},{10,12},{12... | collective-permute-start | bytes 3932168 | tf_op jit(solution)/shard_map/ppermute | solution.py:521
  14.4 30.3 %collective-permute-start.1 = (bf16[256,2560]{1,0:T(8,128)(2,1)S(1)}, bf16[256,2560]{1,0:T(8,128)(2,1)}, u32[]{:S(2)}, u32[]{:S(2)}) collective-permute-start(bf16[256,2560]{1,0:T(8,128)(2,1)S(1)} %pad_maximum_fusion.refs_0_), channel_id=1, source_target_pairs={{2,0},{4,2},{6,4},{7,6},{5,7},{3,5},{1,3},{0,1},{10,8},{12,10},{14... | collective-permute-start | bytes 3932168 | tf_op jit(solution)/shard_map/ppermute | solution.py:524
  48.3 147.1 %all-gather.9.cloned.1.call-start = ((), (), s32[]{:S(2)}) async-start(), calls=%async_computation.9 | async-start | bytes 10485760 | tf_op jit(solution)/shard_map/all_gather | solution.py:663
  49.6 29.6 %collective-permute-start.2 = (bf16[256,2560]{1,0:T(8,128)(2,1)S(1)}, bf16[256,2560]{1,0:T(8,128)(2,1)}, u32[]{:S(2)}, u32[]{:S(2)}) collective-permute-start(bf16[256,2560]{1,0:T(8,128)(2,1)S(1)} %copy-done.67), channel_id=1, source_target_pairs={{0,2},{2,4},{4,6},{6,7},{7,5},{5,3},{3,1},{1,0},{8,10},{10,12},{12... | collective-permute-start | bytes 3932168 | tf_op jit(solution)/shard_map/ppermute | solution.py:521
  51.2 29.4 %collective-permute-start.3 = (bf16[256,2560]{1,0:T(8,128)(2,1)}, bf16[256,2560]{1,0:T(8,128)(2,1)}, u32[]{:S(2)}, u32[]{:S(2)}) collective-permute-start(bf16[256,2560]{1,0:T(8,128)(2,1)} %collective-permute-done.1.refs_1_), channel_id=1, source_target_pairs={{2,0},{4,2},{6,4},{7,6},{5,7},{3,5},{1,3},{0,1},{10,8},{12,10},{14... | collective-permute-start | bytes 3932168 | tf_op jit(solution)/shard_map/ppermute | solution.py:524
  80.6 28.4 %collective-permute-start.4 = (bf16[256,2560]{1,0:T(8,128)(2,1)}, bf16[256,2560]{1,0:T(8,128)(2,1)S(1)}, u32[]{:S(2)}, u32[]{:S(2)}) collective-permute-start(bf16[256,2560]{1,0:T(8,128)(2,1)} %collective-permute-done.2.refs_0_), channel_id=1, source_target_pairs={{0,2},{2,4},{4,6},{6,7},{7,5},{5,3},{3,1},{1,0},{8,10},{10,12},{12... | collective-permute-start | bytes 3932168 | tf_op jit(solution)/shard_map/ppermute | solution.py:521
  82.2 28.2 %collective-permute-start.5 = (bf16[256,2560]{1,0:T(8,128)(2,1)}, bf16[256,2560]{1,0:T(8,128)(2,1)}, u32[]{:S(2)}, u32[]{:S(2)}) collective-permute-start(bf16[256,2560]{1,0:T(8,128)(2,1)} %collective-permute-done.3.refs_1_), channel_id=1, source_target_pairs={{2,0},{4,2},{6,4},{7,6},{5,7},{3,5},{1,3},{0,1},{10,8},{12,10},{14... | collective-permute-start | bytes 3932168 | tf_op jit(solution)/shard_map/ppermute | solution.py:524
  137.8 112.2 %all-gather.11.cloned.1.call-start = ((), (), s32[]{:S(2)}) async-start(), calls=%async_computation.10 | async-start | bytes 5242880 | tf_op jit(solution)/shard_map/all_gather | solution.py:663
  139.0 20.6 %collective-permute-start.8 = (bf16[256,2048]{1,0:T(8,128)(2,1)S(1)}, bf16[256,2048]{1,0:T(8,128)(2,1)}, u32[]{:S(2)}, u32[]{:S(2)}) collective-permute-start(bf16[256,2048]{1,0:T(8,128)(2,1)S(1)} %copy-done.13), channel_id=1, source_target_pairs={{0,2},{2,4},{4,6},{6,7},{7,5},{5,3},{3,1},{1,0},{8,10},{10,12},{12... | collective-permute-start | bytes 3145736 | tf_op jit(solution)/shard_map/ppermute | solution.py:521
  140.7 20.5 %collective-permute-start.9 = (bf16[256,2048]{1,0:T(8,128)(2,1)S(1)}, bf16[256,2048]{1,0:T(8,128)(2,1)}, u32[]{:S(2)}, u32[]{:S(2)}) collective-permute-start(bf16[256,2048]{1,0:T(8,128)(2,1)S(1)} %copy-done.13), channel_id=1, source_target_pairs={{2,0},{4,2},{6,4},{7,6},{5,7},{3,5},{1,3},{0,1},{10,8},{12,10},{14... | collective-permute-start | bytes 3145736 | tf_op jit(solution)/shard_map/ppermute | solution.py:524
  195.4 274.3 %reduce-scatter.6.cloned.1.call-start = ((), (), s32[]{:S(2)}) async-start(), calls=%async_computation.11 | async-start | bytes 5242880 | tf_op jit(solution)/shard_map/reduce_scatter | solution.py:637
  195.5 25.7 %collective-permute-start.10 = (bf16[256,2048]{1,0:T(8,128)(2,1)}, bf16[256,2048]{1,0:T(8,128)(2,1)}, u32[]{:S(2)}, u32[]{:S(2)}) collective-permute-start(bf16[256,2048]{1,0:T(8,128)(2,1)} %collective-permute-done.8.refs_2_), channel_id=1, source_target_pairs={{0,2},{2,4},{4,6},{6,7},{7,5},{5,3},{3,1},{1,0},{8,10},{10,12},{12... | collective-permute-start | bytes 3145736 | tf_op jit(solution)/shard_map/ppermute | solution.py:521
  197.0 25.5 %collective-permute-start.11 = (bf16[256,2048]{1,0:T(8,128)(2,1)}, bf16[256,2048]{1,0:T(8,128)(2,1)}, u32[]{:S(2)}, u32[]{:S(2)}) collective-permute-start(bf16[256,2048]{1,0:T(8,128)(2,1)} %collective-permute-done.9.refs_3_), channel_id=1, source_target_pairs={{2,0},{4,2},{6,4},{7,6},{5,7},{3,5},{1,3},{0,1},{10,8},{12,10},{14... | collective-permute-start | bytes 3145736 | tf_op jit(solution)/shard_map/ppermute | solution.py:524
  222.6 24.2 %collective-permute-start.12 = (bf16[256,2048]{1,0:T(8,128)(2,1)S(1)}, bf16[256,2048]{1,0:T(8,128)(2,1)S(1)}, u32[]{:S(2)}, u32[]{:S(2)}) collective-permute-start(bf16[256,2048]{1,0:T(8,128)(2,1)S(1)} %multiply_convert_fusion.refs_0_), channel_id=1, source_target_pairs={{0,2},{2,4},{4,6},{6,7},{7,5},{5,3},{3,1},{1,0},{8,10},{10,12},{12... | collective-permute-start | bytes 3145736 | tf_op jit(solution)/shard_map/ppermute | solution.py:521
  224.1 23.9 %collective-permute-start.13 = (bf16[256,2048]{1,0:T(8,128)(2,1)S(1)}, bf16[256,2048]{1,0:T(8,128)(2,1)S(1)}, u32[]{:S(2)}, u32[]{:S(2)}) collective-permute-start(bf16[256,2048]{1,0:T(8,128)(2,1)S(1)} %multiply_convert_fusion.refs_0_), channel_id=1, source_target_pairs={{2,0},{4,2},{6,4},{7,6},{5,7},{3,5},{1,3},{0,1},{10,8},{12,10},{14... | collective-permute-start | bytes 3145736 | tf_op jit(solution)/shard_map/ppermute | solution.py:524
  248.0 23.4 %collective-permute-start.14 = (bf16[256,2048]{1,0:T(8,128)(2,1)}, bf16[256,2048]{1,0:T(8,128)(2,1)}, u32[]{:S(2)}, u32[]{:S(2)}) collective-permute-start(bf16[256,2048]{1,0:T(8,128)(2,1)} %collective-permute-done.10.refs_2_), channel_id=1, source_target_pairs={{0,2},{2,4},{4,6},{6,7},{7,5},{5,3},{3,1},{1,0},{8,10},{10,12},{12... | collective-permute-start | bytes 3145736 | tf_op jit(solution)/shard_map/ppermute | solution.py:521
  249.5 23.1 %collective-permute-start.15 = (bf16[256,2048]{1,0:T(8,128)(2,1)}, bf16[256,2048]{1,0:T(8,128)(2,1)}, u32[]{:S(2)}, u32[]{:S(2)}) collective-permute-start(bf16[256,2048]{1,0:T(8,128)(2,1)} %collective-permute-done.11.refs_3_), channel_id=1, source_target_pairs={{2,0},{4,2},{6,4},{7,6},{5,7},{3,5},{1,3},{0,1},{10,8},{12,10},{14... | collective-permute-start | bytes 3145736 | tf_op jit(solution)/shard_map/ppermute | solution.py:524
  272.6 26.9 %collective-permute-start.16 = (bf16[256,2048]{1,0:T(8,128)(2,1)}, bf16[256,2048]{1,0:T(8,128)(2,1)S(1)}, u32[]{:S(2)}, u32[]{:S(2)}) collective-permute-start(bf16[256,2048]{1,0:T(8,128)(2,1)} %copy-done.47), channel_id=1, source_target_pairs={{0,2},{2,4},{4,6},{6,7},{7,5},{5,3},{3,1},{1,0},{8,10},{10,12},{12... | collective-permute-start | bytes 3145736 | tf_op jit(solution)/shard_map/ppermute | solution.py:521
  274.0 25.4 %collective-permute-start.17 = (bf16[256,2048]{1,0:T(8,128)(2,1)}, bf16[256,2048]{1,0:T(8,128)(2,1)}, u32[]{:S(2)}, u32[]{:S(2)}) collective-permute-start(bf16[256,2048]{1,0:T(8,128)(2,1)} %copy-done.48), channel_id=1, source_target_pairs={{2,0},{4,2},{6,4},{7,6},{5,7},{3,5},{1,3},{0,1},{10,8},{12,10},{14... | collective-permute-start | bytes 3145736 | tf_op jit(solution)/shard_map/ppermute | solution.py:524
  314.2 27.3 %collective-permute-start.20 = (bf16[256,2048]{1,0:T(8,128)(2,1)}, bf16[256,2048]{1,0:T(8,128)(2,1)S(1)}, u32[]{:S(2)}, u32[]{:S(2)}) collective-permute-start(bf16[256,2048]{1,0:T(8,128)(2,1)} %copy-done.46), channel_id=1, source_target_pairs={{0,2},{2,4},{4,6},{6,7},{7,5},{5,3},{3,1},{1,0},{8,10},{10,12},{12... | collective-permute-start | bytes 3145736 | tf_op jit(solution)/shard_map/ppermute | solution.py:521
  315.9 25.6 %collective-permute-start.21 = (bf16[256,2048]{1,0:T(8,128)(2,1)}, bf16[256,2048]{1,0:T(8,128)(2,1)}, u32[]{:S(2)}, u32[]{:S(2)}) collective-permute-start(bf16[256,2048]{1,0:T(8,128)(2,1)} %collective-permute-done.17.refs_1_), channel_id=1, source_target_pairs={{2,0},{4,2},{6,4},{7,6},{5,7},{3,5},{1,3},{0,1},{10,8},{12,10},{14... | collective-permute-start | bytes 3145736 | tf_op jit(solution)/shard_map/ppermute | solution.py:524
  368.3 29.1 %collective-permute-start.26 = (bf16[128,2048]{1,0:T(8,128)(2,1)}, bf16[128,2048]{1,0:T(8,128)(2,1)S(1)}, u32[]{:S(2)}, u32[]{:S(2)}) collective-permute-start(bf16[128,2048]{1,0:T(8,128)(2,1)} %get-tuple-element.287), channel_id=1, source_target_pairs={{0,2},{2,4},{4,6},{6,7},{7,5},{5,3},{3,1},{1,0},{8,10},{10,12},{12... | collective-permute-start | bytes 1572872 | tf_op jit(solution)/shard_map/ppermute | solution.py:521
  370.0 27.4 %collective-permute-start.27 = (bf16[128,2048]{1,0:T(8,128)(2,1)}, bf16[128,2048]{1,0:T(8,128)(2,1)S(1)}, u32[]{:S(2)}, u32[]{:S(2)}) collective-permute-start(bf16[128,2048]{1,0:T(8,128)(2,1)} %get-tuple-element.288), channel_id=1, source_target_pairs={{2,0},{4,2},{6,4},{7,6},{5,7},{3,5},{1,3},{0,1},{10,8},{12,10},{14... | collective-permute-start | bytes 1572872 | tf_op jit(solution)/shard_map/ppermute | solution.py:524
  370.3 30.8 %collective-permute-start.24 = (bf16[128,2048]{1,0:T(8,128)(2,1)}, bf16[128,2048]{1,0:T(8,128)(2,1)S(1)}, u32[]{:S(2)}, u32[]{:S(2)}) collective-permute-start(bf16[128,2048]{1,0:T(8,128)(2,1)} %get-tuple-element.289), channel_id=1, source_target_pairs={{0,2},{2,4},{4,6},{6,7},{7,5},{5,3},{3,1},{1,0},{8,10},{10,12},{12... | collective-permute-start | bytes 1572872 | tf_op jit(solution)/shard_map/ppermute | solution.py:521
  372.0 30.0 %collective-permute-start.25 = (bf16[128,2048]{1,0:T(8,128)(2,1)}, bf16[128,2048]{1,0:T(8,128)(2,1)}, u32[]{:S(2)}, u32[]{:S(2)}) collective-permute-start(bf16[128,2048]{1,0:T(8,128)(2,1)} %get-tuple-element.290), channel_id=1, source_target_pairs={{2,0},{4,2},{6,4},{7,6},{5,7},{3,5},{1,3},{0,1},{10,8},{12,10},{14... | collective-permute-start | bytes 1572872 | tf_op jit(solution)/shard_map/ppermute | solution.py:524
  402.0 17.7 %collective-permute-start.28 = (bf16[256,2048]{1,0:T(8,128)(2,1)}, bf16[256,2048]{1,0:T(8,128)(2,1)S(1)}, u32[]{:S(2)}, u32[]{:S(2)}) collective-permute-start(bf16[256,2048]{1,0:T(8,128)(2,1)} %add_convert_fusion.16), channel_id=1, source_target_pairs={{0,2},{2,4},{4,6},{6,7},{7,5},{5,3},{3,1},{1,0},{8,10},{10,12},{12... | collective-permute-start | bytes 3145736 | tf_op jit(solution)/shard_map/ppermute | solution.py:521
  421.3 90.3 %reduce-scatter.8.cloned.1.call-start = ((), (), s32[]{:S(2)}) async-start(), calls=%async_computation.12 | async-start | bytes 5242880 | tf_op jit(solution)/shard_map/reduce_scatter | solution.py:637
  481.8 23.4 %all-to-all-start.1 = ((bf16[256,8,256]{2,0,1:T(8,128)(2,1)}), bf16[256,8,256]{2,0,1:T(8,128)(2,1)S(1)}, u32[]{:S(2)}, u32[]{:S(2)}) async-start(bf16[256,8,256]{2,0,1:T(8,128)(2,1)} %bitcast.58), calls=%async_computation.1 | async-start | bytes 2097152 | tf_op jit(solution)/shard_map/all_to_all | solution.py:751
  485.5 100.4 %reduce-scatter.10.cloned.1.call-start = ((), (), s32[]{:S(2)}) async-start(), calls=%async_computation.13 | async-start | bytes 10485760 | tf_op jit(solution)/shard_map/reduce_scatter | solution.py:637
  511.6 124.4 %reduce-scatter.12.cloned.1.call-start = ((), (), s32[]{:S(2)}) async-start(), calls=%async_computation.14 | async-start | bytes 5242880 | tf_op jit(solution)/shard_map/reduce_scatter | solution.py:637
  511.6 25.9 %collective-permute-start.34 = (bf16[256,2048]{1,0:T(8,128)(2,1)}, bf16[256,2048]{1,0:T(8,128)(2,1)}, u32[]{:S(2)}, u32[]{:S(2)}) collective-permute-start(bf16[256,2048]{1,0:T(8,128)(2,1)} %add_convert_fusion.18), channel_id=1, source_target_pairs={{0,2},{2,4},{4,6},{6,7},{7,5},{5,3},{3,1},{1,0},{8,10},{10,12},{12... | collective-permute-start | bytes 3145736 | tf_op jit(solution)/shard_map/ppermute | solution.py:521
  513.2 25.1 %collective-permute-start.35 = (bf16[256,2048]{1,0:T(8,128)(2,1)}, bf16[256,2048]{1,0:T(8,128)(2,1)}, u32[]{:S(2)}, u32[]{:S(2)}) collective-permute-start(bf16[256,2048]{1,0:T(8,128)(2,1)} %add_convert_fusion.17), channel_id=1, source_target_pairs={{2,0},{4,2},{6,4},{7,6},{5,7},{3,5},{1,3},{0,1},{10,8},{12,10},{14... | collective-permute-start | bytes 3145736 | tf_op jit(solution)/shard_map/ppermute | solution.py:524
  558.5 31.9 %collective-permute-start.38 = (bf16[256,2048]{1,0:T(8,128)(2,1)}, bf16[256,2048]{1,0:T(8,128)(2,1)}, u32[]{:S(2)}, u32[]{:S(2)}) collective-permute-start(bf16[256,2048]{1,0:T(8,128)(2,1)} %add_convert_fusion.10), channel_id=1, source_target_pairs={{0,2},{2,4},{4,6},{6,7},{7,5},{5,3},{3,1},{1,0},{8,10},{10,12},{12... | collective-permute-start | bytes 3145736 | tf_op jit(solution)/shard_map/ppermute | solution.py:521
  559.9 30.5 %collective-permute-start.39 = (bf16[256,2048]{1,0:T(8,128)(2,1)}, bf16[256,2048]{1,0:T(8,128)(2,1)}, u32[]{:S(2)}, u32[]{:S(2)}) collective-permute-start(bf16[256,2048]{1,0:T(8,128)(2,1)} %add_convert_fusion.9), channel_id=1, source_target_pairs={{2,0},{4,2},{6,4},{7,6},{5,7},{3,5},{1,3},{0,1},{10,8},{12,10},{14... | collective-permute-start | bytes 3145736 | tf_op jit(solution)/shard_map/ppermute | solution.py:524
  590.4 127.2 %reduce-scatter.14.cloned.1.call-start = ((), (), s32[]{:S(2)}) async-start(), calls=%async_computation.15 | async-start | bytes 3932160 | tf_op jit(solution)/shard_map/reduce_scatter | solution.py:637
  595.7 27.7 %collective-permute-start.40 = (bf16[256,2304]{1,0:T(8,128)(2,1)S(1)}, bf16[256,2304]{1,0:T(8,128)(2,1)S(1)}, u32[]{:S(2)}, u32[]{:S(2)}) collective-permute-start(bf16[256,2304]{1,0:T(8,128)(2,1)S(1)} %copy-done.26), channel_id=1, source_target_pairs={{0,2},{2,4},{4,6},{6,7},{7,5},{5,3},{3,1},{1,0},{8,10},{10,12},{12... | collective-permute-start | bytes 3538952 | tf_op jit(solution)/shard_map/ppermute | solution.py:521
  597.2 27.4 %collective-permute-start.41 = (bf16[256,2304]{1,0:T(8,128)(2,1)S(1)}, bf16[256,2304]{1,0:T(8,128)(2,1)S(1)}, u32[]{:S(2)}, u32[]{:S(2)}) collective-permute-start(bf16[256,2304]{1,0:T(8,128)(2,1)S(1)} %copy-done.25), channel_id=1, source_target_pairs={{2,0},{4,2},{6,4},{7,6},{5,7},{3,5},{1,3},{0,1},{10,8},{12,10},{14... | collective-permute-start | bytes 3538952 | tf_op jit(solution)/shard_map/ppermute | solution.py:524
  639.7 33.5 %collective-permute-start.45 = (bf16[256,2560]{1,0:T(8,128)(2,1)}, bf16[256,2560]{1,0:T(8,128)(2,1)}, u32[]{:S(2)}, u32[]{:S(2)}) collective-permute-start(bf16[256,2560]{1,0:T(8,128)(2,1)} %pad_maximum_fusion.1), channel_id=1, source_target_pairs={{0,2},{2,4},{4,6},{6,7},{7,5},{5,3},{3,1},{1,0},{8,10},{10,12},{12... | collective-permute-start | bytes 3932168 | tf_op jit(solution)/shard_map/ppermute | solution.py:521
  641.2 32.0 %collective-permute-start.46 = (bf16[256,2560]{1,0:T(8,128)(2,1)}, bf16[256,2560]{1,0:T(8,128)(2,1)}, u32[]{:S(2)}, u32[]{:S(2)}) collective-permute-start(bf16[256,2560]{1,0:T(8,128)(2,1)} %pad_maximum_fusion.2), channel_id=1, source_target_pairs={{2,0},{4,2},{6,4},{7,6},{5,7},{3,5},{1,3},{0,1},{10,8},{12,10},{14... | collective-permute-start | bytes 3932168 | tf_op jit(solution)/shard_map/ppermute | solution.py:524
  647.3 25.9 %collective-permute-start.47 = (f32[4112]{0:T(1024)S(1)}, f32[4112]{0:T(1024)S(1)}, u32[]{:S(2)}, u32[]{:S(2)}) collective-permute-start(f32[4112]{0:T(1024)S(1)} %add_add_fusion), channel_id=1, source_target_pairs={{0,4},{1,5},{2,6},{3,7},{4,0},{5,1},{6,2},{7,3},{8,12},{9,13},{10,... | collective-permute-start | bytes 49352 | tf_op jit(solution)/shard_map/ppermute | solution.py:624
  674.6 30.5 %collective-permute-start.48 = (bf16[256,2560]{1,0:T(8,128)(2,1)S(1)}, bf16[256,2560]{1,0:T(8,128)(2,1)S(1)}, u32[]{:S(2)}, u32[]{:S(2)}) collective-permute-start(bf16[256,2560]{1,0:T(8,128)(2,1)S(1)} %pad_maximum_fusion.3), channel_id=1, source_target_pairs={{0,2},{2,4},{4,6},{6,7},{7,5},{5,3},{3,1},{1,0},{8,10},{10,12},{12... | collective-permute-start | bytes 3932168 | tf_op jit(solution)/shard_map/ppermute | solution.py:521
  675.9 29.2 %collective-permute-start.49 = (bf16[256,2560]{1,0:T(8,128)(2,1)S(1)}, bf16[256,2560]{1,0:T(8,128)(2,1)S(1)}, u32[]{:S(2)}, u32[]{:S(2)}) collective-permute-start(bf16[256,2560]{1,0:T(8,128)(2,1)S(1)} %pad_maximum_fusion.4), channel_id=1, source_target_pairs={{2,0},{4,2},{6,4},{7,6},{5,7},{3,5},{1,3},{0,1},{10,8},{12,10},{14... | collective-permute-start | bytes 3932168 | tf_op jit(solution)/shard_map/ppermute | solution.py:524
  678.7 26.4 %collective-permute-start.50 = (f32[4112]{0:T(1024)S(1)}, f32[4112]{0:T(1024)S(1)}, u32[]{:S(2)}, u32[]{:S(2)}) collective-permute-start(f32[4112]{0:T(1024)S(1)} %add.277), channel_id=1, source_target_pairs={{0,2},{1,3},{2,0},{3,1},{4,6},{5,7},{6,4},{7,5},{8,10},{9,11},{10,... | collective-permute-start | bytes 49352 | tf_op jit(solution)/shard_map/ppermute | solution.py:624
  707.7 29.6 %collective-permute-start.51 = (bf16[256,2560]{1,0:T(8,128)(2,1)}, bf16[256,2560]{1,0:T(8,128)(2,1)}, u32[]{:S(2)}, u32[]{:S(2)}) collective-permute-start(bf16[256,2560]{1,0:T(8,128)(2,1)} %pad_maximum_fusion.5), channel_id=1, source_target_pairs={{0,2},{2,4},{4,6},{6,7},{7,5},{5,3},{3,1},{1,0},{8,10},{10,12},{12... | collective-permute-start | bytes 3932168 | tf_op jit(solution)/shard_map/ppermute | solution.py:521
  708.0 29.3 %collective-permute-start.52 = (bf16[256,2560]{1,0:T(8,128)(2,1)}, bf16[256,2560]{1,0:T(8,128)(2,1)}, u32[]{:S(2)}, u32[]{:S(2)}) collective-permute-start(bf16[256,2560]{1,0:T(8,128)(2,1)} %pad_maximum_fusion.6), channel_id=1, source_target_pairs={{2,0},{4,2},{6,4},{7,6},{5,7},{3,5},{1,3},{0,1},{10,8},{12,10},{14... | collective-permute-start | bytes 3932168 | tf_op jit(solution)/shard_map/ppermute | solution.py:524
  709.9 26.2 %collective-permute-start.53 = (f32[4112]{0:T(1024)S(1)}, f32[4112]{0:T(1024)S(1)}, u32[]{:S(2)}, u32[]{:S(2)}) collective-permute-start(f32[4112]{0:T(1024)S(1)} %add.282), channel_id=1, source_target_pairs={{0,1},{1,0},{2,3},{3,2},{4,5},{5,4},{6,7},{7,6},{8,9},{9,8},{10,11... | collective-permute-start | bytes 49352 | tf_op jit(solution)/shard_map/ppermute | solution.py:624
  (85 other events, 988.0 us)
Sparse Core Ops, SparseCore 0:
  10.2 31.2 all-gather.4
  48.4 59.1 all-gather.6
  137.9 57.4 all-gather.8
  196.8 34.4 all-gather.10
  421.4 41.4 reduce-scatter.5
  469.9 41.6 reduce-scatter.7
  514.1 71.7 reduce-scatter.9
  590.5 45.3 reduce-scatter.11
  638.5 37.9 reduce-scatter.13

commit v4 on v3

--- a/solution.py
+++ b/solution.py
@@ -115,37 +115,34 @@
 
     lax.fori_loop(0, length // TILE, query_block, 0)
 
-    for h in range(heads):
-        total_m, total_n = memory[h], norm[h : h + 1, :]
-        now_m, now_n = total_m, total_n
-        share = mix[h]
-        for half in range(length // SHORT):
-            fresh = True if half % 2 == 0 else splits[half // 2] == 1
-            now_m = jnp.where(fresh, total_m, now_m)
-            now_n = jnp.where(fresh, total_n, now_n)
-            states[half, h] = now_m
-            norms[half, h : h + 1, :] = now_n
-            both = state_matrix(now_m, now_n)
-
-            def chunk(index, carry):
-                here = tile_rows(index)
-                grown_m, grown_n = carry
+    total = [(memory[h], norm[h : h + 1, :]) for h in range(heads)]
+    now = list(total)
+    per = SHORT // TILE
+    for half in range(length // SHORT):
+        fresh = True if half % 2 == 0 else splits[half // 2] == 1
+        both = []
+        for h in range(heads):
+            now[h] = tuple(jnp.where(fresh, new, old) for new, old in zip(total[h], now[h]))
+            states[half, h] = now[h][0]
+            norms[half, h : h + 1, :] = now[h][1]
+            both.append(state_matrix(*now[h]))
+        for index in range(half * per, (half + 1) * per):
+            here = slice(index * TILE, (index + 1) * TILE)
+            for h in range(heads):
                 query_feat = feature(q_s[here, cols[h]].astype(jnp.float32))
                 key_feat = feature(k_s[here, cols[h]].astype(jnp.float32))
-                read = dot_nn(low(query_feat), both)
+                read = dot_nn(low(query_feat), both[h])
                 recalled = read[:, :size] / read[:, size:]
-                merged[here, cols[h]] = low(share * recalled + (1.0 - share) * attended[here, cols[h]])
-                back = dot_nn(low(key_feat), both)
+                merged[here, cols[h]] = low(mix[h] * recalled + (1.0 - mix[h]) * attended[here, cols[h]])
+                back = dot_nn(low(key_feat), both[h])
                 miss = v_s[here, cols[h]].astype(jnp.float32) - back[:, :size] / back[:, size:]
-                return (
-                    grown_m + dot_tn(low(key_feat), low(miss)),
-                    grown_n + jnp.sum(key_feat, axis=0, keepdims=True),
+                total[h] = (
+                    total[h][0] + dot_tn(low(key_feat), low(miss)),
+                    total[h][1] + jnp.sum(key_feat, axis=0, keepdims=True),
                 )
-
-            per = SHORT // TILE
-            total_m, total_n = lax.fori_loop(half * per, (half + 1) * per, chunk, (total_m, total_n))
-        memory_out[h] = total_m
-        norm_out[h : h + 1, :] = total_n
+    for h in range(heads):
+        memory_out[h] = total[h][0]
+        norm_out[h : h + 1, :] = total[h][1]
 
 
 def backward_kernel(
@@ -193,7 +190,7 @@
                 up_both = jnp.concatenate([low_up, low_memory], axis=1)
 
                 def chunk(index, carry, both=both, low_memory=low_memory, low_up=low_up, up_both=up_both, norm_row=norm_row, up_n=up_n, last=last):
-                    here = tile_rows(index)
+                    here = slice(index * TILE, (index + 1) * TILE)
                     sum_m, sum_n, sum_gate = carry
                     att = attended[here, col]
                     grad = combined_grad[here, col].astype(jnp.float32)
@@ -233,10 +230,10 @@
                         dk_s[here, col] = key_feat_grad * jnp.minimum(key_feat, 1.0)
                     return sum_m, sum_n, sum_gate
 
-                sum_m, sum_n, gate_sum = lax.fori_loop(
-                    half * per, (half + 1) * per, chunk,
-                    (jnp.zeros((size, size), jnp.float32), jnp.zeros((1, size), jnp.float32), gate_sum),
-                )
+                carry = (jnp.zeros((size, size), jnp.float32), jnp.zeros((1, size), jnp.float32), gate_sum)
+                for index in range(half * per, (half + 1) * per):
+                    carry = chunk(index, carry)
+                sum_m, sum_n, gate_sum = carry
                 if half % 2 == 1:
                     later_m, later_n = sum_m, sum_n
                 else:
@@ -341,7 +338,7 @@
 
 def project_kernel(*refs, count):
     pieces, weight = refs[:count], refs[count]
-    normed_all, extra_all, proj_all = refs[-3:]
+    normed_all, proj_all = refs[-2:]
     width = normed_all.shape[1]
 
     @pl.when(pl.program_id(0) == 0)
@@ -350,27 +347,22 @@
         for piece in pieces:
             here = slice(begin, begin + piece.shape[0])
             normed_all[here, :] = piece[:, :width]
-            extra_all[here, :] = piece[:, width:]
             begin += piece.shape[0]
 
     proj_all[...] = low(dot_nn(normed_all[...], weight[...]))
 
 
-def widen_kernel(*refs):
+def widen_kernel(*refs, moves):
     out, parts = refs[-1], refs[:-1]
-    columns = out.shape[2]
-    place = 0
-    for part in parts:
-        for begin in range(0, part.shape[1], columns):
-            out[:, place, :] = part[:, begin : begin + columns].astype(jnp.float32)
-            place += 1
-
-
-def widen(parts, shape):
+    for part, begin, size, place, column in moves:
+        out[:, place, column : column + size] = parts[part][:, begin : begin + size].astype(jnp.float32)
+
+
+def widen(parts, moves, shape):
     rows = shape[0]
     tall = min(rows, 128)
     return pl.pallas_call(
-        widen_kernel,
+        functools.partial(widen_kernel, moves=moves),
         grid=(rows // tall,),
         out_shape=jax.ShapeDtypeStruct(shape, jnp.float32),
         in_specs=[pl.BlockSpec((tall, part.shape[1]), lambda i: (i, 0)) for part in parts],
@@ -381,40 +373,47 @@
 
 def feed_kernel(*refs, count):
     normed, cots = refs[:count], refs[count : 2 * count]
-    w_gate, w_up, w_down = refs[2 * count : 2 * count + 3]
+    w_both, w_down = refs[2 * count : 2 * count + 2]
     result_s, grad_s = refs[-2:]
     results, grads = refs[-2 - 2 * count : -2 - count], refs[-2 - count : -2]
-    normed_all, cot_all, hidden, gate_grad, up_grad = refs[-7 - 2 * count : -2 - 2 * count]
+    normed_all, cot_all, hidden, first_grad, second_grad = refs[-7 - 2 * count : -2 - 2 * count]
     step = pl.program_id(0)
+    half = pl.num_programs(0) // 2
+    tile = w_down.shape[0]
 
     @pl.when(step == 0)
     def _():
         fill(normed_all, normed)
         fill(cot_all, cots)
 
-    gate = dot_nn(normed_all[...], w_gate[...])
-    up = dot_nn(normed_all[...], w_up[...])
+    gate_up = dot_nn(normed_all[...], w_both[...])
     hidden_grad = dot_nt(cot_all[...], w_down[...])
+    gate, up = gate_up[:, :tile], gate_up[:, tile:]
     sigmoid_gate = 1.0 / (1.0 + jnp.exp(-gate))
     activated = gate * sigmoid_gate
     low_hidden = low(activated * up)
     low_gate = low(hidden_grad * up * (sigmoid_gate + activated * (1.0 - sigmoid_gate)))
     low_up = low(hidden_grad * activated)
     hidden[...] = low_hidden
-    gate_grad[...] = low_gate
-    up_grad[...] = low_up
-    more_result = dot_nn(low_hidden, w_down[...])
-    more_grad = dot_nt(low_gate, w_gate[...]) + dot_nt(low_up, w_up[...])
+    both_grad = jnp.concatenate([low_gate, low_up], axis=1)
+
+    @pl.when(step < half)
+    def _():
+        first_grad[...] = both_grad
+
+    @pl.when(step >= half)
+    def _():
+        second_grad[...] = both_grad
 
     @pl.when(step == 0)
     def _():
-        result_s[...] = more_result
-        grad_s[...] = more_grad
+        result_s[...] = dot_nn(low_hidden, w_down[...])
+        grad_s[...] = dot_nt(both_grad, w_both[...])
 
     @pl.when(step > 0)
     def _():
-        result_s[...] += more_result
-        grad_s[...] += more_grad
+        result_s[...] += dot_nn(low_hidden, w_down[...])
+        grad_s[...] += dot_nt(both_grad, w_both[...])
 
     @pl.when(step == pl.num_programs(0) - 1)
     def _():
@@ -430,7 +429,6 @@
 
 
 def project_blocks(pieces, weight, place, length, before):
-    both = pieces[0].shape[1]
     width, wide = weight.shape
     count = len(pieces)
     tall = sum(piece.shape[0] for piece in pieces)
@@ -440,7 +438,6 @@
         grid=(wide // tile,),
         out_shape=[
             jax.ShapeDtypeStruct((length, width), jnp.bfloat16),
-            jax.ShapeDtypeStruct((length, both - width), jnp.bfloat16),
             jax.ShapeDtypeStruct((length, wide), jnp.bfloat16),
         ],
         in_specs=[pl.BlockSpec(piece.shape, lambda j: (0, 0)) for piece in pieces]
@@ -448,7 +445,6 @@
         + [ANY] * len(before),
         out_specs=[
             pl.BlockSpec((tall, width), lambda j: (place, 0)),
-            pl.BlockSpec((tall, both - width), lambda j: (place, 0)),
             pl.BlockSpec((tall, tile), lambda j: (place, j)),
         ],
         input_output_aliases={count + 1 + i: i for i in range(len(before))},
@@ -466,6 +462,8 @@
     piece = pl.BlockSpec((rows, width), lambda j: (0, 0))
     kept = pl.BlockSpec((tall, width), lambda j: (place, 0))
     part = pl.BlockSpec((tall, tile), lambda j: (place, j))
+    first = pl.BlockSpec((tall, 2 * tile), lambda j: (place, jnp.minimum(j, tiles // 2 - 1)))
+    second = pl.BlockSpec((tall, 2 * tile), lambda j: (place, jnp.maximum(j - tiles // 2, 0)))
     outs = pl.pallas_call(
         functools.partial(feed_kernel, count=count),
         grid=(tiles,),
@@ -474,17 +472,16 @@
         + [jax.ShapeDtypeStruct((rows, width), jnp.bfloat16)] * (2 * count),
         in_specs=[piece] * (2 * count)
         + [
-            pl.BlockSpec((width, tile), lambda j: (0, j)),
-            pl.BlockSpec((width, tile), lambda j: (0, j + tiles)),
+            pl.BlockSpec((width, 2 * tile), lambda j: (0, j)),
             pl.BlockSpec((tile, width), lambda j: (j, 0)),
         ]
         + [ANY] * len(before),
-        out_specs=[kept] * 2 + [part] * 3 + [piece] * (2 * count),
+        out_specs=[kept] * 2 + [part, first, second] + [piece] * (2 * count),
         scratch_shapes=[pltpu.VMEM((tall, width), jnp.float32)] * 2,
-        input_output_aliases={2 * count + 3 + i: i for i in range(len(before))},
+        input_output_aliases={2 * count + 2 + i: i for i in range(len(before))},
         compiler_params=pltpu.CompilerParams(vmem_limit_bytes=VMEM_LIMIT),
         cost_estimate=NO_COST,
-    )(*normed, *cots, f_in, f_in, f_out, *before)
+    )(*normed, *cots, f_in, f_out, *before)
     return outs[:5], outs[5 : 5 + count], outs[5 + count :]
 
 
@@ -622,6 +619,17 @@
 def swap_sum(values, axis, step, *earlier):
     size = lax.axis_size(axis)
     return values + after(lax.ppermute(values, axis, [(i, i ^ step) for i in range(size)]), *earlier)
+
+
+def halve_rows(values, bit):
+    size = lax.axis_size("seq")
+    mine = lax.div(lax.axis_index("seq"), bit) % 2
+    left = size // (2 * bit)
+    blocks = values.reshape(left, 2, values.shape[0] // (2 * left), values.shape[1])
+    kept = lax.dynamic_index_in_dim(blocks, mine, 1, keepdims=False)
+    sent = lax.dynamic_index_in_dim(blocks, 1 - mine, 1, keepdims=False)
+    moved = lax.ppermute(sent, "seq", [(i, i ^ bit) for i in range(size)])
+    return low(kept.astype(jnp.float32) + moved.astype(jnp.float32)).reshape(-1, values.shape[1])
 
 
 def rms_parts(values):
@@ -673,17 +681,25 @@
     )
 
     gather_a.hop()
-    f_in = whole(after(feed_in, w_in, gather_a.groups[1]).reshape(feed_in.shape[0], -1), 0)
+    feed_tile = min(FEED_TILE, feed_in.shape[2])
+    feed_tiles = feed_in.shape[2] // feed_tile
+    f_in = after(feed_in, gather_a.groups[0]).reshape(-1, 2, feed_tiles, feed_tile)
+    f_in = f_in.transpose(0, 2, 1, 3).reshape(feed_in.shape[0], -1)
+    f_in = whole(after(f_in, w_in, gather_a.groups[1]), 0)
     kept = []
     for step in range(2, half + 1):
-        gather_a.hop(*kept[2:3])
+        gather_a.hop(*kept[1:2])
         if step > 2:
             kept = project_blocks(gather_a.groups[step - 2], w_in, step - 2, length, kept)
     kept = project_blocks(gather_a.groups[half - 1], w_in, half - 1, length, kept)
-    gather_a.groups[half] = after(gather_a.groups[half], kept[2])
-    normed_a, extra, proj = project_blocks(gather_a.groups[0] + gather_a.groups[half], w_in, 0, length, kept)
-    extra = extra.reshape(count, *attention_out.shape)[ring.order].reshape(-1, attention_out.shape[1])
-    w_out = whole(after(extra, f_in), 1)
+    gather_a.groups[half] = after(gather_a.groups[half], kept[1])
+    normed_a, proj = project_blocks(gather_a.groups[0] + gather_a.groups[half], w_in, 0, length, kept)
+    w_out = jnp.zeros((length, gather_a.groups[0][0].shape[1] - width), jnp.bfloat16)
+    for step, group in enumerate(gather_a.groups):
+        for piece, d, begin in zip(group, (-step % count, step), (0, rows // 2 if step == half else 0)):
+            start = ring.ahead_index[d] * rows + begin
+            w_out = lax.dynamic_update_slice_in_dim(w_out, piece[:, width:], start, 0)
+    w_out = whole(after(w_out.reshape(-1, attention_out.shape[1]), f_in), 1)
 
     gather_c = Gather(ring, after(cotangent, gather_a.groups[half]))
     gather_c.hop()
@@ -720,7 +736,7 @@
         if step == 1:
             kept = feed(0, kept)
     kept = feed(half - 1, kept)
-    normed_f, cot, hidden, gate_grad, up_grad = kept
+    normed_f, cot, hidden, first_grad, second_grad = kept
 
     scatter_f = Scatter(ring, lambda d: normed_f_part[d])
     scatter_r = Scatter(ring, lambda d: result_part[d])
@@ -733,13 +749,13 @@
     scatter_f.hold(feed_out_local)
     feed_out_grad = sum_over_seq(after(feed_out_local, scatter_f.moved), 1)
     scatter_f.hop()
-    feed_gate_local = low(dot_tn(normed_f, after(gate_grad, scatter_f.sent)))
-    scatter_f.hold(feed_gate_local)
+    feed_first_local = low(dot_tn(normed_f, after(first_grad, scatter_f.sent)))
+    scatter_f.hold(feed_first_local)
     scatter_f.hop()
-    feed_up_local = low(dot_tn(normed_f, after(up_grad, scatter_f.sent)))
-    scatter_f.hold(feed_up_local)
+    feed_second_local = low(dot_tn(normed_f, after(second_grad, scatter_f.sent)))
+    scatter_f.hold(feed_second_local)
     normed_f_grad = scatter_f.total()
-    feed_gate_grad = sum_over_seq(after(feed_gate_local, feed_out_grad, normed_f_grad), 0)
+    feed_first_grad = sum_over_seq(after(feed_first_local, feed_out_grad, normed_f_grad), 0)
     scatter_r.prepare()
     gain_feed_part = jnp.sum(normed_f_grad * unit_second, axis=0)
     middle_grad = cotangent.astype(jnp.float32) + rms_back(
@@ -747,10 +763,10 @@
     )
     out_grad = low(middle_grad)
     combined_grad = low(dot_nt(out_grad, w_out))
-    attention_out_local = low(dot_tn(merged_mine, after(out_grad, feed_up_local)))
+    attention_out_local = low(dot_tn(merged_mine, after(out_grad, feed_second_local)))
     combined_grad = lax.all_to_all(combined_grad, "blk", 1, 0, tiled=True)
     combined_grad = after(combined_grad, attention_out_local, scatter_r.sent)
-    out_sum = sum_over_seq(after(attention_out_local, feed_gate_grad, combined_grad), 1)
+    out_sum = sum_over_seq(after(attention_out_local, feed_first_grad, combined_grad), 1)
     scatter_r.hop(combined_grad)
     proj_grad, gate_rows = attend_backward(
         ring.order, splits, mix, proj, combined_grad,
@@ -783,9 +799,9 @@
     scatter_a.hop()
     scatter_r.prepare(scatter_a.sent, rider=rider())
     scatter_a.hold(scatter_r.sent)
-    feed_up_grad = sum_over_seq(after(feed_up_local, out_sum, scatter_a.moved), 0)
     scatter_r.hop(scatter_a.moved)
     attention_in_local = low(dot_tn(normed_a, after(proj_grad, scatter_a.moved)))
+    feed_second_grad = sum_over_seq(after(feed_second_local, out_sum, scatter_a.moved), 0)
     gain_attention_part = jnp.sum(attention_in_local.astype(jnp.float32) * w_in.astype(jnp.float32), axis=1) / gain_attention
     gate_part = jnp.sum(gate_rows, axis=1) * mix * (1.0 - mix)
     gate_full = lax.dynamic_update_slice_in_dim(
@@ -796,28 +812,43 @@
     sums = sum_axis(sums, "seq")
     scatter_r.hold(scatter_a.parts, attention_in_local, sums)
     swaps = [1 << bit for bit in range(count.bit_length() - 1)]
+    halvings = [1 << bit for bit in reversed(range(lax.axis_size("seq").bit_length() - 1))]
+    attention_in_grad = attention_in_local
     while scatter_a.step > 1:
         scatter_a.prepare(rider=rider())
         scatter_a.hop(scatter_r.moved)
         if swaps:
             sums = swap_sum(after(sums, scatter_a.sent), "blk", swaps.pop())
-        scatter_a.hold(sums)
+        if halvings:
+            attention_in_grad = halve_rows(after(attention_in_grad, scatter_a.sent), halvings.pop())
+        scatter_a.hold(sums, attention_in_grad)
         scatter_r.prepare(rider=rider())
         scatter_r.hop(scatter_a.moved)
         scatter_a.compute(scatter_r.sent)
         if swaps:
             sums = swap_sum(after(sums, scatter_r.sent), "blk", swaps.pop())
-        scatter_r.hold(scatter_a.parts, sums)
+        if halvings:
+            attention_in_grad = halve_rows(after(attention_in_grad, scatter_r.sent), halvings.pop())
+        scatter_r.hold(scatter_a.parts, sums, attention_in_grad)
     scatter_a.prepare(rider=rider())
-    attention_in_grad = sum_over_seq(after(attention_in_local, feed_up_grad, scatter_a.sent), 0)
     scatter_a.hop()
     sums = after(sums, scatter_a.sent)
     while len(swaps) > 1:
         sums = swap_sum(sums, "blk", swaps.pop())
-    feed_in_grad = widen(after((feed_gate_grad, feed_up_grad), scatter_a.sent), feed_in.shape)
+    while halvings:
+        attention_in_grad = halve_rows(after(attention_in_grad, scatter_a.sent), halvings.pop())
+    halves = after((feed_first_grad, feed_second_grad), scatter_a.sent)
+    moves = []
+    for tile in range(feed_tiles):
+        part, begin = divmod(2 * feed_tile * tile, feed_in.shape[2])
+        for place in range(2):
+            moves.append((part, begin + place * feed_tile, feed_tile, place, tile * feed_tile))
+    feed_in_grad = widen(halves, moves, feed_in.shape)
+    size = attention_in.shape[2]
+    moves = [(0, place * size, size, place, 0) for place in range(attention_in.shape[1])]
+    attention_in_grad = widen((after(attention_in_grad, scatter_a.sent),), moves, attention_in.shape)
     result, feed_out_grad = after((low(middle + scatter_r.total()), feed_out_grad), scatter_a.sent)
     feed_out_grad = feed_out_grad.astype(jnp.float32)
-    attention_in_grad = widen((attention_in_grad,), attention_in.shape)
     while swaps:
         sums = swap_sum(sums, "blk", swaps.pop(), result, feed_in_grad, feed_out_grad, attention_in_grad)
     scatter_a.hold(sums)

time: 762 us -> 737 us (0.967)
  waiting for transfers between devices: 286 us -> 272 us
  Pallas kernels: 172 us -> 160 us
  local copies, waits for them, and re-layouts: 36.9 us -> 45.5 us
    dynamic_update_slice x0 -> x9, local copies, waits for them, and re-layouts: none -> 12.1 us  [per_device(): w_out = lax.dynamic_update_slice_in_dim(w_out, piece[:, width:], start, 0)]
    ppermute x24, waiting for transfers between devices: 155 us -> 144 us  [forth(): return lax.ppermute(values, 'blk', self.ahead)]
    pallas_call x5, Pallas kernels: 104 us -> 95.1 us  [feed_blocks(): pl.pallas_call(functools.partial(feed_kernel, count=count), grid=(tiles,)...]
    reduce_scatter x5 -> x4, waiting for transfers between devices: 33.1 us -> 26.8 us  [sum_over_seq(): lax.psum_scatter(low(values), 'seq', scatter_dimension=dimension, tiled=T...]
    unnamed x141 -> x124, local copies, waits for them, and re-layouts: 16.6 us -> 10.4 us
    convert_element_type x23 -> x24, other arithmetic: 40.2 us -> 38 us  [low(): return values.astype(jnp.bfloat16)]
  transfers between devices with their start and end apart: 64 -> 65, of which waited for: 38 -> 35; matrix products, arithmetic and copies ran while one was open for 22% -> 24% of each run, Pallas kernels for 21% -> 20%
where the time goes in v4:
time: 737 us; the launch traced here: 731 us
  waiting for transfers between devices  272 us (37%)
  Pallas kernels  160 us (22%)
  matrix products  85.5 us (12%)
  starting transfers between devices  63.1 us (9%)
  other arithmetic  60.3 us (8%)
  local copies, waits for them, and re-layouts  45.5 us (6%)
  blocking collectives  23.9 us (3%)
  between operations  21.2 us (3%)
    ppermute x24, waiting for transfers between devices, forth(): return lax.ppermute(values, 'blk', self.ahead)  144 us
    pallas_call x5, Pallas kernels, feed_blocks(): pl.pallas_call(functools.partial(feed_kernel, count=count), grid=(tiles,)...  95.1 us
    ppermute x3, waiting for transfers between devices, swap_sum(): lax.ppermute(values, axis, [(i, i ^ step) for i in range(size)])  62.1 us
    dot_general x5, matrix products, dot_tn(): lax.dot_general(left, right, (((0,), (0,)), ((), ())), preferred_element_...  55.3 us
    convert_element_type x24, other arithmetic, low(): return values.astype(jnp.bfloat16)  38 us
    ppermute x24, starting transfers between devices, forth(): return lax.ppermute(values, 'blk', self.ahead)  34.8 us
    reduce_scatter x4, waiting for transfers between devices, sum_over_seq(): lax.psum_scatter(low(values), 'seq', scatter_dimension=dimension, tiled=T...  26.8 us
    dot_general x10, matrix products, dot_nt(): lax.dot_general(left, right, (((1,), (1,)), ((), ())), preferred_element_...  24.1 us
  transfers between devices with their start and end apart: 65, of which 35 were waited for; matrix products, arithmetic and copies ran while one was open for 24% of the time, Pallas kernels for 20%

profile of v4, /device:TPU:0, one launch (start us, length us, event | category | flops | bytes accessed | tf_op | source)
XLA Modules:
  0.0 730.8 jit_solution(11411633999489770927)
XLA Ops:
  11.0 3.1 collective-permute-start
  14.1 4.5 reshape.143
  18.5 24.3 %collective-permute-done.refs_0_ = bf16[256,2560]{1,0:T(8,128)(2,1)} collective-permute-done((bf16[256,2560]{1,0:T(8,128)(2,1)S(1)}, bf16[256,2560]{1,0:T(8,128)(2,1)}, u32[]{:S(2)}, u32[]{:S(2)}) %collective-permute-start) | collective-permute-done | bytes 1310752 | tf_op jit(solution)/shard_map/ppermute | solution.py:518
  47.1 26.9 %collective-permute-done.2.refs_0_ = bf16[256,2560]{1,0:T(8,128)(2,1)S(1)} collective-permute-done((bf16[256,2560]{1,0:T(8,128)(2,1)}, bf16[256,2560]{1,0:T(8,128)(2,1)S(1)}, u32[]{:S(2)}, u32[]{:S(2)}) %collective-permute-start.2) | collective-permute-done | bytes 1310752 | tf_op jit(solution)/shard_map/ppermute | solution.py:518
  93.5 10.3 %collective-permute-done.4.refs_0_ = bf16[256,2560]{1,0:T(8,128)(2,1)S(1)} collective-permute-done((bf16[256,2560]{1,0:T(8,128)(2,1)}, bf16[256,2560]{1,0:T(8,128)(2,1)S(1)}, u32[]{:S(2)}, u32[]{:S(2)}) %collective-permute-start.4) | collective-permute-done | bytes 1310752 | tf_op jit(solution)/shard_map/ppermute | solution.py:518
  108.3 5.7 shard_map.230
  118.8 5.7 shard_map.231
  124.5 5.7 shard_map.232
  139.1 6.5 shard_map.233
  145.6 13.3 %shard_map.234 = (bf16[2048,256]{1,0:T(8,128)(2,1)}, f32[2048,256]{1,0:T(8,128)}, f32[4,2,512]{2,1,0:T(2,128)}, f32[2,2,128,128]{3,2,1,0:T(8,128)}, f32[2,2,128]...) custom-call(s32[8]{0:T(128)} %gather_fusion, s32[1]{0:T(128)} %bitcast.69.splits, f32[2]{0:T(128)} %add_divide_fusion.mix, ...), custom_call_target="tpu_custom_call" | custom-call | flops 4000000000 | bytes 4096 | tf_op jit(solution)/shard_map/pallas_call | solution.py:298
  160.4 23.9 %all_to_all.38 = bf16[8,256,256]{1,2,0:T(8,128)(2,1)} all-to-all(bf16[8,256,256]{1,2,0:T(8,128)(2,1)S(1)} %copy.59), channel_id=1, replica_groups=mesh['seq'=4,'blk'=8] {'blk'}, dimensions={0} | all-to-all | bytes 2097152 | tf_op jit(solution)/shard_map/all_to_all | solution.py:709
  184.3 6.6 all-gather.9.cloned.1.call-done
  193.1 6.2 multiply_reduce_fusion.3
  199.5 17.2 %collective-permute-done.10.refs_2_ = bf16[256,2048]{1,0:T(8,128)(2,1)} collective-permute-done((bf16[256,2048]{1,0:T(8,128)(2,1)}, bf16[256,2048]{1,0:T(8,128)(2,1)}, u32[]{:S(2)}, u32[]{:S(2)}) %collective-permute-start.10) | collective-permute-done | bytes 1048608 | tf_op jit(solution)/shard_map/ppermute | solution.py:518
  219.9 22.2 %collective-permute-done.12.refs_0_ = bf16[256,2048]{1,0:T(8,128)(2,1)S(1)} collective-permute-done((bf16[256,2048]{1,0:T(8,128)(2,1)S(1)}, bf16[256,2048]{1,0:T(8,128)(2,1)S(1)}, u32[]{:S(2)}, u32[]{:S(2)}) %collective-permute-start.12) | collective-permute-done | bytes 1048608 | tf_op jit(solution)/shard_map/ppermute | solution.py:518
  246.3 13.4 %shard_map.235 = (bf16[2048,2048]{1,0:T(8,128)(2,1)}, bf16[2048,2048]{1,0:T(8,128)(2,1)}, bf16[2048,1024]{1,0:T(8,128)(2,1)}, bf16[2048,1024]{1,0:T(8,128)(2,1)}...) custom-call(bf16[256,2048]{1,0:T(8,128)(2,1)} %copy-done.40, ...), custom_call_target="tpu_custom_call" | custom-call | flops 4000000000 | bytes 4096 | tf_op jit(solution)/shard_map/pallas_call | solution.py:467
  259.7 7.8 %collective-permute-done.14.refs_2_ = bf16[256,2048]{1,0:T(8,128)(2,1)S(1)} collective-permute-done((bf16[256,2048]{1,0:T(8,128)(2,1)}, bf16[256,2048]{1,0:T(8,128)(2,1)S(1)}, u32[]{:S(2)}, u32[]{:S(2)}) %collective-permute-start.14) | collective-permute-done | bytes 1048608 | tf_op jit(solution)/shard_map/ppermute | solution.py:518
  271.1 22.8 %shard_map.236 = (bf16[2048,2048]{1,0:T(8,128)(2,1)}, bf16[2048,2048]{1,0:T(8,128)(2,1)}, bf16[2048,1024]{1,0:T(8,128)(2,1)}, bf16[2048,1024]{1,0:T(8,128)(2,1)}...) custom-call(bf16[256,2048]{1,0:T(8,128)(2,1)} %copy-done.32, ...), custom_call_target="tpu_custom_call", output_to_operand_aliasing={{0}: (6, {}), {1}: (7, {}), {2}: (8, {}), {3}: (9, {}), {4}... | custom-call | flops 4000000000 | bytes 4096 | tf_op jit(solution)/shard_map/pallas_call | solution.py:467
  297.2 6.9 collective-permute-done.18.refs_2_
  304.1 2.8 collective-permute-done.19.refs_3_
  309.5 22.8 %shard_map.237 = (bf16[2048,2048]{1,0:T(8,128)(2,1)}, bf16[2048,2048]{1,0:T(8,128)(2,1)}, bf16[2048,1024]{1,0:T(8,128)(2,1)}, bf16[2048,1024]{1,0:T(8,128)(2,1)}...) custom-call(bf16[256,2048]{1,0:T(8,128)(2,1)} %collective-permute-do, ...), custom_call_target="tpu_custom_call", output_to_operand_aliasing={{0}: (6, {}), {1}: (7, {}), {2}: (8, {}), {3}: (9, {}), {4}... | custom-call | flops 4000000000 | bytes 4096 | tf_op jit(solution)/shard_map/pallas_call | solution.py:467
  336.0 5.6 collective-permute-done.22.refs_0_
  341.6 3.7 collective-permute-done.23.refs_1_
  345.3 13.4 %shard_map.238 = (bf16[2048,2048]{1,0:T(8,128)(2,1)}, bf16[2048,2048]{1,0:T(8,128)(2,1)}, bf16[2048,1024]{1,0:T(8,128)(2,1)}, bf16[2048,1024]{1,0:T(8,128)(2,1)}...) custom-call(bf16[128,2048]{1,0:T(8,128)(2,1)} %copy-done.50, ...), custom_call_target="tpu_custom_call", output_to_operand_aliasing={{0}: (6, {}), {1}: (7, {}), {2}: (8, {}), {3}: (9, {}), {4}... | custom-call | flops 4000000000 | bytes 4096 | tf_op jit(solution)/shard_map/pallas_call | solution.py:467
  362.8 22.7 %shard_map.239 = (bf16[2048,2048]{1,0:T(8,128)(2,1)}, bf16[2048,2048]{1,0:T(8,128)(2,1)}, bf16[2048,1024]{1,0:T(8,128)(2,1)}, bf16[2048,1024]{1,0:T(8,128)(2,1)}...) custom-call(bf16[256,2048]{1,0:T(8,128)(2,1)} %copy-done.24, ...), custom_call_target="tpu_custom_call", output_to_operand_aliasing={{0}: (6, {}), {1}: (7, {}), {2}: (8, {}), {3}: (9, {}), {4}... | custom-call | flops 4000000000 | bytes 4096 | tf_op jit(solution)/shard_map/pallas_call | solution.py:467
  392.3 13.1 %convolution_convert_fusion.1 = bf16[1024,2048]{1,0:T(8,128)(2,1)} fusion(bf16[2048,1024]{1,0:T(8,128)(2,1)S(1)} %copy-done.6, bf16[2048,2048]{1,0:T(8,128)(2,1)} %get-tuple-element.305), kind=kOutput, calls=%fused_computation.4 | convolution fusion | flops 8592031744 | bytes 16777216 | tf_op jit(solution)/shard_map/dot_general | solution.py:29
  408.9 3.1 add_convert_fusion.13
  415.4 13.1 %convolution_convert_fusion.3 = bf16[2048,1024]{1,0:T(8,128)(2,1)} fusion(bf16[2048,2048]{1,0:T(8,128)(2,1)} %get-tuple-element.313, bf16[2048,1024]{1,0:T(8,128)(2,1)S(1)} %copy-done.7), kind=kOutput, calls=%fused_computation.6 | convolution fusion | flops 8592031744 | bytes 16777216 | tf_op jit(solution)/shard_map/dot_general | solution.py:29
  431.7 3.1 add_convert_fusion.11
  439.5 12.9 %convolution_convert_fusion.2 = bf16[2048,1024]{1,0:T(8,128)(2,1)} fusion(bf16[2048,2048]{1,0:T(8,128)(2,1)} %get-tuple-element.313, bf16[2048,1024]{1,0:T(8,128)(2,1)S(1)} %copy-done.8), kind=kOutput, calls=%fused_computation.5 | convolution fusion | flops 8592031744 | bytes 16777216 | tf_op jit(solution)/shard_map/dot_general | solution.py:29
  452.8 3.5 multiply_reduce_fusion.1
  459.8 7.2 convolution_convert_fusion.11
  468.1 3.7 all-to-all-start.1
  475.5 5.7 convolution_convert_fusion
  481.2 11.5 %all-to-all-done.1 = bf16[256,8,256]{2,0,1:T(8,128)(2,1)S(1)} async-done(((bf16[256,8,256]{2,0,1:T(8,128)(2,1)}), bf16[256,8,256]{2,0,1:T(8,128)(2,1)S(1)}, u32[]{:S(2)}, u32[]{:S(2)}) %all-to-all-start.1) | async-done | bytes 1048608 | tf_op jit(solution)/shard_map/all_to_all | solution.py:767
  492.7 6.1 reduce-scatter.7.cloned.1.call-done.refs_0_
  501.3 19.2 %shard_map.240 = (bf16[2048,768]{1,0:T(8,128)(2,1)}, f32[2,128]{1,0:T(2,128)}) custom-call(s32[8]{0:T(128)} %gather_fusion, s32[1]{0:T(128)} %bitcast.70.splits, f32[2]{0:T(128)} %add_divide_fusion.mix, bf16[2048,768]{1,0:T(8,128)(2,1)} %get-tuple-element.228.proj, bf16[2048,256]{1,0:T(8,128)(2,1)} %bitcast.79, f32[2048,256]{1,0:T(8,128)} %get-tuple-element.333.attended, ...), custom_call_target="tpu_custom_call" | custom-call | flops 4000000000 | bytes 4096 | tf_op jit(solution)/shard_map/pallas_call | solution.py:319
  537.3 4.3 collective-permute-done.36
  552.5 20.7 %reduce-scatter.9.cloned.1.call-done = bf16[2048,512]{1,0:T(8,128)(2,1)} async-done(((bf16[2048,2048]{1,0:T(8,128)(2,1)}), bf16[2048,512]{1,0:T(8,128)(2,1)}) %reduce-scatter.9.cloned.1.call-update) | async-done | bytes 2097168 | tf_op jit(solution)/shard_map/reduce_scatter | solution.py:645
  579.8 10.6 %multiply_reduce_fusion = (f32[2048]{0:T(1024)S(1)}, bf16[2048,768]{1,0:T(8,128)(2,1)S(1)}) fusion(bf16[2048,768]{1,0:T(8,128)(2,1)S(1)} %copy-done.2, bf16[2048,2048]{1,0:T(8,128)(2,1)} %get-tuple-element.365, bf16[2048,768]{1,0:T(8,128)(2,1)} %get-tuple-element.366), kind=kOutput, calls=%fused_computation.3 | convolution fusion | flops 6450313216 | bytes 17833984 | tf_op jit(solution)/shard_map/dot_general | solution.py:29
  594.7 11.0 %collective-permute-done.40 = bf16[256,2304]{1,0:T(8,128)(2,1)} collective-permute-done((bf16[256,2304]{1,0:T(8,128)(2,1)}, bf16[256,2304]{1,0:T(8,128)(2,1)}, u32[]{:S(2)}, u32[]{:S(2)}) %collective-permute-start.40) | collective-permute-done | bytes 1179680 | tf_op jit(solution)/shard_map/ppermute | solution.py:518
  624.8 23.0 %collective-permute-done.47 = f32[4112]{0:T(1024)S(1)} collective-permute-done((f32[4112]{0:T(1024)S(1)}, f32[4112]{0:T(1024)S(1)}, u32[]{:S(2)}, u32[]{:S(2)}) %collective-permute-start.47) | collective-permute-done | bytes 16480 | tf_op jit(solution)/shard_map/ppermute | solution.py:621
  655.0 26.5 %collective-permute-done.51 = f32[4112]{0:T(1024)S(1)} collective-permute-done((f32[4112]{0:T(1024)S(1)}, f32[4112]{0:T(1024)S(1)}, u32[]{:S(2)}, u32[]{:S(2)}) %collective-permute-start.51) | collective-permute-done | bytes 16480 | tf_op jit(solution)/shard_map/ppermute | solution.py:621
  690.3 3.7 shard_map.242
  693.9 3.0 copy.63
  697.0 4.7 shard_map.241
  701.7 12.6 %collective-permute-done.55 = f32[4112]{0:T(1024)S(1)} collective-permute-done((f32[4112]{0:T(1024)S(1)}, f32[4112]{0:T(1024)S(1)}, u32[]{:S(2)}, u32[]{:S(2)}) %collective-permute-start.55) | collective-permute-done | bytes 16480 | tf_op jit(solution)/shard_map/ppermute | solution.py:621
  715.5 3.4 fusion.7
  (332 shorter events, 180.1 us)
Async XLA Ops:
  7.2 37.2 %all-gather.5.cloned.1.call-start = ((), (), s32[]{:S(2)}) async-start(), calls=%async_computation.6 | async-start | bytes 3932160 | tf_op jit(solution)/shard_map/all_gather | solution.py:671
  9.9 123.8 %all-gather.7.cloned.1.call-start = ((), (), s32[]{:S(2)}) async-start(), calls=%async_computation.7 | async-start | bytes 10485760 | tf_op jit(solution)/shard_map/all_gather | solution.py:671
  11.0 31.9 %collective-permute-start = (bf16[256,2560]{1,0:T(8,128)(2,1)S(1)}, bf16[256,2560]{1,0:T(8,128)(2,1)}, u32[]{:S(2)}, u32[]{:S(2)}) collective-permute-start(bf16[256,2560]{1,0:T(8,128)(2,1)S(1)} %pad_maximum_fusion.refs_0_), channel_id=1, source_target_pairs={{0,2},{2,4},{4,6},{6,7},{7,5},{5,3},{3,1},{1,0},{8,10},{10,12},{12... | collective-permute-start | bytes 3932168 | tf_op jit(solution)/shard_map/ppermute | solution.py:518
  14.0 30.3 %collective-permute-start.1 = (bf16[256,2560]{1,0:T(8,128)(2,1)S(1)}, bf16[256,2560]{1,0:T(8,128)(2,1)}, u32[]{:S(2)}, u32[]{:S(2)}) collective-permute-start(bf16[256,2560]{1,0:T(8,128)(2,1)S(1)} %pad_maximum_fusion.refs_0_), channel_id=1, source_target_pairs={{2,0},{4,2},{6,4},{7,6},{5,7},{3,5},{1,3},{0,1},{10,8},{12,10},{14... | collective-permute-start | bytes 3932168 | tf_op jit(solution)/shard_map/ppermute | solution.py:521
  44.4 146.5 %all-gather.9.cloned.1.call-start = ((), (), s32[]{:S(2)}) async-start(), calls=%async_computation.8 | async-start | bytes 10485760 | tf_op jit(solution)/shard_map/all_gather | solution.py:671
  44.5 29.6 %collective-permute-start.2 = (bf16[256,2560]{1,0:T(8,128)(2,1)}, bf16[256,2560]{1,0:T(8,128)(2,1)S(1)}, u32[]{:S(2)}, u32[]{:S(2)}) collective-permute-start(bf16[256,2560]{1,0:T(8,128)(2,1)} %collective-permute-done.refs_0_), channel_id=1, source_target_pairs={{0,2},{2,4},{4,6},{6,7},{7,5},{5,3},{3,1},{1,0},{8,10},{10,12},{12... | collective-permute-start | bytes 3932168 | tf_op jit(solution)/shard_map/ppermute | solution.py:518
  46.1 29.4 %collective-permute-start.3 = (bf16[256,2560]{1,0:T(8,128)(2,1)}, bf16[256,2560]{1,0:T(8,128)(2,1)}, u32[]{:S(2)}, u32[]{:S(2)}) collective-permute-start(bf16[256,2560]{1,0:T(8,128)(2,1)} %collective-permute-done.1.refs_1_), channel_id=1, source_target_pairs={{2,0},{4,2},{6,4},{7,6},{5,7},{3,5},{1,3},{0,1},{10,8},{12,10},{14... | collective-permute-start | bytes 3932168 | tf_op jit(solution)/shard_map/ppermute | solution.py:521
  75.4 28.4 %collective-permute-start.4 = (bf16[256,2560]{1,0:T(8,128)(2,1)}, bf16[256,2560]{1,0:T(8,128)(2,1)S(1)}, u32[]{:S(2)}, u32[]{:S(2)}) collective-permute-start(bf16[256,2560]{1,0:T(8,128)(2,1)} %copy-done.26), channel_id=1, source_target_pairs={{0,2},{2,4},{4,6},{6,7},{7,5},{5,3},{3,1},{1,0},{8,10},{10,12},{12... | collective-permute-start | bytes 3932168 | tf_op jit(solution)/shard_map/ppermute | solution.py:518
  78.4 28.3 %collective-permute-start.5 = (bf16[256,2560]{1,0:T(8,128)(2,1)}, bf16[256,2560]{1,0:T(8,128)(2,1)}, u32[]{:S(2)}, u32[]{:S(2)}) collective-permute-start(bf16[256,2560]{1,0:T(8,128)(2,1)} %collective-permute-done.3.refs_1_), channel_id=1, source_target_pairs={{2,0},{4,2},{6,4},{7,6},{5,7},{3,5},{1,3},{0,1},{10,8},{12,10},{14... | collective-permute-start | bytes 3932168 | tf_op jit(solution)/shard_map/ppermute | solution.py:521
  133.7 112.6 %all-gather.11.cloned.1.call-start = ((), (), s32[]{:S(2)}) async-start(), calls=%async_computation.9 | async-start | bytes 5242880 | tf_op jit(solution)/shard_map/all_gather | solution.py:671
  133.8 25.2 %collective-permute-start.8 = (bf16[256,2048]{1,0:T(8,128)(2,1)S(1)}, bf16[256,2048]{1,0:T(8,128)(2,1)}, u32[]{:S(2)}, u32[]{:S(2)}) collective-permute-start(bf16[256,2048]{1,0:T(8,128)(2,1)S(1)} %copy-done.15), channel_id=1, source_target_pairs={{0,2},{2,4},{4,6},{6,7},{7,5},{5,3},{3,1},{1,0},{8,10},{10,12},{12... | collective-permute-start | bytes 3145736 | tf_op jit(solution)/shard_map/ppermute | solution.py:518
  135.6 23.4 %collective-permute-start.9 = (bf16[256,2048]{1,0:T(8,128)(2,1)S(1)}, bf16[256,2048]{1,0:T(8,128)(2,1)}, u32[]{:S(2)}, u32[]{:S(2)}) collective-permute-start(bf16[256,2048]{1,0:T(8,128)(2,1)S(1)} %copy-done.15), channel_id=1, source_target_pairs={{2,0},{4,2},{6,4},{7,6},{5,7},{3,5},{1,3},{0,1},{10,8},{12,10},{14... | collective-permute-start | bytes 3145736 | tf_op jit(solution)/shard_map/ppermute | solution.py:521
  191.0 265.4 %reduce-scatter.5.cloned.1.call-start = ((), (), s32[]{:S(2)}) async-start(), calls=%async_computation.10 | async-start | bytes 5242880 | tf_op jit(solution)/shard_map/reduce_scatter | solution.py:645
  191.0 25.7 %collective-permute-start.10 = (bf16[256,2048]{1,0:T(8,128)(2,1)}, bf16[256,2048]{1,0:T(8,128)(2,1)}, u32[]{:S(2)}, u32[]{:S(2)}) collective-permute-start(bf16[256,2048]{1,0:T(8,128)(2,1)} %collective-permute-done.8.refs_2_), channel_id=1, source_target_pairs={{0,2},{2,4},{4,6},{6,7},{7,5},{5,3},{3,1},{1,0},{8,10},{10,12},{12... | collective-permute-start | bytes 3145736 | tf_op jit(solution)/shard_map/ppermute | solution.py:518
  192.6 25.4 %collective-permute-start.11 = (bf16[256,2048]{1,0:T(8,128)(2,1)}, bf16[256,2048]{1,0:T(8,128)(2,1)}, u32[]{:S(2)}, u32[]{:S(2)}) collective-permute-start(bf16[256,2048]{1,0:T(8,128)(2,1)} %collective-permute-done.9.refs_3_), channel_id=1, source_target_pairs={{2,0},{4,2},{6,4},{7,6},{5,7},{3,5},{1,3},{0,1},{10,8},{12,10},{14... | collective-permute-start | bytes 3145736 | tf_op jit(solution)/shard_map/ppermute | solution.py:521
  217.9 24.2 %collective-permute-start.12 = (bf16[256,2048]{1,0:T(8,128)(2,1)S(1)}, bf16[256,2048]{1,0:T(8,128)(2,1)S(1)}, u32[]{:S(2)}, u32[]{:S(2)}) collective-permute-start(bf16[256,2048]{1,0:T(8,128)(2,1)S(1)} %multiply_convert_fusion.refs_0_), channel_id=1, source_target_pairs={{0,2},{2,4},{4,6},{6,7},{7,5},{5,3},{3,1},{1,0},{8,10},{10,12},{12... | collective-permute-start | bytes 3145736 | tf_op jit(solution)/shard_map/ppermute | solution.py:518
  219.4 23.9 %collective-permute-start.13 = (bf16[256,2048]{1,0:T(8,128)(2,1)S(1)}, bf16[256,2048]{1,0:T(8,128)(2,1)S(1)}, u32[]{:S(2)}, u32[]{:S(2)}) collective-permute-start(bf16[256,2048]{1,0:T(8,128)(2,1)S(1)} %multiply_convert_fusion.refs_0_), channel_id=1, source_target_pairs={{2,0},{4,2},{6,4},{7,6},{5,7},{3,5},{1,3},{0,1},{10,8},{12,10},{14... | collective-permute-start | bytes 3145736 | tf_op jit(solution)/shard_map/ppermute | solution.py:521
  244.3 23.3 %collective-permute-start.14 = (bf16[256,2048]{1,0:T(8,128)(2,1)}, bf16[256,2048]{1,0:T(8,128)(2,1)S(1)}, u32[]{:S(2)}, u32[]{:S(2)}) collective-permute-start(bf16[256,2048]{1,0:T(8,128)(2,1)} %collective-permute-done.10.refs_2_), channel_id=1, source_target_pairs={{0,2},{2,4},{4,6},{6,7},{7,5},{5,3},{3,1},{1,0},{8,10},{10,12},{12... | collective-permute-start | bytes 3145736 | tf_op jit(solution)/shard_map/ppermute | solution.py:518
  245.8 23.1 %collective-permute-start.15 = (bf16[256,2048]{1,0:T(8,128)(2,1)}, bf16[256,2048]{1,0:T(8,128)(2,1)}, u32[]{:S(2)}, u32[]{:S(2)}) collective-permute-start(bf16[256,2048]{1,0:T(8,128)(2,1)} %collective-permute-done.11.refs_3_), channel_id=1, source_target_pairs={{2,0},{4,2},{6,4},{7,6},{5,7},{3,5},{1,3},{0,1},{10,8},{12,10},{14... | collective-permute-start | bytes 3145736 | tf_op jit(solution)/shard_map/ppermute | solution.py:521
  268.9 25.1 %collective-permute-start.16 = (bf16[256,2048]{1,0:T(8,128)(2,1)}, bf16[256,2048]{1,0:T(8,128)(2,1)}, u32[]{:S(2)}, u32[]{:S(2)}) collective-permute-start(bf16[256,2048]{1,0:T(8,128)(2,1)} %copy-done.32), channel_id=1, source_target_pairs={{0,2},{2,4},{4,6},{6,7},{7,5},{5,3},{3,1},{1,0},{8,10},{10,12},{12... | collective-permute-start | bytes 3145736 | tf_op jit(solution)/shard_map/ppermute | solution.py:518
  270.6 23.4 %collective-permute-start.17 = (bf16[256,2048]{1,0:T(8,128)(2,1)}, bf16[256,2048]{1,0:T(8,128)(2,1)}, u32[]{:S(2)}, u32[]{:S(2)}) collective-permute-start(bf16[256,2048]{1,0:T(8,128)(2,1)} %copy-done.33), channel_id=1, source_target_pairs={{2,0},{4,2},{6,4},{7,6},{5,7},{3,5},{1,3},{0,1},{10,8},{12,10},{14... | collective-permute-start | bytes 3145736 | tf_op jit(solution)/shard_map/ppermute | solution.py:521
  306.9 25.4 %collective-permute-start.20 = (bf16[256,2048]{1,0:T(8,128)(2,1)}, bf16[256,2048]{1,0:T(8,128)(2,1)S(1)}, u32[]{:S(2)}, u32[]{:S(2)}) collective-permute-start(bf16[256,2048]{1,0:T(8,128)(2,1)} %collective-permute-done.16.refs_0_), channel_id=1, source_target_pairs={{0,2},{2,4},{4,6},{6,7},{7,5},{5,3},{3,1},{1,0},{8,10},{10,12},{12... | collective-permute-start | bytes 3145736 | tf_op jit(solution)/shard_map/ppermute | solution.py:518
  309.5 22.8 %collective-permute-start.21 = (bf16[256,2048]{1,0:T(8,128)(2,1)}, bf16[256,2048]{1,0:T(8,128)(2,1)}, u32[]{:S(2)}, u32[]{:S(2)}) collective-permute-start(bf16[256,2048]{1,0:T(8,128)(2,1)} %collective-permute-done.17.refs_1_), channel_id=1, source_target_pairs={{2,0},{4,2},{6,4},{7,6},{5,7},{3,5},{1,3},{0,1},{10,8},{12,10},{14... | collective-permute-start | bytes 3145736 | tf_op jit(solution)/shard_map/ppermute | solution.py:521
  358.7 26.9 %collective-permute-start.26 = (bf16[128,2048]{1,0:T(8,128)(2,1)}, bf16[128,2048]{1,0:T(8,128)(2,1)S(1)}, u32[]{:S(2)}, u32[]{:S(2)}) collective-permute-start(bf16[128,2048]{1,0:T(8,128)(2,1)} %get-tuple-element.283), channel_id=1, source_target_pairs={{0,2},{2,4},{4,6},{6,7},{7,5},{5,3},{3,1},{1,0},{8,10},{10,12},{12... | collective-permute-start | bytes 1572872 | tf_op jit(solution)/shard_map/ppermute | solution.py:518
  359.6 25.9 %collective-permute-start.27 = (bf16[128,2048]{1,0:T(8,128)(2,1)}, bf16[128,2048]{1,0:T(8,128)(2,1)S(1)}, u32[]{:S(2)}, u32[]{:S(2)}) collective-permute-start(bf16[128,2048]{1,0:T(8,128)(2,1)} %get-tuple-element.284), channel_id=1, source_target_pairs={{2,0},{4,2},{6,4},{7,6},{5,7},{3,5},{1,3},{0,1},{10,8},{12,10},{14... | collective-permute-start | bytes 1572872 | tf_op jit(solution)/shard_map/ppermute | solution.py:521
  360.8 28.5 %collective-permute-start.24 = (bf16[128,2048]{1,0:T(8,128)(2,1)}, bf16[128,2048]{1,0:T(8,128)(2,1)S(1)}, u32[]{:S(2)}, u32[]{:S(2)}) collective-permute-start(bf16[128,2048]{1,0:T(8,128)(2,1)} %get-tuple-element.285), channel_id=1, source_target_pairs={{0,2},{2,4},{4,6},{6,7},{7,5},{5,3},{3,1},{1,0},{8,10},{10,12},{12... | collective-permute-start | bytes 1572872 | tf_op jit(solution)/shard_map/ppermute | solution.py:518
  361.6 28.4 %collective-permute-start.25 = (bf16[128,2048]{1,0:T(8,128)(2,1)}, bf16[128,2048]{1,0:T(8,128)(2,1)}, u32[]{:S(2)}, u32[]{:S(2)}) collective-permute-start(bf16[128,2048]{1,0:T(8,128)(2,1)} %get-tuple-element.286), channel_id=1, source_target_pairs={{2,0},{4,2},{6,4},{7,6},{5,7},{3,5},{1,3},{0,1},{10,8},{12,10},{14... | collective-permute-start | bytes 1572872 | tf_op jit(solution)/shard_map/ppermute | solution.py:521
  408.8 90.0 %reduce-scatter.7.cloned.1.call-start = ((), (), s32[]{:S(2)}) async-start(), calls=%async_computation.11 | async-start | bytes 5242880 | tf_op jit(solution)/shard_map/reduce_scatter | solution.py:645
  468.1 24.6 %all-to-all-start.1 = ((bf16[256,8,256]{2,0,1:T(8,128)(2,1)}), bf16[256,8,256]{2,0,1:T(8,128)(2,1)S(1)}, u32[]{:S(2)}, u32[]{:S(2)}) async-start(bf16[256,8,256]{2,0,1:T(8,128)(2,1)} %bitcast.68), calls=%async_computation.1 | async-start | bytes 2097152 | tf_op jit(solution)/shard_map/all_to_all | solution.py:767
  471.8 101.4 %reduce-scatter.9.cloned.1.call-start = ((), (), s32[]{:S(2)}) async-start(), calls=%async_computation.12 | async-start | bytes 10485760 | tf_op jit(solution)/shard_map/reduce_scatter | solution.py:645
  498.8 198.2 %reduce-scatter.11.cloned.1.call-start = ((), (), s32[]{:S(2)}) async-start(), calls=%async_computation.13 | async-start | bytes 5242880 | tf_op jit(solution)/shard_map/reduce_scatter | solution.py:645
  498.9 25.3 %collective-permute-start.34 = (bf16[256,2048]{1,0:T(8,128)(2,1)}, bf16[256,2048]{1,0:T(8,128)(2,1)}, u32[]{:S(2)}, u32[]{:S(2)}) collective-permute-start(bf16[256,2048]{1,0:T(8,128)(2,1)} %add_convert_fusion.18), channel_id=1, source_target_pairs={{0,2},{2,4},{4,6},{6,7},{7,5},{5,3},{3,1},{1,0},{8,10},{10,12},{12... | collective-permute-start | bytes 3145736 | tf_op jit(solution)/shard_map/ppermute | solution.py:518
  500.4 25.3 %collective-permute-start.35 = (bf16[256,2048]{1,0:T(8,128)(2,1)}, bf16[256,2048]{1,0:T(8,128)(2,1)}, u32[]{:S(2)}, u32[]{:S(2)}) collective-permute-start(bf16[256,2048]{1,0:T(8,128)(2,1)} %add_convert_fusion.17), channel_id=1, source_target_pairs={{2,0},{4,2},{6,4},{7,6},{5,7},{3,5},{1,3},{0,1},{10,8},{12,10},{14... | collective-permute-start | bytes 3145736 | tf_op jit(solution)/shard_map/ppermute | solution.py:521
  545.2 32.4 %collective-permute-start.38 = (bf16[256,2048]{1,0:T(8,128)(2,1)}, bf16[256,2048]{1,0:T(8,128)(2,1)}, u32[]{:S(2)}, u32[]{:S(2)}) collective-permute-start(bf16[256,2048]{1,0:T(8,128)(2,1)} %add_convert_fusion.10), channel_id=1, source_target_pairs={{0,2},{2,4},{4,6},{6,7},{7,5},{5,3},{3,1},{1,0},{8,10},{10,12},{12... | collective-permute-start | bytes 3145736 | tf_op jit(solution)/shard_map/ppermute | solution.py:518
  546.7 31.0 %collective-permute-start.39 = (bf16[256,2048]{1,0:T(8,128)(2,1)}, bf16[256,2048]{1,0:T(8,128)(2,1)}, u32[]{:S(2)}, u32[]{:S(2)}) collective-permute-start(bf16[256,2048]{1,0:T(8,128)(2,1)} %add_convert_fusion.9), channel_id=1, source_target_pairs={{2,0},{4,2},{6,4},{7,6},{5,7},{3,5},{1,3},{0,1},{10,8},{12,10},{14... | collective-permute-start | bytes 3145736 | tf_op jit(solution)/shard_map/ppermute | solution.py:521
  577.7 28.0 %collective-permute-start.40 = (bf16[256,2304]{1,0:T(8,128)(2,1)}, bf16[256,2304]{1,0:T(8,128)(2,1)}, u32[]{:S(2)}, u32[]{:S(2)}) collective-permute-start(bf16[256,2304]{1,0:T(8,128)(2,1)} %pad_maximum_fusion.7), channel_id=1, source_target_pairs={{0,2},{2,4},{4,6},{6,7},{7,5},{5,3},{3,1},{1,0},{8,10},{10,12},{12... | collective-permute-start | bytes 3538952 | tf_op jit(solution)/shard_map/ppermute | solution.py:518
  579.2 27.8 %collective-permute-start.41 = (bf16[256,2304]{1,0:T(8,128)(2,1)}, bf16[256,2304]{1,0:T(8,128)(2,1)}, u32[]{:S(2)}, u32[]{:S(2)}) collective-permute-start(bf16[256,2304]{1,0:T(8,128)(2,1)} %pad_maximum_fusion.8), channel_id=1, source_target_pairs={{2,0},{4,2},{6,4},{7,6},{5,7},{3,5},{1,3},{0,1},{10,8},{12,10},{14... | collective-permute-start | bytes 3538952 | tf_op jit(solution)/shard_map/ppermute | solution.py:521
  613.4 34.4 %collective-permute-start.48 = (bf16[2,512,768]{2,1,0:T(8,128)(2,1)}, bf16[2,512,768]{2,1,0:T(8,128)(2,1)}, u32[]{:S(2)}, u32[]{:S(2)}) collective-permute-start(bf16[2,512,768]{2,1,0:T(8,128)(2,1)} %dynamic-slice_bitcast_fusion), channel_id=1, source_target_pairs={{0,8},{8,0},{16,24},{24,16},{1,9},{9,1},{17,25},{25,17},{2,10},{10... | collective-permute-start | bytes 4718600 | tf_op jit(solution)/shard_map/ppermute | solution.py:631
  613.4 36.4 %collective-permute-start.45 = (bf16[256,2560]{1,0:T(8,128)(2,1)}, bf16[256,2560]{1,0:T(8,128)(2,1)S(1)}, u32[]{:S(2)}, u32[]{:S(2)}) collective-permute-start(bf16[256,2560]{1,0:T(8,128)(2,1)} %pad_maximum_fusion.1), channel_id=1, source_target_pairs={{0,2},{2,4},{4,6},{6,7},{7,5},{5,3},{3,1},{1,0},{8,10},{10,12},{12... | collective-permute-start | bytes 3932168 | tf_op jit(solution)/shard_map/ppermute | solution.py:518
  614.9 34.9 %collective-permute-start.46 = (bf16[256,2560]{1,0:T(8,128)(2,1)}, bf16[256,2560]{1,0:T(8,128)(2,1)S(1)}, u32[]{:S(2)}, u32[]{:S(2)}) collective-permute-start(bf16[256,2560]{1,0:T(8,128)(2,1)} %pad_maximum_fusion.2), channel_id=1, source_target_pairs={{2,0},{4,2},{6,4},{7,6},{5,7},{3,5},{1,3},{0,1},{10,8},{12,10},{14... | collective-permute-start | bytes 3932168 | tf_op jit(solution)/shard_map/ppermute | solution.py:521
  619.8 28.0 %collective-permute-start.47 = (f32[4112]{0:T(1024)S(1)}, f32[4112]{0:T(1024)S(1)}, u32[]{:S(2)}, u32[]{:S(2)}) collective-permute-start(f32[4112]{0:T(1024)S(1)} %add_add_fusion), channel_id=1, source_target_pairs={{0,4},{1,5},{2,6},{3,7},{4,0},{5,1},{6,2},{7,3},{8,12},{9,13},{10,... | collective-permute-start | bytes 49352 | tf_op jit(solution)/shard_map/ppermute | solution.py:621
  650.2 32.4 %collective-permute-start.49 = (bf16[256,2560]{1,0:T(8,128)(2,1)S(1)}, bf16[256,2560]{1,0:T(8,128)(2,1)S(1)}, u32[]{:S(2)}, u32[]{:S(2)}) collective-permute-start(bf16[256,2560]{1,0:T(8,128)(2,1)S(1)} %pad_maximum_fusion.3), channel_id=1, source_target_pairs={{0,2},{2,4},{4,6},{6,7},{7,5},{5,3},{3,1},{1,0},{8,10},{10,12},{12... | collective-permute-start | bytes 3932168 | tf_op jit(solution)/shard_map/ppermute | solution.py:518
  651.5 31.1 %collective-permute-start.50 = (bf16[256,2560]{1,0:T(8,128)(2,1)S(1)}, bf16[256,2560]{1,0:T(8,128)(2,1)S(1)}, u32[]{:S(2)}, u32[]{:S(2)}) collective-permute-start(bf16[256,2560]{1,0:T(8,128)(2,1)S(1)} %pad_maximum_fusion.4), channel_id=1, source_target_pairs={{2,0},{4,2},{6,4},{7,6},{5,7},{3,5},{1,3},{0,1},{10,8},{12,10},{14... | collective-permute-start | bytes 3932168 | tf_op jit(solution)/shard_map/ppermute | solution.py:521
  652.4 29.1 %collective-permute-start.52 = (bf16[1,512,768]{2,1,0:T(8,128)(2,1)S(1)}, bf16[1,512,768]{2,1,0:T(8,128)(2,1)S(1)}, u32[]{:S(2)}, u32[]{:S(2)}) collective-permute-start(bf16[1,512,768]{2,1,0:T(8,128)(2,1)S(1)} %dynamic-slice_bitcast_fusion.1), channel_id=1, source_target_pairs={{0,16},{8,24},{16,0},{24,8},{1,17},{9,25},{17,1},{25,9},{2,18},{10... | collective-permute-start | bytes 2359304 | tf_op jit(solution)/shard_map/ppermute | solution.py:631
  653.3 28.2 %collective-permute-start.51 = (f32[4112]{0:T(1024)S(1)}, f32[4112]{0:T(1024)S(1)}, u32[]{:S(2)}, u32[]{:S(2)}) collective-permute-start(f32[4112]{0:T(1024)S(1)} %add.315), channel_id=1, source_target_pairs={{0,2},{1,3},{2,0},{3,1},{4,6},{5,7},{6,4},{7,5},{8,10},{9,11},{10,... | collective-permute-start | bytes 49352 | tf_op jit(solution)/shard_map/ppermute | solution.py:621
  685.1 30.4 %collective-permute-start.53 = (bf16[256,2560]{1,0:T(8,128)(2,1)}, bf16[256,2560]{1,0:T(8,128)(2,1)}, u32[]{:S(2)}, u32[]{:S(2)}) collective-permute-start(bf16[256,2560]{1,0:T(8,128)(2,1)} %pad_maximum_fusion.5), channel_id=1, source_target_pairs={{0,2},{2,4},{4,6},{6,7},{7,5},{5,3},{3,1},{1,0},{8,10},{10,12},{12... | collective-permute-start | bytes 3932168 | tf_op jit(solution)/shard_map/ppermute | solution.py:518
  685.4 30.1 %collective-permute-start.54 = (bf16[256,2560]{1,0:T(8,128)(2,1)}, bf16[256,2560]{1,0:T(8,128)(2,1)}, u32[]{:S(2)}, u32[]{:S(2)}) collective-permute-start(bf16[256,2560]{1,0:T(8,128)(2,1)} %pad_maximum_fusion.6), channel_id=1, source_target_pairs={{2,0},{4,2},{6,4},{7,6},{5,7},{3,5},{1,3},{0,1},{10,8},{12,10},{14... | collective-permute-start | bytes 3932168 | tf_op jit(solution)/shard_map/ppermute | solution.py:521
  687.1 27.2 %collective-permute-start.55 = (f32[4112]{0:T(1024)S(1)}, f32[4112]{0:T(1024)S(1)}, u32[]{:S(2)}, u32[]{:S(2)}) collective-permute-start(f32[4112]{0:T(1024)S(1)} %add.323), channel_id=1, source_target_pairs={{0,1},{1,0},{2,3},{3,2},{4,5},{5,4},{6,7},{7,6},{8,9},{9,8},{10,11... | collective-permute-start | bytes 49352 | tf_op jit(solution)/shard_map/ppermute | solution.py:621
  (78 other events, 1017.0 us)
Sparse Core Ops, SparseCore 0:
  10.2 31.2 all-gather.4
  44.5 58.5 all-gather.6
  133.8 57.0 all-gather.8
  192.3 34.4 all-gather.10
  408.9 41.4 reduce-scatter.4
  456.5 42.2 reduce-scatter.6
  501.4 71.7 reduce-scatter.8
  579.9 44.5 reduce-scatter.10

commit v5 on v4

--- a/solution.py
+++ b/solution.py
@@ -688,7 +688,7 @@
     f_in = whole(after(f_in, w_in, gather_a.groups[1]), 0)
     kept = []
     for step in range(2, half + 1):
-        gather_a.hop(*kept[1:2])
+        gather_a.hop()
         if step > 2:
             kept = project_blocks(gather_a.groups[step - 2], w_in, step - 2, length, kept)
     kept = project_blocks(gather_a.groups[half - 1], w_in, half - 1, length, kept)

time: 737 us -> 736 us (level)
  transfers between devices with their start and end apart: 65 -> 65, of which waited for: 35 -> 34; matrix products, arithmetic and copies ran while one was open for 24% -> 24% of each run, Pallas kernels for 20% -> 20%
where the time goes in v5:
time: 736 us; the launch traced here: 730 us
  waiting for transfers between devices  265 us (36%)
  Pallas kernels  160 us (22%)
  matrix products  85.5 us (12%)
  starting transfers between devices  63 us (9%)
  other arithmetic  60.2 us (8%)
  local copies, waits for them, and re-layouts  45.4 us (6%)
  blocking collectives  30.1 us (4%)
  between operations  21.3 us (3%)
    ppermute x24, waiting for transfers between devices, forth(): return lax.ppermute(values, 'blk', self.ahead)  146 us
    pallas_call x5, Pallas kernels, feed_blocks(): pl.pallas_call(functools.partial(feed_kernel, count=count), grid=(tiles,)...  95.1 us
    ppermute x3, waiting for transfers between devices, swap_sum(): lax.ppermute(values, axis, [(i, i ^ step) for i in range(size)])  62.1 us
    dot_general x5, matrix products, dot_tn(): lax.dot_general(left, right, (((0,), (0,)), ((), ())), preferred_element_...  55.3 us
    convert_element_type x24, other arithmetic, low(): return values.astype(jnp.bfloat16)  38 us
    ppermute x24, starting transfers between devices, forth(): return lax.ppermute(values, 'blk', self.ahead)  34.7 us
    all_to_all x1, blocking collectives, per_device(): lax.all_to_all(after(merged, gather_c.groups[1]), 'blk', 0, 1, tiled=True)  30.1 us
    reduce_scatter x4, waiting for transfers between devices, sum_over_seq(): lax.psum_scatter(low(values), 'seq', scatter_dimension=dimension, tiled=T...  24.4 us
  transfers between devices with their start and end apart: 65, of which 34 were waited for; matrix products, arithmetic and copies ran while one was open for 24% of the time, Pallas kernels for 20%

profile of v5, /device:TPU:0, one launch (start us, length us, event | category | flops | bytes accessed | tf_op | source)
XLA Modules:
  0.0 729.7 jit_solution(591494641928444519)
XLA Ops:
  11.0 3.1 collective-permute-start
  14.1 4.5 reshape.143
  18.5 24.3 %collective-permute-done.refs_0_ = bf16[256,2560]{1,0:T(8,128)(2,1)} collective-permute-done((bf16[256,2560]{1,0:T(8,128)(2,1)S(1)}, bf16[256,2560]{1,0:T(8,128)(2,1)}, u32[]{:S(2)}, u32[]{:S(2)}) %collective-permute-start) | collective-permute-done | bytes 1310752 | tf_op jit(solution)/shard_map/ppermute | solution.py:518
  47.1 26.9 %collective-permute-done.2.refs_0_ = bf16[256,2560]{1,0:T(8,128)(2,1)S(1)} collective-permute-done((bf16[256,2560]{1,0:T(8,128)(2,1)}, bf16[256,2560]{1,0:T(8,128)(2,1)S(1)}, u32[]{:S(2)}, u32[]{:S(2)}) %collective-permute-start.2) | collective-permute-done | bytes 1310752 | tf_op jit(solution)/shard_map/ppermute | solution.py:518
  93.5 10.3 %collective-permute-done.4.refs_0_ = bf16[256,2560]{1,0:T(8,128)(2,1)S(1)} collective-permute-done((bf16[256,2560]{1,0:T(8,128)(2,1)}, bf16[256,2560]{1,0:T(8,128)(2,1)S(1)}, u32[]{:S(2)}, u32[]{:S(2)}) %collective-permute-start.4) | collective-permute-done | bytes 1310752 | tf_op jit(solution)/shard_map/ppermute | solution.py:518
  112.5 5.7 shard_map.230
  118.2 5.7 shard_map.231
  123.9 5.7 shard_map.232
  137.3 6.3 shard_map.233
  143.6 13.4 %shard_map.234 = (bf16[2048,256]{1,0:T(8,128)(2,1)}, f32[2048,256]{1,0:T(8,128)}, f32[4,2,512]{2,1,0:T(2,128)}, f32[2,2,128,128]{3,2,1,0:T(8,128)}, f32[2,2,128]...) custom-call(s32[8]{0:T(128)} %gather_fusion, s32[1]{0:T(128)} %bitcast.69.splits, f32[2]{0:T(128)} %add_divide_fusion.mix, ...), custom_call_target="tpu_custom_call" | custom-call | flops 4000000000 | bytes 4096 | tf_op jit(solution)/shard_map/pallas_call | solution.py:298
  158.5 30.1 %all_to_all.38 = bf16[8,256,256]{1,2,0:T(8,128)(2,1)} all-to-all(bf16[8,256,256]{1,2,0:T(8,128)(2,1)S(1)} %copy.59), channel_id=1, replica_groups=mesh['seq'=4,'blk'=8] {'blk'}, dimensions={0} | all-to-all | bytes 2097152 | tf_op jit(solution)/shard_map/all_to_all | solution.py:709
  191.9 6.2 multiply_reduce_fusion.3
  198.4 17.2 %collective-permute-done.10.refs_2_ = bf16[256,2048]{1,0:T(8,128)(2,1)} collective-permute-done((bf16[256,2048]{1,0:T(8,128)(2,1)}, bf16[256,2048]{1,0:T(8,128)(2,1)}, u32[]{:S(2)}, u32[]{:S(2)}) %collective-permute-start.10) | collective-permute-done | bytes 1048608 | tf_op jit(solution)/shard_map/ppermute | solution.py:518
  218.8 22.2 %collective-permute-done.12.refs_0_ = bf16[256,2048]{1,0:T(8,128)(2,1)S(1)} collective-permute-done((bf16[256,2048]{1,0:T(8,128)(2,1)S(1)}, bf16[256,2048]{1,0:T(8,128)(2,1)S(1)}, u32[]{:S(2)}, u32[]{:S(2)}) %collective-permute-start.12) | collective-permute-done | bytes 1048608 | tf_op jit(solution)/shard_map/ppermute | solution.py:518
  245.2 13.4 %shard_map.235 = (bf16[2048,2048]{1,0:T(8,128)(2,1)}, bf16[2048,2048]{1,0:T(8,128)(2,1)}, bf16[2048,1024]{1,0:T(8,128)(2,1)}, bf16[2048,1024]{1,0:T(8,128)(2,1)}...) custom-call(bf16[256,2048]{1,0:T(8,128)(2,1)} %copy-done.40, ...), custom_call_target="tpu_custom_call" | custom-call | flops 4000000000 | bytes 4096 | tf_op jit(solution)/shard_map/pallas_call | solution.py:467
  258.5 7.8 %collective-permute-done.14.refs_2_ = bf16[256,2048]{1,0:T(8,128)(2,1)S(1)} collective-permute-done((bf16[256,2048]{1,0:T(8,128)(2,1)}, bf16[256,2048]{1,0:T(8,128)(2,1)S(1)}, u32[]{:S(2)}, u32[]{:S(2)}) %collective-permute-start.14) | collective-permute-done | bytes 1048608 | tf_op jit(solution)/shard_map/ppermute | solution.py:518
  269.9 22.8 %shard_map.236 = (bf16[2048,2048]{1,0:T(8,128)(2,1)}, bf16[2048,2048]{1,0:T(8,128)(2,1)}, bf16[2048,1024]{1,0:T(8,128)(2,1)}, bf16[2048,1024]{1,0:T(8,128)(2,1)}...) custom-call(bf16[256,2048]{1,0:T(8,128)(2,1)} %copy-done.32, ...), custom_call_target="tpu_custom_call", output_to_operand_aliasing={{0}: (6, {}), {1}: (7, {}), {2}: (8, {}), {3}: (9, {}), {4}... | custom-call | flops 4000000000 | bytes 4096 | tf_op jit(solution)/shard_map/pallas_call | solution.py:467
  296.0 6.9 collective-permute-done.18.refs_2_
  302.9 2.8 collective-permute-done.19.refs_3_
  308.4 22.8 %shard_map.237 = (bf16[2048,2048]{1,0:T(8,128)(2,1)}, bf16[2048,2048]{1,0:T(8,128)(2,1)}, bf16[2048,1024]{1,0:T(8,128)(2,1)}, bf16[2048,1024]{1,0:T(8,128)(2,1)}...) custom-call(bf16[256,2048]{1,0:T(8,128)(2,1)} %collective-permute-do, ...), custom_call_target="tpu_custom_call", output_to_operand_aliasing={{0}: (6, {}), {1}: (7, {}), {2}: (8, {}), {3}: (9, {}), {4}... | custom-call | flops 4000000000 | bytes 4096 | tf_op jit(solution)/shard_map/pallas_call | solution.py:467
  334.9 5.6 collective-permute-done.22.refs_0_
  340.5 3.7 collective-permute-done.23.refs_1_
  344.1 13.4 %shard_map.238 = (bf16[2048,2048]{1,0:T(8,128)(2,1)}, bf16[2048,2048]{1,0:T(8,128)(2,1)}, bf16[2048,1024]{1,0:T(8,128)(2,1)}, bf16[2048,1024]{1,0:T(8,128)(2,1)}...) custom-call(bf16[128,2048]{1,0:T(8,128)(2,1)} %copy-done.50, ...), custom_call_target="tpu_custom_call", output_to_operand_aliasing={{0}: (6, {}), {1}: (7, {}), {2}: (8, {}), {3}: (9, {}), {4}... | custom-call | flops 4000000000 | bytes 4096 | tf_op jit(solution)/shard_map/pallas_call | solution.py:467
  361.6 22.7 %shard_map.239 = (bf16[2048,2048]{1,0:T(8,128)(2,1)}, bf16[2048,2048]{1,0:T(8,128)(2,1)}, bf16[2048,1024]{1,0:T(8,128)(2,1)}, bf16[2048,1024]{1,0:T(8,128)(2,1)}...) custom-call(bf16[256,2048]{1,0:T(8,128)(2,1)} %copy-done.24, ...), custom_call_target="tpu_custom_call", output_to_operand_aliasing={{0}: (6, {}), {1}: (7, {}), {2}: (8, {}), {3}: (9, {}), {4}... | custom-call | flops 4000000000 | bytes 4096 | tf_op jit(solution)/shard_map/pallas_call | solution.py:467
  391.1 13.1 %convolution_convert_fusion.1 = bf16[1024,2048]{1,0:T(8,128)(2,1)} fusion(bf16[2048,1024]{1,0:T(8,128)(2,1)S(1)} %copy-done.6, bf16[2048,2048]{1,0:T(8,128)(2,1)} %get-tuple-element.305), kind=kOutput, calls=%fused_computation.4 | convolution fusion | flops 8592031744 | bytes 16777216 | tf_op jit(solution)/shard_map/dot_general | solution.py:29
  407.7 3.1 add_convert_fusion.13
  414.2 13.1 %convolution_convert_fusion.3 = bf16[2048,1024]{1,0:T(8,128)(2,1)} fusion(bf16[2048,2048]{1,0:T(8,128)(2,1)} %get-tuple-element.313, bf16[2048,1024]{1,0:T(8,128)(2,1)S(1)} %copy-done.7), kind=kOutput, calls=%fused_computation.6 | convolution fusion | flops 8592031744 | bytes 16777216 | tf_op jit(solution)/shard_map/dot_general | solution.py:29
  430.5 3.1 add_convert_fusion.11
  438.3 12.9 %convolution_convert_fusion.2 = bf16[2048,1024]{1,0:T(8,128)(2,1)} fusion(bf16[2048,2048]{1,0:T(8,128)(2,1)} %get-tuple-element.313, bf16[2048,1024]{1,0:T(8,128)(2,1)S(1)} %copy-done.8), kind=kOutput, calls=%fused_computation.5 | convolution fusion | flops 8592031744 | bytes 16777216 | tf_op jit(solution)/shard_map/dot_general | solution.py:29
  451.6 3.5 multiply_reduce_fusion.1
  458.6 7.2 convolution_convert_fusion.11
  466.9 3.7 all-to-all-start.1
  474.3 5.7 convolution_convert_fusion
  480.0 11.5 %all-to-all-done.1 = bf16[256,8,256]{2,0,1:T(8,128)(2,1)S(1)} async-done(((bf16[256,8,256]{2,0,1:T(8,128)(2,1)}), bf16[256,8,256]{2,0,1:T(8,128)(2,1)S(1)}, u32[]{:S(2)}, u32[]{:S(2)}) %all-to-all-start.1) | async-done | bytes 1048608 | tf_op jit(solution)/shard_map/all_to_all | solution.py:767
  491.5 6.1 reduce-scatter.7.cloned.1.call-done.refs_0_
  500.2 19.2 %shard_map.240 = (bf16[2048,768]{1,0:T(8,128)(2,1)}, f32[2,128]{1,0:T(2,128)}) custom-call(s32[8]{0:T(128)} %gather_fusion, s32[1]{0:T(128)} %bitcast.70.splits, f32[2]{0:T(128)} %add_divide_fusion.mix, bf16[2048,768]{1,0:T(8,128)(2,1)} %get-tuple-element.228.proj, bf16[2048,256]{1,0:T(8,128)(2,1)} %bitcast.79, f32[2048,256]{1,0:T(8,128)} %get-tuple-element.333.attended, ...), custom_call_target="tpu_custom_call" | custom-call | flops 4000000000 | bytes 4096 | tf_op jit(solution)/shard_map/pallas_call | solution.py:319
  520.3 2.6 collective-permute-done.34
  536.1 6.3 collective-permute-done.36
  553.7 18.3 %reduce-scatter.9.cloned.1.call-done = bf16[2048,512]{1,0:T(8,128)(2,1)} async-done(((bf16[2048,2048]{1,0:T(8,128)(2,1)}), bf16[2048,512]{1,0:T(8,128)(2,1)}) %reduce-scatter.9.cloned.1.call-update) | async-done | bytes 2097168 | tf_op jit(solution)/shard_map/reduce_scatter | solution.py:645
  578.6 10.6 %multiply_reduce_fusion = (f32[2048]{0:T(1024)S(1)}, bf16[2048,768]{1,0:T(8,128)(2,1)S(1)}) fusion(bf16[2048,768]{1,0:T(8,128)(2,1)S(1)} %copy-done.2, bf16[2048,2048]{1,0:T(8,128)(2,1)} %get-tuple-element.365, bf16[2048,768]{1,0:T(8,128)(2,1)} %get-tuple-element.366), kind=kOutput, calls=%fused_computation.3 | convolution fusion | flops 6450313216 | bytes 17833984 | tf_op jit(solution)/shard_map/dot_general | solution.py:29
  593.5 11.0 %collective-permute-done.40 = bf16[256,2304]{1,0:T(8,128)(2,1)} collective-permute-done((bf16[256,2304]{1,0:T(8,128)(2,1)}, bf16[256,2304]{1,0:T(8,128)(2,1)}, u32[]{:S(2)}, u32[]{:S(2)}) %collective-permute-start.40) | collective-permute-done | bytes 1179680 | tf_op jit(solution)/shard_map/ppermute | solution.py:518
  623.6 23.0 %collective-permute-done.47 = f32[4112]{0:T(1024)S(1)} collective-permute-done((f32[4112]{0:T(1024)S(1)}, f32[4112]{0:T(1024)S(1)}, u32[]{:S(2)}, u32[]{:S(2)}) %collective-permute-start.47) | collective-permute-done | bytes 16480 | tf_op jit(solution)/shard_map/ppermute | solution.py:621
  653.8 26.5 %collective-permute-done.51 = f32[4112]{0:T(1024)S(1)} collective-permute-done((f32[4112]{0:T(1024)S(1)}, f32[4112]{0:T(1024)S(1)}, u32[]{:S(2)}, u32[]{:S(2)}) %collective-permute-start.51) | collective-permute-done | bytes 16480 | tf_op jit(solution)/shard_map/ppermute | solution.py:621
  689.1 3.7 shard_map.242
  692.8 3.0 copy.63
  695.8 4.7 shard_map.241
  700.6 12.6 %collective-permute-done.55 = f32[4112]{0:T(1024)S(1)} collective-permute-done((f32[4112]{0:T(1024)S(1)}, f32[4112]{0:T(1024)S(1)}, u32[]{:S(2)}, u32[]{:S(2)}) %collective-permute-start.55) | collective-permute-done | bytes 16480 | tf_op jit(solution)/shard_map/ppermute | solution.py:621
  714.3 3.4 fusion.7
  (332 shorter events, 177.1 us)
Async XLA Ops:
  7.2 37.2 %all-gather.5.cloned.1.call-start = ((), (), s32[]{:S(2)}) async-start(), calls=%async_computation.6 | async-start | bytes 3932160 | tf_op jit(solution)/shard_map/all_gather | solution.py:671
  9.9 122.0 %all-gather.7.cloned.1.call-start = ((), (), s32[]{:S(2)}) async-start(), calls=%async_computation.7 | async-start | bytes 10485760 | tf_op jit(solution)/shard_map/all_gather | solution.py:671
  11.0 31.9 %collective-permute-start = (bf16[256,2560]{1,0:T(8,128)(2,1)S(1)}, bf16[256,2560]{1,0:T(8,128)(2,1)}, u32[]{:S(2)}, u32[]{:S(2)}) collective-permute-start(bf16[256,2560]{1,0:T(8,128)(2,1)S(1)} %pad_maximum_fusion.refs_0_), channel_id=1, source_target_pairs={{0,2},{2,4},{4,6},{6,7},{7,5},{5,3},{3,1},{1,0},{8,10},{10,12},{12... | collective-permute-start | bytes 3932168 | tf_op jit(solution)/shard_map/ppermute | solution.py:518
  14.0 30.3 %collective-permute-start.1 = (bf16[256,2560]{1,0:T(8,128)(2,1)S(1)}, bf16[256,2560]{1,0:T(8,128)(2,1)}, u32[]{:S(2)}, u32[]{:S(2)}) collective-permute-start(bf16[256,2560]{1,0:T(8,128)(2,1)S(1)} %pad_maximum_fusion.refs_0_), channel_id=1, source_target_pairs={{2,0},{4,2},{6,4},{7,6},{5,7},{3,5},{1,3},{0,1},{10,8},{12,10},{14... | collective-permute-start | bytes 3932168 | tf_op jit(solution)/shard_map/ppermute | solution.py:521
  44.4 145.3 %all-gather.9.cloned.1.call-start = ((), (), s32[]{:S(2)}) async-start(), calls=%async_computation.8 | async-start | bytes 10485760 | tf_op jit(solution)/shard_map/all_gather | solution.py:671
  44.5 29.6 %collective-permute-start.2 = (bf16[256,2560]{1,0:T(8,128)(2,1)}, bf16[256,2560]{1,0:T(8,128)(2,1)S(1)}, u32[]{:S(2)}, u32[]{:S(2)}) collective-permute-start(bf16[256,2560]{1,0:T(8,128)(2,1)} %collective-permute-done.refs_0_), channel_id=1, source_target_pairs={{0,2},{2,4},{4,6},{6,7},{7,5},{5,3},{3,1},{1,0},{8,10},{10,12},{12... | collective-permute-start | bytes 3932168 | tf_op jit(solution)/shard_map/ppermute | solution.py:518
  46.1 29.4 %collective-permute-start.3 = (bf16[256,2560]{1,0:T(8,128)(2,1)}, bf16[256,2560]{1,0:T(8,128)(2,1)}, u32[]{:S(2)}, u32[]{:S(2)}) collective-permute-start(bf16[256,2560]{1,0:T(8,128)(2,1)} %collective-permute-done.1.refs_1_), channel_id=1, source_target_pairs={{2,0},{4,2},{6,4},{7,6},{5,7},{3,5},{1,3},{0,1},{10,8},{12,10},{14... | collective-permute-start | bytes 3932168 | tf_op jit(solution)/shard_map/ppermute | solution.py:521
  75.4 28.4 %collective-permute-start.4 = (bf16[256,2560]{1,0:T(8,128)(2,1)}, bf16[256,2560]{1,0:T(8,128)(2,1)S(1)}, u32[]{:S(2)}, u32[]{:S(2)}) collective-permute-start(bf16[256,2560]{1,0:T(8,128)(2,1)} %copy-done.26), channel_id=1, source_target_pairs={{0,2},{2,4},{4,6},{6,7},{7,5},{5,3},{3,1},{1,0},{8,10},{10,12},{12... | collective-permute-start | bytes 3932168 | tf_op jit(solution)/shard_map/ppermute | solution.py:518
  77.0 28.2 %collective-permute-start.5 = (bf16[256,2560]{1,0:T(8,128)(2,1)}, bf16[256,2560]{1,0:T(8,128)(2,1)}, u32[]{:S(2)}, u32[]{:S(2)}) collective-permute-start(bf16[256,2560]{1,0:T(8,128)(2,1)} %collective-permute-done.3.refs_1_), channel_id=1, source_target_pairs={{2,0},{4,2},{6,4},{7,6},{5,7},{3,5},{1,3},{0,1},{10,8},{12,10},{14... | collective-permute-start | bytes 3932168 | tf_op jit(solution)/shard_map/ppermute | solution.py:521
  106.1 23.5 %collective-permute-start.6 = (bf16[128,2560]{1,0:T(8,128)(2,1)}, bf16[128,2560]{1,0:T(8,128)(2,1)S(1)}, u32[]{:S(2)}, u32[]{:S(2)}) collective-permute-start(bf16[128,2560]{1,0:T(8,128)(2,1)} %slice.168), channel_id=1, source_target_pairs={{0,2},{2,4},{4,6},{6,7},{7,5},{5,3},{3,1},{1,0},{8,10},{10,12},{12... | collective-permute-start | bytes 1966088 | tf_op jit(solution)/shard_map/ppermute | solution.py:518
  131.9 113.3 %all-gather.11.cloned.1.call-start = ((), (), s32[]{:S(2)}) async-start(), calls=%async_computation.9 | async-start | bytes 5242880 | tf_op jit(solution)/shard_map/all_gather | solution.py:671
  132.0 25.0 %collective-permute-start.8 = (bf16[256,2048]{1,0:T(8,128)(2,1)S(1)}, bf16[256,2048]{1,0:T(8,128)(2,1)}, u32[]{:S(2)}, u32[]{:S(2)}) collective-permute-start(bf16[256,2048]{1,0:T(8,128)(2,1)S(1)} %copy-done.15), channel_id=1, source_target_pairs={{0,2},{2,4},{4,6},{6,7},{7,5},{5,3},{3,1},{1,0},{8,10},{10,12},{12... | collective-permute-start | bytes 3145736 | tf_op jit(solution)/shard_map/ppermute | solution.py:518
  133.6 23.4 %collective-permute-start.9 = (bf16[256,2048]{1,0:T(8,128)(2,1)S(1)}, bf16[256,2048]{1,0:T(8,128)(2,1)}, u32[]{:S(2)}, u32[]{:S(2)}) collective-permute-start(bf16[256,2048]{1,0:T(8,128)(2,1)S(1)} %copy-done.15), channel_id=1, source_target_pairs={{2,0},{4,2},{6,4},{7,6},{5,7},{3,5},{1,3},{0,1},{10,8},{12,10},{14... | collective-permute-start | bytes 3145736 | tf_op jit(solution)/shard_map/ppermute | solution.py:521
  189.8 265.4 %reduce-scatter.5.cloned.1.call-start = ((), (), s32[]{:S(2)}) async-start(), calls=%async_computation.10 | async-start | bytes 5242880 | tf_op jit(solution)/shard_map/reduce_scatter | solution.py:645
  189.8 25.7 %collective-permute-start.10 = (bf16[256,2048]{1,0:T(8,128)(2,1)}, bf16[256,2048]{1,0:T(8,128)(2,1)}, u32[]{:S(2)}, u32[]{:S(2)}) collective-permute-start(bf16[256,2048]{1,0:T(8,128)(2,1)} %collective-permute-done.8.refs_2_), channel_id=1, source_target_pairs={{0,2},{2,4},{4,6},{6,7},{7,5},{5,3},{3,1},{1,0},{8,10},{10,12},{12... | collective-permute-start | bytes 3145736 | tf_op jit(solution)/shard_map/ppermute | solution.py:518
  191.4 25.4 %collective-permute-start.11 = (bf16[256,2048]{1,0:T(8,128)(2,1)}, bf16[256,2048]{1,0:T(8,128)(2,1)}, u32[]{:S(2)}, u32[]{:S(2)}) collective-permute-start(bf16[256,2048]{1,0:T(8,128)(2,1)} %collective-permute-done.9.refs_3_), channel_id=1, source_target_pairs={{2,0},{4,2},{6,4},{7,6},{5,7},{3,5},{1,3},{0,1},{10,8},{12,10},{14... | collective-permute-start | bytes 3145736 | tf_op jit(solution)/shard_map/ppermute | solution.py:521
  216.7 24.2 %collective-permute-start.12 = (bf16[256,2048]{1,0:T(8,128)(2,1)S(1)}, bf16[256,2048]{1,0:T(8,128)(2,1)S(1)}, u32[]{:S(2)}, u32[]{:S(2)}) collective-permute-start(bf16[256,2048]{1,0:T(8,128)(2,1)S(1)} %multiply_convert_fusion.refs_0_), channel_id=1, source_target_pairs={{0,2},{2,4},{4,6},{6,7},{7,5},{5,3},{3,1},{1,0},{8,10},{10,12},{12... | collective-permute-start | bytes 3145736 | tf_op jit(solution)/shard_map/ppermute | solution.py:518
  218.2 23.9 %collective-permute-start.13 = (bf16[256,2048]{1,0:T(8,128)(2,1)S(1)}, bf16[256,2048]{1,0:T(8,128)(2,1)S(1)}, u32[]{:S(2)}, u32[]{:S(2)}) collective-permute-start(bf16[256,2048]{1,0:T(8,128)(2,1)S(1)} %multiply_convert_fusion.refs_0_), channel_id=1, source_target_pairs={{2,0},{4,2},{6,4},{7,6},{5,7},{3,5},{1,3},{0,1},{10,8},{12,10},{14... | collective-permute-start | bytes 3145736 | tf_op jit(solution)/shard_map/ppermute | solution.py:521
  243.1 23.3 %collective-permute-start.14 = (bf16[256,2048]{1,0:T(8,128)(2,1)}, bf16[256,2048]{1,0:T(8,128)(2,1)S(1)}, u32[]{:S(2)}, u32[]{:S(2)}) collective-permute-start(bf16[256,2048]{1,0:T(8,128)(2,1)} %collective-permute-done.10.refs_2_), channel_id=1, source_target_pairs={{0,2},{2,4},{4,6},{6,7},{7,5},{5,3},{3,1},{1,0},{8,10},{10,12},{12... | collective-permute-start | bytes 3145736 | tf_op jit(solution)/shard_map/ppermute | solution.py:518
  244.6 23.1 %collective-permute-start.15 = (bf16[256,2048]{1,0:T(8,128)(2,1)}, bf16[256,2048]{1,0:T(8,128)(2,1)}, u32[]{:S(2)}, u32[]{:S(2)}) collective-permute-start(bf16[256,2048]{1,0:T(8,128)(2,1)} %collective-permute-done.11.refs_3_), channel_id=1, source_target_pairs={{2,0},{4,2},{6,4},{7,6},{5,7},{3,5},{1,3},{0,1},{10,8},{12,10},{14... | collective-permute-start | bytes 3145736 | tf_op jit(solution)/shard_map/ppermute | solution.py:521
  267.7 25.1 %collective-permute-start.16 = (bf16[256,2048]{1,0:T(8,128)(2,1)}, bf16[256,2048]{1,0:T(8,128)(2,1)}, u32[]{:S(2)}, u32[]{:S(2)}) collective-permute-start(bf16[256,2048]{1,0:T(8,128)(2,1)} %copy-done.32), channel_id=1, source_target_pairs={{0,2},{2,4},{4,6},{6,7},{7,5},{5,3},{3,1},{1,0},{8,10},{10,12},{12... | collective-permute-start | bytes 3145736 | tf_op jit(solution)/shard_map/ppermute | solution.py:518
  269.4 23.4 %collective-permute-start.17 = (bf16[256,2048]{1,0:T(8,128)(2,1)}, bf16[256,2048]{1,0:T(8,128)(2,1)}, u32[]{:S(2)}, u32[]{:S(2)}) collective-permute-start(bf16[256,2048]{1,0:T(8,128)(2,1)} %copy-done.33), channel_id=1, source_target_pairs={{2,0},{4,2},{6,4},{7,6},{5,7},{3,5},{1,3},{0,1},{10,8},{12,10},{14... | collective-permute-start | bytes 3145736 | tf_op jit(solution)/shard_map/ppermute | solution.py:521
  305.8 25.4 %collective-permute-start.20 = (bf16[256,2048]{1,0:T(8,128)(2,1)}, bf16[256,2048]{1,0:T(8,128)(2,1)S(1)}, u32[]{:S(2)}, u32[]{:S(2)}) collective-permute-start(bf16[256,2048]{1,0:T(8,128)(2,1)} %collective-permute-done.16.refs_0_), channel_id=1, source_target_pairs={{0,2},{2,4},{4,6},{6,7},{7,5},{5,3},{3,1},{1,0},{8,10},{10,12},{12... | collective-permute-start | bytes 3145736 | tf_op jit(solution)/shard_map/ppermute | solution.py:518
  357.5 26.9 %collective-permute-start.26 = (bf16[128,2048]{1,0:T(8,128)(2,1)}, bf16[128,2048]{1,0:T(8,128)(2,1)S(1)}, u32[]{:S(2)}, u32[]{:S(2)}) collective-permute-start(bf16[128,2048]{1,0:T(8,128)(2,1)} %get-tuple-element.283), channel_id=1, source_target_pairs={{0,2},{2,4},{4,6},{6,7},{7,5},{5,3},{3,1},{1,0},{8,10},{10,12},{12... | collective-permute-start | bytes 1572872 | tf_op jit(solution)/shard_map/ppermute | solution.py:518
  358.4 26.0 %collective-permute-start.27 = (bf16[128,2048]{1,0:T(8,128)(2,1)}, bf16[128,2048]{1,0:T(8,128)(2,1)S(1)}, u32[]{:S(2)}, u32[]{:S(2)}) collective-permute-start(bf16[128,2048]{1,0:T(8,128)(2,1)} %get-tuple-element.284), channel_id=1, source_target_pairs={{2,0},{4,2},{6,4},{7,6},{5,7},{3,5},{1,3},{0,1},{10,8},{12,10},{14... | collective-permute-start | bytes 1572872 | tf_op jit(solution)/shard_map/ppermute | solution.py:521
  359.6 28.5 %collective-permute-start.24 = (bf16[128,2048]{1,0:T(8,128)(2,1)}, bf16[128,2048]{1,0:T(8,128)(2,1)S(1)}, u32[]{:S(2)}, u32[]{:S(2)}) collective-permute-start(bf16[128,2048]{1,0:T(8,128)(2,1)} %get-tuple-element.285), channel_id=1, source_target_pairs={{0,2},{2,4},{4,6},{6,7},{7,5},{5,3},{3,1},{1,0},{8,10},{10,12},{12... | collective-permute-start | bytes 1572872 | tf_op jit(solution)/shard_map/ppermute | solution.py:518
  360.4 28.5 %collective-permute-start.25 = (bf16[128,2048]{1,0:T(8,128)(2,1)}, bf16[128,2048]{1,0:T(8,128)(2,1)}, u32[]{:S(2)}, u32[]{:S(2)}) collective-permute-start(bf16[128,2048]{1,0:T(8,128)(2,1)} %get-tuple-element.286), channel_id=1, source_target_pairs={{2,0},{4,2},{6,4},{7,6},{5,7},{3,5},{1,3},{0,1},{10,8},{12,10},{14... | collective-permute-start | bytes 1572872 | tf_op jit(solution)/shard_map/ppermute | solution.py:521
  407.6 90.0 %reduce-scatter.7.cloned.1.call-start = ((), (), s32[]{:S(2)}) async-start(), calls=%async_computation.11 | async-start | bytes 5242880 | tf_op jit(solution)/shard_map/reduce_scatter | solution.py:645
  466.9 24.6 %all-to-all-start.1 = ((bf16[256,8,256]{2,0,1:T(8,128)(2,1)}), bf16[256,8,256]{2,0,1:T(8,128)(2,1)S(1)}, u32[]{:S(2)}, u32[]{:S(2)}) async-start(bf16[256,8,256]{2,0,1:T(8,128)(2,1)} %bitcast.68), calls=%async_computation.1 | async-start | bytes 2097152 | tf_op jit(solution)/shard_map/all_to_all | solution.py:767
  470.6 101.4 %reduce-scatter.9.cloned.1.call-start = ((), (), s32[]{:S(2)}) async-start(), calls=%async_computation.12 | async-start | bytes 10485760 | tf_op jit(solution)/shard_map/reduce_scatter | solution.py:645
  497.7 198.2 %reduce-scatter.11.cloned.1.call-start = ((), (), s32[]{:S(2)}) async-start(), calls=%async_computation.13 | async-start | bytes 5242880 | tf_op jit(solution)/shard_map/reduce_scatter | solution.py:645
  497.7 25.3 %collective-permute-start.34 = (bf16[256,2048]{1,0:T(8,128)(2,1)}, bf16[256,2048]{1,0:T(8,128)(2,1)}, u32[]{:S(2)}, u32[]{:S(2)}) collective-permute-start(bf16[256,2048]{1,0:T(8,128)(2,1)} %add_convert_fusion.18), channel_id=1, source_target_pairs={{0,2},{2,4},{4,6},{6,7},{7,5},{5,3},{3,1},{1,0},{8,10},{10,12},{12... | collective-permute-start | bytes 3145736 | tf_op jit(solution)/shard_map/ppermute | solution.py:518
  499.3 25.3 %collective-permute-start.35 = (bf16[256,2048]{1,0:T(8,128)(2,1)}, bf16[256,2048]{1,0:T(8,128)(2,1)}, u32[]{:S(2)}, u32[]{:S(2)}) collective-permute-start(bf16[256,2048]{1,0:T(8,128)(2,1)} %add_convert_fusion.17), channel_id=1, source_target_pairs={{2,0},{4,2},{6,4},{7,6},{5,7},{3,5},{1,3},{0,1},{10,8},{12,10},{14... | collective-permute-start | bytes 3145736 | tf_op jit(solution)/shard_map/ppermute | solution.py:521
  546.5 30.0 %collective-permute-start.38 = (bf16[256,2048]{1,0:T(8,128)(2,1)}, bf16[256,2048]{1,0:T(8,128)(2,1)}, u32[]{:S(2)}, u32[]{:S(2)}) collective-permute-start(bf16[256,2048]{1,0:T(8,128)(2,1)} %add_convert_fusion.10), channel_id=1, source_target_pairs={{0,2},{2,4},{4,6},{6,7},{7,5},{5,3},{3,1},{1,0},{8,10},{10,12},{12... | collective-permute-start | bytes 3145736 | tf_op jit(solution)/shard_map/ppermute | solution.py:518
  548.0 28.5 %collective-permute-start.39 = (bf16[256,2048]{1,0:T(8,128)(2,1)}, bf16[256,2048]{1,0:T(8,128)(2,1)}, u32[]{:S(2)}, u32[]{:S(2)}) collective-permute-start(bf16[256,2048]{1,0:T(8,128)(2,1)} %add_convert_fusion.9), channel_id=1, source_target_pairs={{2,0},{4,2},{6,4},{7,6},{5,7},{3,5},{1,3},{0,1},{10,8},{12,10},{14... | collective-permute-start | bytes 3145736 | tf_op jit(solution)/shard_map/ppermute | solution.py:521
  576.5 28.0 %collective-permute-start.40 = (bf16[256,2304]{1,0:T(8,128)(2,1)}, bf16[256,2304]{1,0:T(8,128)(2,1)}, u32[]{:S(2)}, u32[]{:S(2)}) collective-permute-start(bf16[256,2304]{1,0:T(8,128)(2,1)} %pad_maximum_fusion.7), channel_id=1, source_target_pairs={{0,2},{2,4},{4,6},{6,7},{7,5},{5,3},{3,1},{1,0},{8,10},{10,12},{12... | collective-permute-start | bytes 3538952 | tf_op jit(solution)/shard_map/ppermute | solution.py:518
  578.0 27.8 %collective-permute-start.41 = (bf16[256,2304]{1,0:T(8,128)(2,1)}, bf16[256,2304]{1,0:T(8,128)(2,1)}, u32[]{:S(2)}, u32[]{:S(2)}) collective-permute-start(bf16[256,2304]{1,0:T(8,128)(2,1)} %pad_maximum_fusion.8), channel_id=1, source_target_pairs={{2,0},{4,2},{6,4},{7,6},{5,7},{3,5},{1,3},{0,1},{10,8},{12,10},{14... | collective-permute-start | bytes 3538952 | tf_op jit(solution)/shard_map/ppermute | solution.py:521
  612.3 34.4 %collective-permute-start.48 = (bf16[2,512,768]{2,1,0:T(8,128)(2,1)}, bf16[2,512,768]{2,1,0:T(8,128)(2,1)}, u32[]{:S(2)}, u32[]{:S(2)}) collective-permute-start(bf16[2,512,768]{2,1,0:T(8,128)(2,1)} %dynamic-slice_bitcast_fusion), channel_id=1, source_target_pairs={{0,8},{8,0},{16,24},{24,16},{1,9},{9,1},{17,25},{25,17},{2,10},{10... | collective-permute-start | bytes 4718600 | tf_op jit(solution)/shard_map/ppermute | solution.py:631
  612.3 36.4 %collective-permute-start.45 = (bf16[256,2560]{1,0:T(8,128)(2,1)}, bf16[256,2560]{1,0:T(8,128)(2,1)S(1)}, u32[]{:S(2)}, u32[]{:S(2)}) collective-permute-start(bf16[256,2560]{1,0:T(8,128)(2,1)} %pad_maximum_fusion.1), channel_id=1, source_target_pairs={{0,2},{2,4},{4,6},{6,7},{7,5},{5,3},{3,1},{1,0},{8,10},{10,12},{12... | collective-permute-start | bytes 3932168 | tf_op jit(solution)/shard_map/ppermute | solution.py:518
  613.7 34.9 %collective-permute-start.46 = (bf16[256,2560]{1,0:T(8,128)(2,1)}, bf16[256,2560]{1,0:T(8,128)(2,1)S(1)}, u32[]{:S(2)}, u32[]{:S(2)}) collective-permute-start(bf16[256,2560]{1,0:T(8,128)(2,1)} %pad_maximum_fusion.2), channel_id=1, source_target_pairs={{2,0},{4,2},{6,4},{7,6},{5,7},{3,5},{1,3},{0,1},{10,8},{12,10},{14... | collective-permute-start | bytes 3932168 | tf_op jit(solution)/shard_map/ppermute | solution.py:521
  618.7 28.0 %collective-permute-start.47 = (f32[4112]{0:T(1024)S(1)}, f32[4112]{0:T(1024)S(1)}, u32[]{:S(2)}, u32[]{:S(2)}) collective-permute-start(f32[4112]{0:T(1024)S(1)} %add_add_fusion), channel_id=1, source_target_pairs={{0,4},{1,5},{2,6},{3,7},{4,0},{5,1},{6,2},{7,3},{8,12},{9,13},{10,... | collective-permute-start | bytes 49352 | tf_op jit(solution)/shard_map/ppermute | solution.py:621
  649.0 32.4 %collective-permute-start.49 = (bf16[256,2560]{1,0:T(8,128)(2,1)S(1)}, bf16[256,2560]{1,0:T(8,128)(2,1)S(1)}, u32[]{:S(2)}, u32[]{:S(2)}) collective-permute-start(bf16[256,2560]{1,0:T(8,128)(2,1)S(1)} %pad_maximum_fusion.3), channel_id=1, source_target_pairs={{0,2},{2,4},{4,6},{6,7},{7,5},{5,3},{3,1},{1,0},{8,10},{10,12},{12... | collective-permute-start | bytes 3932168 | tf_op jit(solution)/shard_map/ppermute | solution.py:518
  650.4 31.1 %collective-permute-start.50 = (bf16[256,2560]{1,0:T(8,128)(2,1)S(1)}, bf16[256,2560]{1,0:T(8,128)(2,1)S(1)}, u32[]{:S(2)}, u32[]{:S(2)}) collective-permute-start(bf16[256,2560]{1,0:T(8,128)(2,1)S(1)} %pad_maximum_fusion.4), channel_id=1, source_target_pairs={{2,0},{4,2},{6,4},{7,6},{5,7},{3,5},{1,3},{0,1},{10,8},{12,10},{14... | collective-permute-start | bytes 3932168 | tf_op jit(solution)/shard_map/ppermute | solution.py:521
  651.2 29.1 %collective-permute-start.52 = (bf16[1,512,768]{2,1,0:T(8,128)(2,1)S(1)}, bf16[1,512,768]{2,1,0:T(8,128)(2,1)S(1)}, u32[]{:S(2)}, u32[]{:S(2)}) collective-permute-start(bf16[1,512,768]{2,1,0:T(8,128)(2,1)S(1)} %dynamic-slice_bitcast_fusion.1), channel_id=1, source_target_pairs={{0,16},{8,24},{16,0},{24,8},{1,17},{9,25},{17,1},{25,9},{2,18},{10... | collective-permute-start | bytes 2359304 | tf_op jit(solution)/shard_map/ppermute | solution.py:631
  652.1 28.2 %collective-permute-start.51 = (f32[4112]{0:T(1024)S(1)}, f32[4112]{0:T(1024)S(1)}, u32[]{:S(2)}, u32[]{:S(2)}) collective-permute-start(f32[4112]{0:T(1024)S(1)} %add.315), channel_id=1, source_target_pairs={{0,2},{1,3},{2,0},{3,1},{4,6},{5,7},{6,4},{7,5},{8,10},{9,11},{10,... | collective-permute-start | bytes 49352 | tf_op jit(solution)/shard_map/ppermute | solution.py:621
  683.9 30.4 %collective-permute-start.53 = (bf16[256,2560]{1,0:T(8,128)(2,1)}, bf16[256,2560]{1,0:T(8,128)(2,1)}, u32[]{:S(2)}, u32[]{:S(2)}) collective-permute-start(bf16[256,2560]{1,0:T(8,128)(2,1)} %pad_maximum_fusion.5), channel_id=1, source_target_pairs={{0,2},{2,4},{4,6},{6,7},{7,5},{5,3},{3,1},{1,0},{8,10},{10,12},{12... | collective-permute-start | bytes 3932168 | tf_op jit(solution)/shard_map/ppermute | solution.py:518
  684.2 30.1 %collective-permute-start.54 = (bf16[256,2560]{1,0:T(8,128)(2,1)}, bf16[256,2560]{1,0:T(8,128)(2,1)}, u32[]{:S(2)}, u32[]{:S(2)}) collective-permute-start(bf16[256,2560]{1,0:T(8,128)(2,1)} %pad_maximum_fusion.6), channel_id=1, source_target_pairs={{2,0},{4,2},{6,4},{7,6},{5,7},{3,5},{1,3},{0,1},{10,8},{12,10},{14... | collective-permute-start | bytes 3932168 | tf_op jit(solution)/shard_map/ppermute | solution.py:521
  686.0 27.2 %collective-permute-start.55 = (f32[4112]{0:T(1024)S(1)}, f32[4112]{0:T(1024)S(1)}, u32[]{:S(2)}, u32[]{:S(2)}) collective-permute-start(f32[4112]{0:T(1024)S(1)} %add.323), channel_id=1, source_target_pairs={{0,1},{1,0},{2,3},{3,2},{4,5},{5,4},{6,7},{7,6},{8,9},{9,8},{10,11... | collective-permute-start | bytes 49352 | tf_op jit(solution)/shard_map/ppermute | solution.py:621
  (78 other events, 1038.2 us)
Sparse Core Ops, SparseCore 0:
  10.2 31.2 all-gather.4
  44.5 58.5 all-gather.6
  132.0 57.6 all-gather.8
  191.2 34.4 all-gather.10
  407.7 41.4 reduce-scatter.4
  455.3 42.2 reduce-scatter.6
  500.2 71.7 reduce-scatter.8
  578.7 44.5 reduce-scatter.10
